TPU v7x, 128 devices: a whole 4x4x4 slice. The times are simulated.
128 devices in a mesh: grid: 16 (over z, x_lo, core), vec: 8 (over x_hi, y).
Axes of the slice: x: 4 (x_hi: 2, x_lo: 2; x = x_hi * 2 + x_lo), y: 4, z: 4, core: 2. Of those that a mesh axis runs over, the one named last changes fastest.
Arguments:
- orbitals: bfloat16 [884736, 512], P(('grid', 'vec')), may hold values from -1.296875 to 1.296875
- inverse_panel: bfloat16 [2048, 64], replicated, may hold values from -0.125 to 0.125
- points: int32 [2048], replicated, may hold values from 0 to 884735, as said below
Outputs:
- projected: float32 [2048, 64], P(('grid', 'vec'))
Inputs may be any that keep to these rules, and one draw needn't show every extreme that they name: `points`: distinct cell indices.
All inputs are finite; a program needn't handle non-finite values.
Results may differ from a plain program's by a relative error of at most 0.005.
Values may be sent and summed in bfloat16 or wider, within the bound.
No kernel may reach another device: no remote copies, remote signals or barrier semaphores. Data moves between devices by JAX's collectives and lax.ppermute only.
A program may use at most 128 MiB of HBM per device.

v0:
```python
import math

import jax
import jax.numpy as jnp
from jax import lax
from jax.sharding import PartitionSpec as P

NG = 96


SCREEN = 2.25


def wave_tables(count):
    index = lax.iota(jnp.int32, count)
    phase = index[:, None] * index[None, :] % count
    angle = phase.astype(jnp.float32) * (2.0 * math.pi / count)
    return (jnp.cos(angle).astype(jnp.bfloat16), jnp.sin(angle).astype(jnp.bfloat16))


def wavenumber(index, count):
    return jnp.where(index < count // 2, index, index - count).astype(jnp.float32)


def screened(wave_x, wave_y, wave_z):
    squared = (
        wave_x[:, None, None] * wave_x[:, None, None]
        + wave_y[None, :, None] * wave_y[None, :, None]
        + wave_z[None, None, :] * wave_z[None, None, :]
    )
    factor = NG / (2.0 * math.pi) * (NG / (2.0 * math.pi))
    return jnp.where(squared > 0.5, factor / (squared + SCREEN), jnp.float32(0.0))


def mult(data, table, form):
    return jnp.einsum(form, data, table, preferred_element_type=jnp.float32)


def shards(orbitals, inverse_panel, points):
    bf = jnp.bfloat16
    row_count = orbitals.shape[0]
    grid_count = lax.axis_size("grid")
    vec_count = lax.axis_size("vec")
    npoints = points.shape[0]
    offset = (lax.axis_index("grid") * vec_count + lax.axis_index("vec")) * row_count
    local_pos = points - offset
    inside = (local_pos >= 0) & (local_pos < row_count)
    picked = jnp.take(orbitals, jnp.clip(local_pos, 0, row_count - 1), axis=0)
    picked = jnp.where(inside[:, None], picked, jnp.zeros_like(picked)).astype(jnp.float32)
    summed_rows = lax.psum(picked, ("grid", "vec"))
    point_rows = summed_rows.astype(bf)

    def pair_block(block):
        correlation = lax.dot_general(
            block, point_rows, (((1,), (1,)), ((), ())), preferred_element_type=jnp.float32
        )
        return (correlation * correlation).astype(bf)

    pair = lax.map(pair_block, orbitals.reshape(4, row_count // 4, orbitals.shape[1])).reshape(
        row_count, npoints
    )
    fit_cols = lax.dot_general(
        inverse_panel, pair, (((0,), (1,)), ((), ())), preferred_element_type=jnp.float32
    ).astype(bf)
    slab = lax.all_to_all(fit_cols, "vec", split_axis=0, concat_axis=1, tiled=True)
    col_local = slab.shape[0]
    planes = NG // grid_count
    field = slab.reshape(col_local, planes, NG, NG)
    cos_tab, sin_tab = wave_tables(NG)
    z_re = mult(field, cos_tab, "vxyz,zk->vxyk").astype(bf)
    z_im = (-mult(field, sin_tab, "vxyz,zk->vxyk")).astype(bf)
    y_re = (mult(z_re, cos_tab, "vxyz,yk->vxkz") + mult(z_im, sin_tab, "vxyz,yk->vxkz")).astype(bf)
    y_im = (mult(z_im, cos_tab, "vxyz,yk->vxkz") - mult(z_re, sin_tab, "vxyz,yk->vxkz")).astype(bf)
    stacked = jnp.stack([y_re, y_im])
    waves = wavenumber(lax.iota(jnp.int32, NG), NG)
    y_waves = wavenumber(lax.axis_index("grid") * planes + lax.iota(jnp.int32, planes), NG)
    kernel = screened(waves, y_waves, waves)[None]
    piece = lax.all_to_all(stacked, "grid", split_axis=3, concat_axis=2, tiled=True)
    p_re = piece[0]
    p_im = piece[1]
    x_re = mult(p_re, cos_tab, "vxyz,xk->vkyz") + mult(p_im, sin_tab, "vxyz,xk->vkyz")
    x_im = mult(p_im, cos_tab, "vxyz,xk->vkyz") - mult(p_re, sin_tab, "vxyz,xk->vkyz")
    q_re = (x_re * kernel).astype(bf)
    q_im = (x_im * kernel).astype(bf)
    i_re = (mult(q_re, cos_tab, "vxyz,xk->vkyz") - mult(q_im, sin_tab, "vxyz,xk->vkyz")).astype(bf)
    i_im = (mult(q_im, cos_tab, "vxyz,xk->vkyz") + mult(q_re, sin_tab, "vxyz,xk->vkyz")).astype(bf)
    spectrum = lax.all_to_all(
        jnp.stack([i_re, i_im]), "grid", split_axis=2, concat_axis=3, tiled=True
    )
    s_re = spectrum[0]
    s_im = spectrum[1]
    h_re = (mult(s_re, cos_tab, "vxyz,yk->vxkz") - mult(s_im, sin_tab, "vxyz,yk->vxkz")).astype(bf)
    h_im = (mult(s_im, cos_tab, "vxyz,yk->vxkz") + mult(s_re, sin_tab, "vxyz,yk->vxkz")).astype(bf)
    final = mult(h_re, cos_tab, "vxyz,zk->vxyk") - mult(h_im, sin_tab, "vxyz,zk->vxyk")
    potential = (final / float(NG**3)).astype(bf).reshape(col_local, planes * NG * NG)
    pot_rows = lax.all_to_all(potential, "vec", split_axis=1, concat_axis=0, tiled=True)
    scale = 1.0 / math.sqrt(float(NG**3))
    term = lax.dot_general(
        pair, pot_rows, (((0,), (1,)), ((), ())), preferred_element_type=jnp.float32
    )
    return lax.psum_scatter(
        term * jnp.float32(scale), ("grid", "vec"), scatter_dimension=0, tiled=True
    )


def solution(mesh):
    in_specs = (P(("grid", "vec"), None), P(), P())
    out_specs = P(("grid", "vec"), None)
    return jax.shard_map(shards, mesh=mesh, in_specs=in_specs, out_specs=out_specs, check_vma=False)
```

profile of v0, /device:TPU:1, one launch (start us, length us, event | category | flops | bytes accessed | tf_op | source)
XLA Modules:
  0.0 953.7 jit_solution(18184125983649761044)
XLA Ops:
  6.5 0.8 compare_and_fusion.1
  7.3 0.7 fusion.62
  8.0 11.5 %gather_fusion = bf16[2048,512]{1,0:T(8,128)(2,1)S(1)} fusion(bf16[6912,512]{1,0:T(8,128)(2,1)} %param.5, s32[2048]{0:T(1024)S(1)} %fusion.62), kind=kCustom, calls=%fused_computation | custom fusion | bytes 4202496 | tf_op jit(solution)/shard_map/jit(_take)/gather | solution.py:48
  19.5 3.5 select_convert_fusion
  23.0 106.7 %all-reduce.1 = bf16[2048,512]{1,0:T(8,128)(2,1)S(1)} all-reduce(f32[2048,512]{1,0:T(8,128)} %select_convert_fusion), channel_id=1, replica_groups=mesh['grid'=16,'vec'=8] {'grid','vec'}, use_global_device_ids=true, to_apply=%region_0.1 | all-reduce | flops 1048576 | bytes 6291456 | tf_op jit(solution)/shard_map/psum | solution.py:50
  129.7 29.6 %while.10 = (s32[]{:T(128)}, bf16[4,1728,2048]{2,1,0:T(8,128)(2,1)}, bf16[4,1728,512]{2,1,0:T(8,128)(2,1)}, bf16[2048,512]{1,0:T(8,128)(2,1)S(1)}, s32[]{:T(128)}) while((s32[]{:T(128)}, bf16[4,1728,2048]{2,1,0:T(8,128)(2,1)}, bf16[4,1728,512]{2,1,0:T(8,128)(2,1)}, bf16[2048,512]{1,0:T(8,128)(2,1)S(1)}, s32[]{:T(128)}) %tuple.26), condition=%wide.region_2.3_spmd, body=%wide.region_1.2_spmd.sunk | while | flops 3630956544 | bytes 10945597 | solution.py:59
  129.7 7.4 bitcast_dynamic-update-slice_fusion.2
  137.1 7.4 bitcast_dynamic-update-slice_fusion.2
  144.6 7.4 bitcast_dynamic-update-slice_fusion.2
  151.9 7.4 bitcast_dynamic-update-slice_fusion.2
  159.3 13.9 %fusion.3 = bf16[8,8,6912]{2,1,0:T(8,128)(2,1)S(1)} fusion(bf16[6912,2048]{1,0:T(8,128)(2,1)} %bitcast.122, bf16[2048,64]{0,1:T(8,128)(2,1)S(1)} %copy-done), kind=kOutput, calls=%fused_computation.7 | convolution fusion | flops 1812381696 | bytes 29458432 | tf_op jit(solution)/shard_map/dot_general | solution.py:62
  173.3 18.5 %all_to_all.65 = bf16[8,8,6912]{2,1,0:T(8,128)(2,1)S(1)} all-to-all(bf16[8,8,6912]{2,1,0:T(8,128)(2,1)S(1)} %fusion.3), channel_id=1, replica_groups=mesh['grid'=16,'vec'=8] {'vec'}, dimensions={0} | all-to-all | bytes 1769472 | tf_op jit(solution)/shard_map/all_to_all | solution.py:65
  191.9 1.8 reshape.103
  195.7 0.7 fusion.43
  197.1 0.7 fusion.5
  198.3 3.1 copy.82
  201.4 6.1 all-to-all-start.1
  208.0 29.5 %all-to-all-done.1 = bf16[2,8,6,96,96]{4,1,2,0,3:T(8,128)(2,1)S(1)} async-done(((bf16[2,8,6,96,96]{4,1,2,0,3:T(8,128)(2,1)}), bf16[2,8,6,96,96]{4,1,2,0,3:T(8,128)(2,1)S(1)}, u32[]{:S(2)}, u32[]{:S(2)}) %all-to-all-start.1) | async-done | bytes 1769504 | tf_op jit(solution)/shard_map/all_to_all | solution.py:78
  238.5 0.7 fusion.25
  239.3 0.7 fusion.21
  240.1 1.1 fusion.6
  241.9 1.1 fusion.7
  245.6 1.5 copy.98
  247.1 33.3 %all_to_all.66 = bf16[2,8,96,6,96]{4,1,3,0,2:T(8,128)(2,1)S(1)} all-to-all(bf16[2,8,96,6,96]{4,1,3,0,2:T(8,128)(2,1)S(1)} %copy.98), channel_id=1, replica_groups=mesh['grid'=16,'vec'=8] {'grid'}, dimensions={2} | all-to-all | bytes 3538944 | tf_op jit(solution)/shard_map/all_to_all | solution.py:87
  281.3 2.2 fusion.19
  283.6 2.1 fusion.13
  285.7 4.1 fusion.11
  289.8 3.4 multiply_convert_fusion.1
  293.3 0.9 all_to_all.57
  294.4 16.3 %all_to_all.67 = bf16[8,8,6912]{2,0,1:T(8,128)(2,1)S(1)} all-to-all(bf16[8,8,6912]{2,0,1:T(8,128)(2,1)S(1)} %copy.110), channel_id=1, replica_groups=mesh['grid'=16,'vec'=8] {'vec'}, dimensions={1} | all-to-all | bytes 1769472 | tf_op jit(solution)/shard_map/all_to_all | solution.py:96
  310.6 13.9 %convolution_multiply_fusion = f32[2048,64]{1,0:T(8,128)} fusion(bf16[6912,2048]{1,0:T(8,128)(2,1)} %bitcast.123, bf16[8,8,6912]{2,0,1:T(8,128)(2,1)S(1)} %all_to_all.67), kind=kOutput, calls=%fused_computation.8 | convolution fusion | flops 1812070400 | bytes 29720576 | tf_op jit(solution)/shard_map/dot_general | solution.py:98
  324.6 622.3 %reduce-scatter.2.cloned.1.call-done = f32[16,64]{1,0:T(8,128)} async-done(((f32[2048,64]{1,0:T(8,128)}), f32[16,64]{1,0:T(8,128)}) %reduce-scatter.2.cloned.1.call-update) | async-done | bytes 4112 | tf_op jit(solution)/shard_map/reduce_scatter | solution.py:101
  (31 shorter events, 9.4 us)
Async XLA Ops:
  6.5 152.8 %copy-start = (bf16[2048,64]{0,1:T(8,128)(2,1)S(1)}, bf16[2048,64]{0,1:T(8,128)(2,1)}, u32[]{:S(2)}) copy-start(bf16[2048,64]{0,1:T(8,128)(2,1)} %param.6) | copy-start | bytes 786436
  201.4 36.1 %all-to-all-start.1 = ((bf16[2,8,6,96,96]{4,1,2,0,3:T(8,128)(2,1)}), bf16[2,8,6,96,96]{4,1,2,0,3:T(8,128)(2,1)S(1)}, u32[]{:S(2)}, u32[]{:S(2)}) async-start(bf16[2,8,6,96,96]{4,1,2,0,3:T(8,128)(2,1)} %copy.82), calls=%async_computation.1 | async-start | bytes 4718592 | tf_op jit(solution)/shard_map/all_to_all | solution.py:78
  207.5 739.4 %reduce-scatter.2.cloned.1.call-start = ((), (), s32[]{:S(2)}) async-start(), calls=%async_computation.5 | async-start | bytes 1056768 | tf_op jit(solution)/shard_map/reduce_scatter | solution.py:101
  310.6 636.2 %copy-start.1 = (bf16[2048,64]{0,1:T(8,128)(2,1)S(1)}, bf16[2048,64]{0,1:T(8,128)(2,1)}, u32[]{:S(2)}) copy-start(bf16[2048,64]{0,1:T(8,128)(2,1)} %param.6) | copy-start | bytes 786436
Sparse Core Ops, SparseCore 0:
  324.7 622.1 reduce-scatter.1
where the time goes:
time: 968 us; the launch traced here: 954 us
  waiting for transfers between devices  652 us (67%)
  blocking collectives  175 us (18%)
  matrix products  79.8 us (8%)
  local copies, waits for them, and re-layouts  21.2 us (2%)
  between operations  13.7 us (1%)
    reduce_scatter x1, waiting for transfers between devices, shards(): lax.psum_scatter(term * jnp.float32(scale), ('grid', 'vec'), scatter_dime...  622 us
    psum x1, blocking collectives, shards(): summed_rows = lax.psum(picked, ('grid', 'vec'))  107 us
    all_to_all x1, blocking collectives, shards(): lax.all_to_all(jnp.stack([i_re, i_im]), 'grid', split_axis=2, concat_axis...  33.3 us
    dot_general x4, matrix products, pair_block(): lax.dot_general(block, point_rows, (((1,), (1,)), ((), ())), preferred_el...  29.6 us
    all_to_all x1, waiting for transfers between devices, shards(): lax.all_to_all(stacked, 'grid', split_axis=3, concat_axis=2, tiled=True)  29.5 us
    dot_general x18, matrix products, mult(): return jnp.einsum(form, data, table, preferred_element_type=jnp.float32)  22.4 us
  transfers between devices with their start and end apart: 2, of which 2 were waited for; matrix products, arithmetic and copies ran while one was open for 0% of the time, Pallas kernels for 0%

commit v1 on v0

v1 whole, which is shorter than its diff:
```python
import math

import jax
import jax.numpy as jnp
from jax import lax
from jax.sharding import PartitionSpec as P

NG = 96
HALF = NG // 2
SCREEN = 2.25
BOTH = ("grid", "vec")


def wave_tables(count):
    index = lax.iota(jnp.int32, count)
    phase = index[:, None] * index[None, :] % count
    angle = phase.astype(jnp.float32) * (2.0 * math.pi / count)
    return (jnp.cos(angle).astype(jnp.bfloat16), jnp.sin(angle).astype(jnp.bfloat16))


def real_basis():
    cos_tab, sin_tab = wave_tables(NG)
    return jnp.concatenate([cos_tab[:, : HALF + 1], sin_tab[:, 1:HALF]], axis=1)


def wave_of(column):
    return jnp.where(column <= HALF, column, column - HALF)


def weight_of(wave):
    return jnp.where((wave == 0) | (wave == HALF), 1.0, 2.0).astype(jnp.float32)


def shards(orbitals, inverse_panel, points):
    bf = jnp.bfloat16
    f32 = jnp.float32
    row_count = orbitals.shape[0]
    vec_count = lax.axis_size("vec")
    devices = lax.axis_size("grid") * vec_count
    me = lax.axis_index("grid") * vec_count + lax.axis_index("vec")
    npoints = points.shape[0]
    local_pos = points - me * row_count
    inside = (local_pos >= 0) & (local_pos < row_count)
    picked = jnp.take(orbitals, jnp.clip(local_pos, 0, row_count - 1), axis=0)
    picked = jnp.where(inside[:, None], picked, jnp.zeros_like(picked)).astype(f32)
    point_rows = lax.psum(picked, BOTH).astype(bf)

    def pair_block(block):
        correlation = lax.dot_general(
            block, point_rows, (((1,), (1,)), ((), ())), preferred_element_type=f32
        )
        return (correlation * correlation).astype(bf)

    pair = lax.map(pair_block, orbitals.reshape(4, row_count // 4, orbitals.shape[1])).reshape(
        row_count, npoints
    )
    cols = inverse_panel.shape[1]
    fit = jnp.dot(pair, inverse_panel, preferred_element_type=f32).astype(bf)
    basis = real_basis()
    lines = row_count // NG
    field = fit.reshape(lines, NG, cols)
    spec_z = jnp.einsum("yzc,zm->ymc", field, basis, preferred_element_type=f32).astype(bf)
    send = spec_z.reshape(lines // 8, 8, 32, 3, 4, 16).transpose(2, 4, 0, 3, 1, 5)
    send = send.reshape(devices, lines // 8 * 3, 128)
    planes = lax.all_to_all(send, BOTH, 0, 0)
    planes = planes.reshape(NG, NG // 8, 3, 8, 16).transpose(2, 4, 0, 1, 3).reshape(48, NG, NG)
    spec_y = jnp.einsum("pxy,yk->pxk", planes, basis, preferred_element_type=f32).astype(bf)
    spec_x = jnp.einsum("pxk,xl->plk", spec_y, basis, preferred_element_type=f32)
    wave = wave_of(lax.iota(jnp.int32, NG))
    wave_z = wave_of((me // 4) * 3 + lax.iota(jnp.int32, 3))
    wf = wave.astype(f32)
    wz = wave_z.astype(f32)
    squared = (wf * wf)[None, :, None] + (wf * wf)[None, None, :] + (wz * wz)[:, None, None]
    factor = NG / (2.0 * math.pi) * (NG / (2.0 * math.pi))
    kernel = jnp.where(squared > 0.5, factor / (squared + SCREEN), jnp.float32(0.0))
    weight = weight_of(wave)
    kernel = kernel * (
        weight[None, :, None] * weight[None, None, :] * weight_of(wave_z)[:, None, None]
    )
    scaled = (spec_x.reshape(3, 16, NG, NG) * kernel[:, None]).astype(bf).reshape(48, NG, NG)
    back_x = jnp.einsum("plk,xl->pxk", scaled, basis, preferred_element_type=f32).astype(bf)
    back_y = jnp.einsum("pxk,yk->pxy", back_x, basis, preferred_element_type=f32).astype(bf)
    ret = back_y.reshape(3, 16, NG, NG // 8, 8).transpose(2, 3, 0, 4, 1)
    ret = ret.reshape(devices, lines // 8 * 3, 128)
    got = lax.all_to_all(ret, BOTH, 0, 0)
    got = got.reshape(32, 4, lines // 8, 3, 8, 16).transpose(2, 4, 0, 3, 1, 5)
    got = got.reshape(lines, NG, cols)
    final = jnp.einsum("ymc,zm->yzc", got, basis, preferred_element_type=f32)
    potential = (final / float(NG**3)).astype(bf).reshape(row_count, cols)
    term = lax.dot_general(
        pair, potential, (((0,), (0,)), ((), ())), preferred_element_type=f32
    )
    scale = 1.0 / math.sqrt(float(NG**3))
    parts = (term * f32(scale)).reshape(devices, 8, 128)
    parts = lax.all_to_all(parts, BOTH, 0, 0)
    return jnp.sum(parts, axis=0).reshape(npoints // devices, cols)


def solution(mesh):
    in_specs = (P(BOTH, None), P(), P())
    return jax.shard_map(
        shards, mesh=mesh, in_specs=in_specs, out_specs=P(BOTH, None), check_vma=False
    )
```

time: 968 us -> 342 us (0.35); the launches traced: 954 us -> 338 us
  waiting for transfers between devices: 652 us -> 17.9 us
  local copies, waits for them, and re-layouts: 21.2 us -> 100 us
  blocking collectives: 175 us -> 149 us
  matrix products: 79.8 us -> 58.1 us
  between operations: 13.7 us -> 0.51 us
    reduce_scatter x1 -> x0, waiting for transfers between devices: 622 us -> none  [shards(): lax.psum_scatter(term * jnp.float32(scale), ('grid', 'vec'), scatter_dime...]
    reshape x1 -> x12, local copies, waits for them, and re-layouts: 1.77 us -> 61.5 us  [the longest x2 22.8 us: shards(): send = send.reshape(devices, lines // 8 * 3, 128)]
    all_to_all x3 -> x2, blocking collectives: 68 us -> 42 us  [the longest x1 23.5 us: shards(): got = lax.all_to_all(ret, BOTH, 0, 0)]
    transpose x0 -> x3, local copies, waits for them, and re-layouts: none -> 24.5 us  [the longest x1 9.67 us: shards(): got = got.reshape(32, 4, lines // 8, 3, 8, 16).transpose(2, 4, 0, 3, 1, 5)]
    dot_general x20 -> x6, matrix products: 50.2 us -> 28.5 us  [the longest x1 13.9 us: shards(): fit = jnp.dot(pair, inverse_panel, preferred_element_type=f32).astype(bf)]
    all_to_all x1, waiting for transfers between devices: 29.5 us -> 17.9 us  [shards(): planes = lax.all_to_all(send, BOTH, 0, 0)]
  transfers between devices with their start and end apart: 2 -> 1, of which waited for: 2 -> 1; matrix products, arithmetic and copies ran while one was open for 0% -> 0% of each run, Pallas kernels for 0% -> 0%
where the time goes in v1:
time: 342 us; the launch traced here: 338 us
  blocking collectives  149 us (44%)
  local copies, waits for them, and re-layouts  100 us (29%)
  matrix products  58.1 us (17%)
  waiting for transfers between devices  17.9 us (5%)
  starting transfers between devices  6.34 us (2%)
  other arithmetic  5.79 us (2%)
    psum x1, blocking collectives, shards(): point_rows = lax.psum(picked, BOTH).astype(bf)  107 us
    dot_general x4, matrix products, pair_block(): lax.dot_general(block, point_rows, (((1,), (1,)), ((), ())), preferred_el...  29.6 us
    all_to_all x1, blocking collectives, shards(): got = lax.all_to_all(ret, BOTH, 0, 0)  23.5 us
    reshape x2, local copies, waits for them, and re-layouts, shards(): send = send.reshape(devices, lines // 8 * 3, 128)  22.8 us
    all_to_all x1, blocking collectives, shards(): parts = lax.all_to_all(parts, BOTH, 0, 0)  18.5 us
    all_to_all x1, waiting for transfers between devices, shards(): planes = lax.all_to_all(send, BOTH, 0, 0)  17.9 us
    dot_general x1, matrix products, shards(): fit = jnp.dot(pair, inverse_panel, preferred_element_type=f32).astype(bf)  13.9 us
    dot_general x1, matrix products, shards(): lax.dot_general(pair, potential, (((0,), (0,)), ((), ())), preferred_elem...  11.7 us
  transfers between devices with their start and end apart: 1, of which 1 were waited for; matrix products, arithmetic and copies ran while one was open for 0% of the time, Pallas kernels for 0%

profile of v1, /device:TPU:1, one launch (start us, length us, event | category | flops | bytes accessed | tf_op | source)
XLA Modules:
  0.0 338.0 jit_solution(18054202011786445219)
XLA Ops:
  0.5 0.7 fusion.17
  1.9 11.5 %gather_fusion = bf16[2048,512]{1,0:T(8,128)(2,1)S(1)} fusion(bf16[6912,512]{1,0:T(8,128)(2,1)} %param.5, s32[2048]{0:T(1024)S(1)} %fusion.17), kind=kCustom, calls=%fused_computation | custom fusion | bytes 4202496 | tf_op jit(solution)/shard_map/jit(_take)/gather | solution.py:44
  13.4 3.5 %select_convert_fusion = f32[2048,512]{1,0:T(8,128)} fusion(bf16[2048,512]{1,0:T(8,128)(2,1)S(1)} %gather_fusion, pred[2048]{0:T(1024)(128)(4,1)S(1)} %get-tuple-element.37, pred[2048]{0:T(1024)(128)(4,1)S(1)} %get-tuple-element.36), kind=kLoop, calls=%fused_computation.11 | loop fusion | flops 3145728 | bytes 6295552 | tf_op jit(solution)/shard_map/convert_element_type | solution.py:45
  16.9 107.3 %all-reduce.1 = bf16[2048,512]{1,0:T(8,128)(2,1)S(1)} all-reduce(f32[2048,512]{1,0:T(8,128)} %select_convert_fusion), channel_id=1, replica_groups=mesh['grid'=16,'vec'=8] {'grid','vec'}, use_global_device_ids=true, to_apply=%region_0.1 | all-reduce | flops 1048576 | bytes 6291456 | tf_op jit(solution)/shard_map/psum | solution.py:46
  124.2 29.6 %while.10 = (s32[]{:T(128)}, bf16[4,1728,2048]{2,1,0:T(8,128)(2,1)}, bf16[4,1728,512]{2,1,0:T(8,128)(2,1)}, bf16[2048,512]{1,0:T(8,128)(2,1)S(1)}, s32[]{:T(128)}) while((s32[]{:T(128)}, bf16[4,1728,2048]{2,1,0:T(8,128)(2,1)}, bf16[4,1728,512]{2,1,0:T(8,128)(2,1)}, bf16[2048,512]{1,0:T(8,128)(2,1)S(1)}, s32[]{:T(128)}) %tuple.24), condition=%wide.region_2.3_spmd, body=%wide.region_1.2_spmd.sunk | while | flops 3630956544 | bytes 10945605 | solution.py:54
  124.2 7.4 %bitcast_dynamic-update-slice_fusion.2 = bf16[4,1728,2048]{2,1,0:T(8,128)(2,1)} fusion(bf16[4,1728,2048]{2,1,0:T(8,128)(2,1)} %get-tuple-element.73, s32[]{:T(128)S(6)} %copy.35, bf16[2048,512]{1,0:T(8,128)(2,1)S(1)} %get-tuple-element.80, bf16[4,1728,512]{2,1,0:T(8,128)(2,1)} %get-tuple-element.79), kind=kOutput, calls=%fused_computation.2.clone.1 | convolution fusion | flops 3630956544 | bytes 10945536 | tf_op jit(solution)/shard_map/while/body/eval_jaxpr/dot_general | solution.py:49
  131.6 7.4 %bitcast_dynamic-update-slice_fusion.2 = bf16[4,1728,2048]{2,1,0:T(8,128)(2,1)} fusion(bf16[4,1728,2048]{2,1,0:T(8,128)(2,1)} %get-tuple-element.73, s32[]{:T(128)S(6)} %copy.35, bf16[2048,512]{1,0:T(8,128)(2,1)S(1)} %get-tuple-element.80, bf16[4,1728,512]{2,1,0:T(8,128)(2,1)} %get-tuple-element.79), kind=kOutput, calls=%fused_computation.2.clone.1 | convolution fusion | flops 3630956544 | bytes 10945536 | tf_op jit(solution)/shard_map/while/body/eval_jaxpr/dot_general | solution.py:49
  139.0 7.4 %bitcast_dynamic-update-slice_fusion.2 = bf16[4,1728,2048]{2,1,0:T(8,128)(2,1)} fusion(bf16[4,1728,2048]{2,1,0:T(8,128)(2,1)} %get-tuple-element.73, s32[]{:T(128)S(6)} %copy.35, bf16[2048,512]{1,0:T(8,128)(2,1)S(1)} %get-tuple-element.80, bf16[4,1728,512]{2,1,0:T(8,128)(2,1)} %get-tuple-element.79), kind=kOutput, calls=%fused_computation.2.clone.1 | convolution fusion | flops 3630956544 | bytes 10945536 | tf_op jit(solution)/shard_map/while/body/eval_jaxpr/dot_general | solution.py:49
  146.4 7.4 %bitcast_dynamic-update-slice_fusion.2 = bf16[4,1728,2048]{2,1,0:T(8,128)(2,1)} fusion(bf16[4,1728,2048]{2,1,0:T(8,128)(2,1)} %get-tuple-element.73, s32[]{:T(128)S(6)} %copy.35, bf16[2048,512]{1,0:T(8,128)(2,1)S(1)} %get-tuple-element.80, bf16[4,1728,512]{2,1,0:T(8,128)(2,1)} %get-tuple-element.79), kind=kOutput, calls=%fused_computation.2.clone.1 | convolution fusion | flops 3630956544 | bytes 10945536 | tf_op jit(solution)/shard_map/while/body/eval_jaxpr/dot_general | solution.py:49
  153.8 13.9 %convolution_convert_fusion = bf16[6912,64]{0,1:T(8,128)(2,1)S(1)} fusion(bf16[6912,2048]{1,0:T(8,128)(2,1)} %bitcast.62, bf16[2048,64]{0,1:T(8,128)(2,1)S(1)} %copy-done), kind=kOutput, calls=%fused_computation.6 | convolution fusion | flops 1812381696 | bytes 29458432 | tf_op jit(solution)/shard_map/dot_general | solution.py:58
  167.7 1.8 reshape.171
  170.0 1.1 copy.14
  171.1 5.8 %reshape.172 = bf16[9,8,32,3,4,16]{5,4,3,2,1,0:T(4,128)(2,1)} reshape(bf16[72,96,64]{2,1,0:T(8,128)(2,1)S(1)} %copy.14) | data formatting | bytes 1769472 | tf_op jit(solution)/shard_map/reshape | solution.py:63
  176.9 14.0 %copy.29 = bf16[32,4,9,3,8,16]{5,4,3,2,1,0:T(8,128)(2,1)} copy(bf16[32,4,9,3,8,16]{5,1,3,0,4,2:T(4,128)(2,1)} %bitcast.65) | data formatting | bytes 1769472 | tf_op jit(solution)/shard_map/reshape | solution.py:64
  190.9 8.8 %reshape.194 = bf16[128,27,128]{2,1,0:T(8,128)(2,1)} reshape(bf16[32,4,9,3,8,16]{5,4,3,2,1,0:T(8,128)(2,1)} %copy.29) | data formatting | bytes 1769472 | tf_op jit(solution)/shard_map/reshape | solution.py:64
  199.7 6.3 %all-to-all-start = ((bf16[128,27,128]{2,1,0:T(8,128)(2,1)}), bf16[128,27,128]{2,1,0:T(8,128)(2,1)S(1)}, u32[]{:S(2)}, u32[]{:S(2)}) async-start(bf16[128,27,128]{2,1,0:T(8,128)(2,1)} %reshape.194), calls=%async_computation | async-start | bytes 2097152 | tf_op jit(solution)/shard_map/all_to_all | solution.py:65
  206.3 17.9 %all-to-all-done = bf16[128,27,128]{2,1,0:T(8,128)(2,1)S(1)} async-done(((bf16[128,27,128]{2,1,0:T(8,128)(2,1)}), bf16[128,27,128]{2,1,0:T(8,128)(2,1)S(1)}, u32[]{:S(2)}, u32[]{:S(2)}) %all-to-all-start) | async-done | bytes 884768 | tf_op jit(solution)/shard_map/all_to_all | solution.py:65
  224.3 5.9 %reshape.174 = bf16[96,12,3,8,16]{4,3,2,1,0:T(8,128)(2,1)} reshape(bf16[128,27,128]{2,1,0:T(8,128)(2,1)S(1)} %all-to-all-done) | data formatting | bytes 1769472 | tf_op jit(solution)/shard_map/reshape | solution.py:66
  230.2 8.0 %copy.17 = bf16[3,16,96,12,8]{2,4,3,1,0:T(8,128)(2,1)S(1)} copy(bf16[3,16,96,12,8]{1,4,0,3,2:T(8,128)(2,1)} %bitcast.67) | data formatting | bytes 1769472 | tf_op jit(solution)/shard_map/transpose | solution.py:66
  238.2 0.9 fusion.3
  239.2 0.8 convolution_convert_fusion.1
  240.6 6.8 %copy.21 = bf16[96,12,3,8,16]{4,3,2,1,0:T(8,128)(2,1)} copy(bf16[96,12,3,8,16]{0,3,1,4,2:T(8,128)(2,1)S(1)} %bitcast.69) | data formatting | bytes 1769472 | tf_op jit(solution)/shard_map/transpose | solution.py:83
  247.5 8.0 %reshape.177 = bf16[128,27,128]{2,1,0:T(8,128)(2,1)S(1)} reshape(bf16[96,12,3,8,16]{4,3,2,1,0:T(8,128)(2,1)} %copy.21) | data formatting | bytes 1769472 | tf_op jit(solution)/shard_map/reshape | solution.py:84
  255.5 23.5 %all_to_all.15 = bf16[128,27,128]{2,1,0:T(8,128)(2,1)S(1)} all-to-all(bf16[128,27,128]{2,1,0:T(8,128)(2,1)S(1)} %reshape.177), channel_id=1, replica_groups=mesh['grid'=16,'vec'=8] {'grid','vec'}, dimensions={0} | all-to-all | bytes 1769472 | tf_op jit(solution)/shard_map/all_to_all | solution.py:85
  279.3 6.1 %reshape.178 = bf16[32,4,9,3,8,16]{5,4,1,0,3,2:T(8,128)(2,1)} reshape(bf16[128,27,128]{2,0,1:T(8,128)(2,1)S(1)} %copy.22) | data formatting | bytes 1769472 | tf_op jit(solution)/shard_map/reshape | solution.py:86
  285.4 9.7 %copy.23 = bf16[9,8,32,3,4,16]{5,4,3,2,1,0:T(4,128)(2,1)} copy(bf16[9,8,32,3,4,16]{5,1,4,2,3,0:T(8,128)(2,1)} %bitcast.66) | data formatting | bytes 1769472 | tf_op jit(solution)/shard_map/transpose | solution.py:86
  295.1 8.3 %reshape.179 = bf16[72,96,64]{2,1,0:T(8,128)(2,1)S(1)} reshape(bf16[9,8,32,3,4,16]{5,4,3,2,1,0:T(4,128)(2,1)} %copy.23) | data formatting | bytes 1769472 | tf_op jit(solution)/shard_map/reshape | solution.py:87
  303.4 1.0 copy.24
  304.4 0.8 fusion.4
  305.2 0.9 reshape.180
  306.1 11.7 %convolution_multiply_fusion = f32[2048,64]{0,1:T(8,128)S(1)} fusion(bf16[6912,64]{0,1:T(8,128)(2,1)S(1)} %reshape.180, bf16[6912,2048]{1,0:T(8,128)(2,1)} %bitcast.63), kind=kOutput, calls=%fused_computation.10 | convolution fusion | flops 1812070400 | bytes 29720576 | tf_op jit(solution)/shard_map/dot_general | solution.py:90
  318.4 18.5 %all_to_all.16 = f32[128,8,128]{2,1,0:T(8,128)S(1)} all-to-all(f32[128,8,128]{2,1,0:T(8,128)S(1)} %reshape.181), channel_id=1, replica_groups=mesh['grid'=16,'vec'=8] {'grid','vec'}, dimensions={0} | all-to-all | bytes 1048576 | tf_op jit(solution)/shard_map/all_to_all | solution.py:95
  (22 shorter events, 4.3 us)
Async XLA Ops:
  0.0 153.8 %copy-start = (bf16[2048,64]{0,1:T(8,128)(2,1)S(1)}, bf16[2048,64]{0,1:T(8,128)(2,1)}, u32[]{:S(2)}) copy-start(bf16[2048,64]{0,1:T(8,128)(2,1)} %param.6) | copy-start | bytes 786436
  199.7 24.6 %all-to-all-start = ((bf16[128,27,128]{2,1,0:T(8,128)(2,1)}), bf16[128,27,128]{2,1,0:T(8,128)(2,1)S(1)}, u32[]{:S(2)}, u32[]{:S(2)}) async-start(bf16[128,27,128]{2,1,0:T(8,128)(2,1)} %reshape.194), calls=%async_computation | async-start | bytes 2097152 | tf_op jit(solution)/shard_map/all_to_all | solution.py:65
  306.1 31.6 %copy-start.1 = (bf16[2048,64]{0,1:T(8,128)(2,1)S(1)}, bf16[2048,64]{0,1:T(8,128)(2,1)}, u32[]{:S(2)}) copy-start(bf16[2048,64]{0,1:T(8,128)(2,1)} %param.6) | copy-start | bytes 786436

commit v2 on v1

v2 whole, which is shorter than its diff:
```python
import functools
import math

import jax
import jax.numpy as jnp
import numpy as np
from jax import lax
from jax.experimental import pallas as pl
from jax.experimental.pallas import tpu as pltpu
from jax.sharding import PartitionSpec as P

NG = 96
HALF = NG // 2
SCREEN = 2.25
BOTH = ("grid", "vec")
BF = jnp.bfloat16
F32 = jnp.float32

LINES = 72
OCT = LINES // 8
MG, MI = 32, 3
CG, CI = 4, 16
ROWS = 32
CELLS = 8 * NG


def basis_table():
    index = np.arange(NG)
    phase = (index[:, None] * index[None, :]) % NG
    angle = phase.astype(np.float32) * np.float32(2.0 * math.pi / NG)
    cos_tab = np.cos(angle).astype(BF).astype(np.float32)
    sin_tab = np.sin(angle).astype(BF).astype(np.float32)
    return np.concatenate([cos_tab[:, : HALF + 1], sin_tab[:, 1:HALF]], axis=1)


def tables():
    basis = basis_table()
    ahead = np.zeros((MG, ROWS, OCT, NG), np.float32)
    for octet in range(OCT):
        for mi in range(MI):
            ahead[:, octet * MI + mi, octet, :] = basis[:, mi::MI].T
    ahead = ahead.reshape(MG * ROWS, OCT * NG)
    lane = np.arange(512).reshape(8, CG, CI)
    order = lane.transpose(1, 0, 2).reshape(-1)
    swap = np.zeros((512, 512), np.float32)
    swap[order, np.arange(512)] = 1.0
    wide = np.kron(basis, np.eye(CI, dtype=np.float32))
    x_order = (3 * np.arange(32)[None, :] + np.arange(3)[:, None]).reshape(-1)
    x_basis = basis[x_order]
    return {
        "ahead": ahead,
        "back": ahead.T,
        "swap": swap,
        "unswap": swap.T,
        "wide": wide,
        "wide_t": wide.T,
        "x_ahead": x_basis.T,
        "x_back": x_basis,
    }


def const(array):
    return jnp.asarray(np.ascontiguousarray(array).astype(BF))


def mm(a, b):
    return jnp.dot(a, b, preferred_element_type=F32)


def pair_kernel(orb, rows_t, panel, ahead, swap, pair, send, fit):
    step = pl.program_id(0)
    npts = rows_t.shape[1]
    chunk = 512
    total = jnp.zeros((CELLS, 128), F32)
    for start in range(0, npts, chunk):
        corr = mm(orb[...], rows_t[:, start : start + chunk])
        block = (corr * corr).astype(BF)
        pair[:, start : start + chunk] = block
        total = total + mm(block, panel[start : start + chunk, :])
    low = lax.broadcasted_iota(jnp.int32, (NG, 128), 1) < 64
    for two in range(4):
        even = total[2 * two * NG : (2 * two + 1) * NG]
        odd = total[(2 * two + 1) * NG : (2 * two + 2) * NG]
        fit[pl.ds(pl.multiple_of(step * NG, NG), NG), two * 128 : (two + 1) * 128] = jnp.where(
            low, even, odd
        ).astype(BF)

    @pl.when(step == pl.num_programs(0) - 1)
    def _():
        for part in range(4):
            rows = MG * ROWS // 4
            spec = mm(ahead[part * rows : (part + 1) * rows, :], fit[...]).astype(BF)
            moved = mm(spec, swap[...]).astype(BF)
            for cg in range(CG):
                send[part * MG // 4 : (part + 1) * MG // 4, cg] = moved[
                    :, cg * 128 : (cg + 1) * 128
                ].reshape(MG // 4, ROWS, 128)


def make_pairs(orbitals, rows_t, panel2, tab):
    npts = rows_t.shape[1]
    norb = orbitals.shape[1]
    steps = orbitals.shape[0] // CELLS
    whole = lambda shape: pl.BlockSpec(shape, lambda i: (0,) * len(shape))
    return pl.pallas_call(
        pair_kernel,
        grid=(steps,),
        in_specs=[
            pl.BlockSpec((CELLS, norb), lambda i: (i, 0)),
            whole(rows_t.shape),
            whole(panel2.shape),
            whole(tab["ahead"].shape),
            whole(tab["swap"].shape),
        ],
        out_specs=[
            pl.BlockSpec((CELLS, npts), lambda i: (i, 0)),
            whole((MG, CG, ROWS, 128)),
        ],
        out_shape=[
            jax.ShapeDtypeStruct((orbitals.shape[0], npts), BF),
            jax.ShapeDtypeStruct((MG, CG, ROWS, 128), BF),
        ],
        scratch_shapes=[pltpu.VMEM((OCT * NG, 512), BF)],
        compiler_params=pltpu.CompilerParams(vmem_limit_bytes=48 * 2**20),
        name="pairs",
    )(orbitals, rows_t, panel2, const(tab["ahead"]), const(tab["swap"]))


def places():
    for part in range(4):
        for octet in range(OCT):
            for mi in range(MI):
                spot = part * OCT + octet
                yield part * ROWS + octet * MI + mi, mi, spot // 12, spot % 12


def solve_kernel(first, got, wide, wide_t, x_ahead, x_back, out, flat, field):
    flat[...] = got[...].astype(F32)
    for row, mi, xr, yo in places():
        field[mi, xr * 32 : (xr + 1) * 32, yo * 128 : (yo + 1) * 128] = flat[
            pl.ds(row, 32, stride=4 * ROWS), :
        ].astype(BF)
    lane = lax.broadcasted_iota(jnp.int32, (1, NG * CI), 1) // CI
    subl = lax.broadcasted_iota(jnp.int32, (NG, 1), 0)
    wave_of = lambda k: jnp.where(k <= HALF, k, k - HALF)
    weight = lambda w: jnp.where((w == 0) | (w == HALF), 1.0, 2.0).astype(F32)
    wave_y, wave_x = wave_of(lane), wave_of(subl)
    square = lambda w: w.astype(F32) * w.astype(F32)
    factor = NG / (2.0 * math.pi) * (NG / (2.0 * math.pi))
    flat[...] = jnp.zeros_like(flat)
    spec_y = mm(field[...].reshape(MI * NG, NG * CI), wide[...]).astype(BF)
    backs = []
    for mi in range(MI):
        wave_z = wave_of(first[0] + mi)
        spec = mm(x_ahead[...], spec_y[mi * NG : (mi + 1) * NG])
        total = square(wave_x) + square(wave_y) + square(wave_z)
        gain = weight(wave_x) * (weight(wave_y) * weight(wave_z))
        kernel = jnp.where(total > 0.5, factor / (total + SCREEN), 0.0) * gain
        scaled = (spec * kernel).astype(BF)
        backs.append(mm(x_back[...], scaled).astype(BF))
    plane = mm(jnp.concatenate(backs, axis=0), wide_t[...])
    for row, mi, xr, yo in places():
        flat[pl.ds(row, 32, stride=4 * ROWS), :] = plane[
            mi * NG + xr * 32 : mi * NG + (xr + 1) * 32, yo * 128 : (yo + 1) * 128
        ]
    out[...] = flat[...].astype(BF)


def solve(first, got, tab):
    vmem = pl.BlockSpec(memory_space=pltpu.VMEM)
    return pl.pallas_call(
        solve_kernel,
        in_specs=[pl.BlockSpec(memory_space=pltpu.SMEM)] + [vmem] * 5,
        out_specs=vmem,
        out_shape=jax.ShapeDtypeStruct(got.shape, BF),
        scratch_shapes=[
            pltpu.VMEM(got.shape, F32),
            pltpu.VMEM((MI, NG, NG * CI), BF),
        ],
        compiler_params=pltpu.CompilerParams(vmem_limit_bytes=48 * 2**20),
        name="solve",
    )(
        first,
        got,
        const(tab["wide"]),
        const(tab["wide_t"]),
        const(tab["x_ahead"]),
        const(tab["x_back"]),
    )


def project_kernel(got, unswap, back, pair, out, spec, pot, acc):
    step = pl.program_id(0)

    @pl.when(step == 0)
    def _():
        for part in range(4):
            rows = MG * ROWS // 4
            block = jnp.concatenate(
                [
                    got[part * MG // 4 : (part + 1) * MG // 4, cg].reshape(rows, 128)
                    for cg in range(CG)
                ],
                axis=1,
            )
            spec[part * rows : (part + 1) * rows, :] = mm(block, unswap[...]).astype(BF)
        for octet in range(OCT):
            final = mm(back[octet * NG : (octet + 1) * NG, :], spec[...])
            final = final / float(NG**3)
            for yi in range(8):
                start = (octet * 8 + yi) * NG
                pot[start : start + NG, :] = final[:, yi * 64 : (yi + 1) * 64].astype(BF)
        acc[...] = jnp.zeros_like(acc)

    block = pot[pl.ds(pl.multiple_of(step * CELLS, CELLS), CELLS), :]
    acc[...] += lax.dot_general(
        block, pair[...], (((0,), (0,)), ((), ())), preferred_element_type=F32
    )

    @pl.when(step == pl.num_programs(0) - 1)
    def _():
        scale = 1.0 / math.sqrt(float(NG**3))
        turned = (acc[...] * scale).T.reshape(128, 2, 8, 64)
        out[...] = jnp.concatenate([turned[:, 0], turned[:, 1]], axis=-1)


def project(got, pair, tab):
    steps = pair.shape[0] // CELLS
    whole = lambda shape: pl.BlockSpec(shape, lambda i: (0,) * len(shape))
    return pl.pallas_call(
        project_kernel,
        grid=(steps,),
        in_specs=[
            whole(got.shape),
            whole(tab["unswap"].shape),
            whole(tab["back"].shape),
            pl.BlockSpec((CELLS, pair.shape[1]), lambda i: (i, 0)),
        ],
        out_specs=whole((128, 8, 128)),
        out_shape=jax.ShapeDtypeStruct((128, 8, 128), F32),
        scratch_shapes=[
            pltpu.VMEM((MG * ROWS, 512), BF),
            pltpu.VMEM((pair.shape[0], 64), BF),
            pltpu.VMEM((64, pair.shape[1]), F32),
        ],
        compiler_params=pltpu.CompilerParams(vmem_limit_bytes=48 * 2**20),
        name="project",
    )(got, const(tab["unswap"]), const(tab["back"]), pair)


def gather_rows(orbitals, points, me):
    row_count = orbitals.shape[0]
    local_pos = points - me * row_count
    inside = (local_pos >= 0) & (local_pos < row_count)
    picked = jnp.take(orbitals, jnp.clip(local_pos, 0, row_count - 1), axis=0)
    picked = jnp.where(inside[:, None], picked, jnp.zeros_like(picked)).astype(F32)
    return lax.psum(picked, BOTH).astype(BF)


def shards(orbitals, inverse_panel, points):
    tab = tables()
    vec_count = lax.axis_size("vec")
    devices = lax.axis_size("grid") * vec_count
    me = lax.axis_index("grid") * vec_count + lax.axis_index("vec")
    npoints, cols = inverse_panel.shape
    rows_t = gather_rows(orbitals, points, me).T
    panel2 = jnp.concatenate([inverse_panel, inverse_panel], axis=1)
    pair, send = make_pairs(orbitals, rows_t, panel2, tab)
    planes = lax.all_to_all(send.reshape(devices, ROWS, 128), BOTH, 0, 0)
    first = (me // CG * MI).astype(jnp.int32).reshape(1)
    ret = solve(first, planes.reshape(devices * ROWS, 128), tab)
    got = lax.all_to_all(ret.reshape(devices, ROWS, 128), BOTH, 0, 0)
    parts = project(got.reshape(MG, CG, ROWS, 128), pair, tab)
    parts = lax.all_to_all(parts, BOTH, 0, 0)
    total = jnp.sum(parts, axis=0)
    return jnp.concatenate([total[:, :cols], total[:, cols:]], axis=0)


def solution(mesh):
    in_specs = (P(BOTH, None), P(), P())
    return jax.shard_map(
        shards, mesh=mesh, in_specs=in_specs, out_specs=P(BOTH, None), check_vma=False
    )
```

time: 342 us -> 257 us (0.75)
  local copies, waits for them, and re-layouts: 100 us -> 17.8 us
  Pallas kernels: 0 us -> 59.3 us
  matrix products: 58.1 us -> 0 us
    reshape x12 -> x0, local copies, waits for them, and re-layouts: 61.5 us -> none  [the longest x2 22.8 us: shards(): send = send.reshape(devices, lines // 8 * 3, 128)]
    pallas_call x0 -> x3, Pallas kernels: none -> 59.3 us  [the longest x1 33.3 us: make_pairs(): pl.pallas_call(pair_kernel, grid=(steps,), in_specs=[pl.BlockSpec((CELLS,...]
    dot_general x10 -> x0, matrix products: 58.1 us -> none  [the longest x4 29.6 us: pair_block(): lax.dot_general(block, point_rows, (((1,), (1,)), ((), ())), preferred_el...]
    transpose x3 -> x0, local copies, waits for them, and re-layouts: 24.5 us -> none  [the longest x1 9.67 us: shards(): got = got.reshape(32, 4, lines // 8, 3, 8, 16).transpose(2, 4, 0, 3, 1, 5)]
    unnamed x4 -> x15, local copies, waits for them, and re-layouts: 0.01 us -> 3.74 us
    gather x1 -> x2, local copies, waits for them, and re-layouts: 11.5 us -> 14 us  [gather_rows(): picked = jnp.take(orbitals, jnp.clip(local_pos, 0, row_count - 1), axis=0)]
where the time goes in v2:
time: 257 us; the launch traced here: 256 us
  blocking collectives  148 us (58%)
  Pallas kernels  59.3 us (23%)
  waiting for transfers between devices  18.4 us (7%)
  local copies, waits for them, and re-layouts  17.8 us (7%)
  other arithmetic  6.27 us (2%)
  starting transfers between devices  6.01 us (2%)
    psum x1, blocking collectives, gather_rows(): return lax.psum(picked, BOTH).astype(BF)  107 us
    pallas_call x1, Pallas kernels, make_pairs(): pl.pallas_call(pair_kernel, grid=(steps,), in_specs=[pl.BlockSpec((CELLS,...  33.3 us
    all_to_all x1, blocking collectives, shards(): got = lax.all_to_all(ret.reshape(devices, ROWS, 128), BOTH, 0, 0)  23.2 us
    all_to_all x1, blocking collectives, shards(): parts = lax.all_to_all(parts, BOTH, 0, 0)  18.5 us
    all_to_all x1, waiting for transfers between devices, shards(): planes = lax.all_to_all(send.reshape(devices, ROWS, 128), BOTH, 0, 0)  18.4 us
    pallas_call x1, Pallas kernels, project(): pl.pallas_call(project_kernel, grid=(steps,), in_specs=[whole(got.shape),...  16.1 us
    gather x2, local copies, waits for them, and re-layouts, gather_rows(): picked = jnp.take(orbitals, jnp.clip(local_pos, 0, row_count - 1), axis=0)  14 us
    pallas_call x1, Pallas kernels, solve(): pl.pallas_call(solve_kernel, in_specs=[pl.BlockSpec(memory_space=pltpu.SM...  9.9 us
  transfers between devices with their start and end apart: 1, of which 1 were waited for; matrix products, arithmetic and copies ran while one was open for 0% of the time, Pallas kernels for 0%

profile of v2, /device:TPU:1, one launch (start us, length us, event | category | flops | bytes accessed | tf_op | source)
XLA Modules:
  0.0 256.3 jit_solution(10372277821565073394)
XLA Ops:
  0.0 0.7 compare_and_fusion.1
  0.7 0.7 fusion
  1.4 1.2 copy.13
  2.6 0.3 pad_maximum_fusion.panel
  2.9 11.5 %gather_fusion = bf16[2048,512]{1,0:T(8,128)(2,1)S(1)} fusion(bf16[6912,512]{1,0:T(8,128)(2,1)} %orb.1, s32[2048]{0:T(1024)S(1)} %fusion), kind=kCustom, calls=%fused_computation | custom fusion | bytes 4202496 | tf_op jit(solution)/shard_map/jit(_take)/gather | solution.py:255
  14.5 2.5 copy.12
  17.0 3.8 %select_convert_fusion = f32[2048,512]{0,1:T(8,128)} fusion(bf16[2048,512]{0,1:T(8,128)(2,1)} %copy.12, pred[2048]{0:T(1024)(128)(4,1)S(1)} %get-tuple-element.10, pred[2048]{0:T(1024)(128)(4,1)S(1)} %get-tuple-element.9), kind=kLoop, calls=%fused_computation.2 | loop fusion | flops 3145728 | bytes 6295552 | tf_op jit(solution)/shard_map/convert_element_type | solution.py:256
  20.8 0.0 copy-start.4
  20.8 106.7 %all-reduce.1 = bf16[2048,512]{0,1:T(8,128)(2,1)S(1)} all-reduce(f32[2048,512]{0,1:T(8,128)} %select_convert_fusion), channel_id=1, replica_groups=mesh['grid'=16,'vec'=8] {'grid','vec'}, use_global_device_ids=true, to_apply=%region_0.1 | all-reduce | flops 1048576 | bytes 6291456 | tf_op jit(solution)/shard_map/psum | solution.py:257
  127.5 0.0 copy-done.4
  127.5 0.0 copy-start
  127.6 1.5 copy-done
  129.0 33.3 %pairs.1 = (bf16[6912,2048]{1,0:T(8,128)(2,1)}, bf16[32,4,32,128]{3,2,1,0:T(8,128)(2,1)S(1)}) custom-call(bf16[6912,512]{1,0:T(8,128)(2,1)} %orb.1, bf16[512,2048]{1,0:T(8,128)(2,1)S(1)} %bitcast.8, bf16[2048,128]{1,0:T(8,128)(2,1)S(1)} %pad_maximum_fusion.panel, bf16[1024,864]{1,0:T(8,128)(2,1)S(1)} %copy-done, bf16[512,512]{1,0:T(8,128)(2,1)S(1)} %copy-done.4), custom_call_target="tpu_custom_call" | custom-call | tf_op jit(solution)/shard_map/pairs/pallas_call | solution.py:105
  162.3 0.0 copy-start.2
  162.3 1.0 copy-done.2
  163.3 0.0 copy-start.5
  163.3 0.0 copy-start.6
  163.4 6.0 %all-to-all-start = ((bf16[128,32,128]{2,1,0:T(8,128)(2,1)}), bf16[128,32,128]{2,1,0:T(8,128)(2,1)S(1)}, u32[]{:S(2)}, u32[]{:S(2)}) async-start(bf16[128,32,128]{2,1,0:T(8,128)(2,1)} %bitcast.12), calls=%async_computation | async-start | bytes 2097152 | tf_op jit(solution)/shard_map/all_to_all | solution.py:269
  169.4 18.4 %all-to-all-done = bf16[128,32,128]{2,1,0:T(8,128)(2,1)S(1)} async-done(((bf16[128,32,128]{2,1,0:T(8,128)(2,1)}), bf16[128,32,128]{2,1,0:T(8,128)(2,1)S(1)}, u32[]{:S(2)}, u32[]{:S(2)}) %all-to-all-start) | async-done | bytes 1048608 | tf_op jit(solution)/shard_map/all_to_all | solution.py:269
  187.7 0.0 copy-done.5
  187.7 0.0 copy-done.6
  187.7 0.0 copy-start.3
  187.8 9.9 %solve.1 = bf16[4096,128]{1,0:T(8,128)(2,1)S(1)} custom-call(s32[1]{0:T(128)} %bitcast.first, bf16[4096,128]{1,0:T(8,128)(2,1)S(1)} %bitcast.9, bf16[1536,1536]{1,0:T(8,128)(2,1)} %constant.70.clone.wide, bf16[1536,1536]{1,0:T(8,128)(2,1)} %constant.71.clone.wide_t, bf16[96,96]{1,0:T(8,128)(2,1)S(1)} %copy-done.6, bf16[96,96]{1,0:T(8,128)(2,1)S(1)} %copy-done.5), custom_call_target="tpu_custom_call" | custom-call | tf_op jit(solution)/shard_map/solve/pallas_call | solution.py:171
  197.7 0.0 copy-start.1
  197.7 23.2 %all_to_all.15 = bf16[128,32,128]{2,1,0:T(8,128)(2,1)S(1)} all-to-all(bf16[128,32,128]{2,1,0:T(8,128)(2,1)S(1)} %bitcast.10), channel_id=1, replica_groups=mesh['grid'=16,'vec'=8] {'grid','vec'}, dimensions={0} | all-to-all | bytes 2097152 | tf_op jit(solution)/shard_map/all_to_all | solution.py:272
  220.8 0.0 copy-done.3
  220.8 0.0 copy-done.1
  220.8 16.1 %project.1 = f32[128,8,128]{2,1,0:T(8,128)S(1)} custom-call(bf16[32,4,32,128]{3,2,1,0:T(8,128)(2,1)S(1)} %bitcast.11, bf16[512,512]{1,0:T(8,128)(2,1)S(1)} %copy-done.3, bf16[864,1024]{1,0:T(8,128)(2,1)S(1)} %copy-done.1, bf16[6912,2048]{1,0:T(8,128)(2,1)} %get-tuple-element.8.pair), custom_call_target="tpu_custom_call" | custom-call | tf_op jit(solution)/shard_map/project/pallas_call | solution.py:230
  237.0 18.5 %all_to_all.16 = f32[128,8,128]{2,1,0:T(8,128)S(1)} all-to-all(f32[128,8,128]{2,1,0:T(8,128)S(1)} %project.1), channel_id=1, replica_groups=mesh['grid'=16,'vec'=8] {'grid','vec'}, dimensions={0} | all-to-all | bytes 1048576 | tf_op jit(solution)/shard_map/all_to_all | solution.py:274
  255.5 0.1 reduce_sum.9
  255.6 0.1 fusion.1
  255.7 0.6 pad_maximum_fusion.1
Async XLA Ops:
  20.8 106.8 %copy-start.4 = (bf16[512,512]{1,0:T(8,128)(2,1)S(1)}, bf16[512,512]{1,0:T(8,128)(2,1)}, u32[]{:S(2)}) copy-start(bf16[512,512]{1,0:T(8,128)(2,1)} %constant.69.clone.swap) | copy-start | bytes 1572868
  127.5 1.5 copy-start
  162.3 1.0 copy-start.2
  163.3 24.4 %copy-start.5 = (bf16[96,96]{1,0:T(8,128)(2,1)S(1)}, bf16[96,96]{1,0:T(8,128)(2,1)}, u32[]{:S(2)}) copy-start(bf16[96,96]{1,0:T(8,128)(2,1)} %constant.73.clone.x_back) | copy-start | bytes 55300
  163.3 24.4 %copy-start.6 = (bf16[96,96]{1,0:T(8,128)(2,1)S(1)}, bf16[96,96]{1,0:T(8,128)(2,1)}, u32[]{:S(2)}) copy-start(bf16[96,96]{1,0:T(8,128)(2,1)} %constant.72.clone.x_ahead) | copy-start | bytes 55300
  163.4 24.4 %all-to-all-start = ((bf16[128,32,128]{2,1,0:T(8,128)(2,1)}), bf16[128,32,128]{2,1,0:T(8,128)(2,1)S(1)}, u32[]{:S(2)}, u32[]{:S(2)}) async-start(bf16[128,32,128]{2,1,0:T(8,128)(2,1)} %bitcast.12), calls=%async_computation | async-start | bytes 2097152 | tf_op jit(solution)/shard_map/all_to_all | solution.py:269
  187.7 33.1 %copy-start.3 = (bf16[512,512]{1,0:T(8,128)(2,1)S(1)}, bf16[512,512]{1,0:T(8,128)(2,1)}, u32[]{:S(2)}) copy-start(bf16[512,512]{1,0:T(8,128)(2,1)} %constant.74.clone.unswap) | copy-start | bytes 1572868
  197.7 23.2 %copy-start.1 = (bf16[864,1024]{1,0:T(8,128)(2,1)S(1)}, bf16[864,1024]{1,0:T(8,128)(2,1)}, u32[]{:S(2)}) copy-start(bf16[864,1024]{1,0:T(8,128)(2,1)} %constant.75.clone.back) | copy-start | bytes 5308420

commit v3 on v2

--- a/solution.py
+++ b/solution.py
@@ -248,13 +248,110 @@
     )(got, const(tab["unswap"]), const(tab["back"]), pair)
 
 
-def gather_rows(orbitals, points, me):
+ROOM = 32
+GROUP = 320
+
+
+def parts_of(device):
+    grid, vec = device // 8, device % 8
+    return grid // 4, (vec // 4) * 2 + (grid // 2) % 2, grid % 2, vec % 4
+
+
+def device_at(z, x, core, y):
+    return (z * 4 + (x % 2) * 2 + core) * 8 + (x // 2) * 4 + y
+
+
+def bring(data, dz=0, dx=0, dcore=0, dy=0):
+    pairs = []
+    for device in range(128):
+        z, x, core, y = parts_of(device)
+        source = device_at((z + dz) % 4, (x + dx) % 4, (core + dcore) % 2, (y + dy) % 4)
+        pairs.append((source, device))
+    return lax.ppermute(data, BOTH, pairs)
+
+
+def place_kernel(count, slot, *refs):
+    blocks, out, turned = refs[:count], refs[count], refs[count + 1]
+    start = 0
+    for block in blocks:
+        rows = block.shape[0]
+        turned[start : start + rows, :] = block[...]
+        start += rows
+    slots = turned.shape[0]
+    chunk = 256
+    for first in range(0, slot.shape[1], chunk):
+        index = lax.broadcasted_iota(jnp.int32, (slots, chunk), 0)
+        pick = jnp.where(index == slot[:, first : first + chunk], 1.0, 0.0).astype(BF)
+        out[:, first : first + chunk] = lax.dot_general(
+            turned[...], pick, (((0,), (0,)), ((), ())), preferred_element_type=F32
+        ).astype(BF)
+
+
+def place(slot, blocks):
+    vmem = pl.BlockSpec(memory_space=pltpu.VMEM)
+    norb = blocks[0].shape[1]
+    slots = sum(block.shape[0] for block in blocks)
+    return pl.pallas_call(
+        functools.partial(place_kernel, len(blocks)),
+        in_specs=[vmem] * (1 + len(blocks)),
+        out_specs=vmem,
+        out_shape=jax.ShapeDtypeStruct((norb, slot.shape[0]), BF),
+        scratch_shapes=[pltpu.VMEM((slots, norb), BF)],
+        compiler_params=pltpu.CompilerParams(vmem_limit_bytes=32 * 2**20),
+        name="place",
+    )(slot[None], *blocks)
+
+
+def summed_rows(orbitals, points, me):
     row_count = orbitals.shape[0]
     local_pos = points - me * row_count
     inside = (local_pos >= 0) & (local_pos < row_count)
     picked = jnp.take(orbitals, jnp.clip(local_pos, 0, row_count - 1), axis=0)
     picked = jnp.where(inside[:, None], picked, jnp.zeros_like(picked)).astype(F32)
-    return lax.psum(picked, BOTH).astype(BF)
+    return lax.psum(picked, BOTH).astype(BF).T
+
+
+def ranks(label):
+    index = lax.iota(jnp.int32, label.shape[0])
+    same = (label[:, None] == label[None, :]) & (index[:, None] < index[None, :])
+    return jnp.sum(same.astype(jnp.int32), axis=0)
+
+
+def spread_rows(orbitals, points, me, owner, own_rank, group_rank):
+    row_count = orbitals.shape[0]
+    z, x, core, y = parts_of(owner)
+    my_z, my_x, my_core, my_y = parts_of(me)
+    room = lax.iota(jnp.int32, ROOM)
+    mine = (owner == me)[None] & (own_rank[None] == room[:, None])
+    pick = jnp.sum(jnp.where(mine, (points - me * row_count)[None], 0), axis=1)
+    own = jnp.take(orbitals, pick, axis=0)
+    line = jnp.concatenate([own] + [bring(own, dy=d) for d in (1, 2, 3)], axis=0)
+    square = jnp.concatenate([line] + [bring(line, dz=d) for d in (1, 2, 3)], axis=0)
+    spot = (z - my_z) % 4 * (4 * ROOM) + (y - my_y) % 4 * ROOM + own_rank
+    group = lax.iota(jnp.int32, GROUP)
+    here = ((x == my_x) & (core == my_core))[None] & (group_rank[None] == group[:, None])
+    source = jnp.sum(jnp.where(here, spot[None] + 1, 0), axis=1) - 1
+    choose = source[:, None] == lax.iota(jnp.int32, 16 * ROOM)[None]
+    held = mm(choose.astype(BF), square).astype(BF)
+    right, left = bring(held, dx=1), bring(held, dx=3)
+    half = GROUP // 2
+    far_a, far_b = bring(right[:half], dx=1), bring(left[half:], dx=3)
+    blocks = [held, right, far_a, far_b, left]
+    blocks = blocks + [bring(block, dcore=1) for block in blocks]
+    slot = ((core - my_core) % 2 * 4 + (x - my_x) % 4) * GROUP + group_rank
+    return place(slot, blocks)
+
+
+def gather_rows(orbitals, points, me):
+    owner = points // orbitals.shape[0]
+    _, x, core, _ = parts_of(owner)
+    own_rank, group_rank = ranks(owner), ranks(x * 2 + core)
+    fits = (jnp.max(own_rank) < ROOM) & (jnp.max(group_rank) < GROUP)
+    return lax.cond(
+        fits,
+        lambda: spread_rows(orbitals, points, me, owner, own_rank, group_rank),
+        lambda: summed_rows(orbitals, points, me),
+    )
 
 
 def shards(orbitals, inverse_panel, points):
@@ -263,7 +360,7 @@
     devices = lax.axis_size("grid") * vec_count
     me = lax.axis_index("grid") * vec_count + lax.axis_index("vec")
     npoints, cols = inverse_panel.shape
-    rows_t = gather_rows(orbitals, points, me).T
+    rows_t = gather_rows(orbitals, points, me)
     panel2 = jnp.concatenate([inverse_panel, inverse_panel], axis=1)
     pair, send = make_pairs(orbitals, rows_t, panel2, tab)
     planes = lax.all_to_all(send.reshape(devices, ROWS, 128), BOTH, 0, 0)

time: 257 us -> 192 us (0.75)
  blocking collectives: 148 us -> 41.7 us
  starting transfers between devices: 6.01 us -> 35.4 us
  local copies, waits for them, and re-layouts: 17.8 us -> 5.95 us
  waiting for transfers between devices: 18.4 us -> 27.3 us
  Pallas kernels: 59.3 us -> 67.5 us
  other arithmetic: 6.27 us -> 12.1 us
    psum x1 -> x0, blocking collectives: 107 us -> none  [gather_rows(): return lax.psum(picked, BOTH).astype(BF)]
    ppermute x0 -> x15, starting transfers between devices: none -> 27.8 us  [bring(): return lax.ppermute(data, BOTH, pairs)]
    gather x2 -> x1, local copies, waits for them, and re-layouts: 14 us -> 4.55 us  [spread_rows(): own = jnp.take(orbitals, pick, axis=0)]
    ppermute x0 -> x15, waiting for transfers between devices: none -> 8.96 us  [bring(): return lax.ppermute(data, BOTH, pairs)]
    reduce_sum x0 -> x3, other arithmetic: none -> 7.92 us  [the longest x1 7.13 us: ranks(): return jnp.sum(same.astype(jnp.int32), axis=0)]
    pallas_call x0 -> x1, Pallas kernels: none -> 7.08 us  [place(): pl.pallas_call(functools.partial(place_kernel, len(blocks)), in_specs=[vm...]
    convert_element_type x1 -> x0, other arithmetic: 3.82 us -> none  [gather_rows(): jnp.where(inside[:, None], picked, jnp.zeros_like(picked)).astype(F32)]
  transfers between devices with their start and end apart: 1 -> 16, of which waited for: 1 -> 6; matrix products, arithmetic and copies ran while one was open for 0% -> 0% of each run, Pallas kernels for 0% -> 0%
where the time goes in v3:
time: 192 us
  Pallas kernels  67.5 us (35%)
  blocking collectives  41.7 us (22%)
  starting transfers between devices  35.4 us (18%)
  waiting for transfers between devices  27.3 us (14%)
  other arithmetic  12.1 us (6%)
  local copies, waits for them, and re-layouts  5.95 us (3%)
    pallas_call x1, Pallas kernels, make_pairs(): pl.pallas_call(pair_kernel, grid=(steps,), in_specs=[pl.BlockSpec((CELLS,...  34.4 us
    ppermute x15, starting transfers between devices, bring(): return lax.ppermute(data, BOTH, pairs)  27.8 us
    all_to_all x1, blocking collectives, shards(): got = lax.all_to_all(ret.reshape(devices, ROWS, 128), BOTH, 0, 0)  23.2 us
    all_to_all x1, blocking collectives, shards(): parts = lax.all_to_all(parts, BOTH, 0, 0)  18.5 us
    all_to_all x1, waiting for transfers between devices, shards(): planes = lax.all_to_all(send.reshape(devices, ROWS, 128), BOTH, 0, 0)  18.3 us
    pallas_call x1, Pallas kernels, project(): pl.pallas_call(project_kernel, grid=(steps,), in_specs=[whole(got.shape),...  16.1 us
    pallas_call x1, Pallas kernels, solve(): pl.pallas_call(solve_kernel, in_specs=[pl.BlockSpec(memory_space=pltpu.SM...  9.99 us
    ppermute x15, waiting for transfers between devices, bring(): return lax.ppermute(data, BOTH, pairs)  8.96 us
  transfers between devices with their start and end apart: 16, of which 6 were waited for; matrix products, arithmetic and copies ran while one was open for 0% of the time, Pallas kernels for 0%

profile of v3, /device:TPU:1, one launch (start us, length us, event | category | flops | bytes accessed | tf_op | source)
XLA Modules:
  0.0 191.9 jit_solution(2456958547945975741)
XLA Ops:
  0.0 0.7 fusion.36
  0.7 7.1 %convert_reduce_fusion = (s32[2048]{0:T(1024)S(1)}, s32[2048]{0:T(1024)S(1)}) fusion(s32[2048]{0:T(1024)S(1)} %get-tuple-element.49, s32[2048]{0:T(1024)S(1)} %get-tuple-element.50), kind=kLoop, calls=%fused_computation.96 | loop fusion | flops 37744640 | bytes 32768 | tf_op jit(solution)/shard_map/reduce_sum | solution.py:317
  7.9 0.7 reduce_max.18
  8.5 0.7 reduce_max.19
  10.5 1.2 copy.16
  12.0 50.9 %conditional.1 = (bf16[512,2048]{1,0:T(8,128)(2,1)}) conditional(s32[]{:T(128)} %convert_element_type.21, (s32[]{:T(128)}, s32[2048]{0:T(1024)}, bf16[6912,512]{1,0:T(8,128)(2,1)}) %tuple.11, (s32[2048]{0:T(1024)S(1)}, s32[]{:T(128)}, s32[2048]{0:T(1024)S(1)}, s32[2048]{0:T(1024)S(1)}, s32[2048]{0:T(1024)}, ...), branch_computations={%region_4.6_spmd, %region_6.9_spmd} | conditional | flops 171896144 | bytes 21012508 | solution.py:350
  12.2 0.9 fusion.19
  13.3 4.6 %gather_fusion = bf16[32,512]{1,0:T(8,128)(2,1)S(1)} fusion(bf16[6912,512]{1,0:T(8,128)(2,1)} %get-tuple-element.34, s32[1024]{0:T(1024)S(1)} %pad_clamp_fusion), kind=kCustom, calls=%fused_computation.1 | custom fusion | bytes 65664 | tf_op jit(solution)/shard_map/cond/branch_1_fun/jit(_take)/gather | solution.py:327
  17.9 2.1 %collective-permute-start.2 = (bf16[32,512]{1,0:T(8,128)(2,1)S(1)}, bf16[32,512]{1,0:T(8,128)(2,1)S(1)}, u32[]{:S(2)}, u32[]{:S(2)}) collective-permute-start(bf16[32,512]{1,0:T(8,128)(2,1)S(1)} %get-tuple-element.42), channel_id=1, source_target_pairs={{3,0},{0,1},{1,2},{2,3},{7,4},{4,5},{5,6},{6,7},{11,8},{8,9},{9,10... | collective-permute-start | bytes 98312 | tf_op jit(solution)/shard_map/cond/branch_1_fun/ppermute | solution.py:270
  20.1 2.6 %collective-permute-start.1 = (bf16[32,512]{1,0:T(8,128)(2,1)S(1)}, bf16[32,512]{1,0:T(8,128)(2,1)S(1)}, u32[]{:S(2)}, u32[]{:S(2)}) collective-permute-start(bf16[32,512]{1,0:T(8,128)(2,1)S(1)} %get-tuple-element.42), channel_id=1, source_target_pairs={{2,0},{3,1},{0,2},{1,3},{6,4},{7,5},{4,6},{5,7},{10,8},{11,9},{8,1... | collective-permute-start | bytes 98312 | tf_op jit(solution)/shard_map/cond/branch_1_fun/ppermute | solution.py:270
  22.7 1.1 collective-permute-start
  24.4 1.3 collective-permute-done
  25.7 1.7 collective-permute-start.5
  27.5 3.3 %collective-permute-start.4 = (bf16[128,512]{1,0:T(8,128)(2,1)S(1)}, bf16[128,512]{1,0:T(8,128)(2,1)S(1)}, u32[]{:S(2)}, u32[]{:S(2)}) collective-permute-start(bf16[128,512]{1,0:T(8,128)(2,1)S(1)} %pad_maximum_fusion), channel_id=1, source_target_pairs={{64,0},{65,1},{66,2},{67,3},{68,4},{69,5},{70,6},{71,7},{72,8},{73... | collective-permute-start | bytes 393224 | tf_op jit(solution)/shard_map/cond/branch_1_fun/ppermute | solution.py:270
  30.8 0.7 collective-permute-start.3
  31.5 4.3 %collective-permute-done.3 = bf16[128,512]{1,0:T(8,128)(2,1)S(1)} collective-permute-done((bf16[128,512]{1,0:T(8,128)(2,1)S(1)}, bf16[128,512]{1,0:T(8,128)(2,1)S(1)}, u32[]{:S(2)}, u32[]{:S(2)}) %collective-permute-start.3) | collective-permute-done | bytes 131104 | tf_op jit(solution)/shard_map/cond/branch_1_fun/ppermute | solution.py:270
  36.2 1.3 collective-permute-start.8
  37.5 1.5 collective-permute-start.6
  39.0 3.2 %collective-permute-start.10 = (bf16[320,512]{1,0:T(8,128)(2,1)S(1)}, bf16[320,512]{1,0:T(8,128)(2,1)S(1)}, u32[]{:S(2)}, u32[]{:S(2)}) collective-permute-start(bf16[320,512]{1,0:T(8,128)(2,1)S(1)} %convolution_convert_fusion.refs_0_), channel_id=1, source_target_pairs={{8,0},{9,1},{10,2},{11,3},{12,4},{13,5},{14,6},{15,7},{0,8},{1,9},... | collective-permute-start | bytes 983048 | tf_op jit(solution)/shard_map/cond/branch_1_fun/ppermute | solution.py:270
  42.1 1.9 %collective-permute-done.8.refs_4_ = bf16[320,512]{1,0:T(8,128)(2,1)S(1)} collective-permute-done((bf16[320,512]{1,0:T(8,128)(2,1)S(1)}, bf16[320,512]{1,0:T(8,128)(2,1)S(1)}, u32[]{:S(2)}, u32[]{:S(2)}) %collective-permute-start.8) | collective-permute-done | bytes 327712 | tf_op jit(solution)/shard_map/cond/branch_1_fun/ppermute | solution.py:270
  44.4 2.7 %collective-permute-start.7 = (bf16[160,512]{1,0:T(8,128)(2,1)S(1)}, bf16[160,512]{1,0:T(8,128)(2,1)S(1)}, u32[]{:S(2)}, u32[]{:S(2)}) collective-permute-start(bf16[160,512]{1,0:T(8,128)(2,1)S(1)} %slice.18), channel_id=1, source_target_pairs={{16,0},{17,1},{18,2},{19,3},{20,4},{21,5},{22,6},{23,7},{24,8},{25... | collective-permute-start | bytes 491528 | tf_op jit(solution)/shard_map/cond/branch_1_fun/ppermute | solution.py:270
  47.1 4.1 %collective-permute-start.14 = (bf16[320,512]{1,0:T(8,128)(2,1)S(1)}, bf16[320,512]{1,0:T(8,128)(2,1)S(1)}, u32[]{:S(2)}, u32[]{:S(2)}) collective-permute-start(bf16[320,512]{1,0:T(8,128)(2,1)S(1)} %collective-permute-done.8.refs_4_), channel_id=1, source_target_pairs={{8,0},{9,1},{10,2},{11,3},{12,4},{13,5},{14,6},{15,7},{0,8},{1,9},... | collective-permute-start | bytes 983048 | tf_op jit(solution)/shard_map/cond/branch_1_fun/ppermute | solution.py:270
  51.2 3.2 %collective-permute-start.13 = (bf16[160,512]{1,0:T(8,128)(2,1)S(1)}, bf16[160,512]{1,0:T(8,128)(2,1)S(1)}, u32[]{:S(2)}, u32[]{:S(2)}) collective-permute-start(bf16[160,512]{1,0:T(8,128)(2,1)S(1)} %collective-permute-done.9.refs_3_), channel_id=1, source_target_pairs={{8,0},{9,1},{10,2},{11,3},{12,4},{13,5},{14,6},{15,7},{0,8},{1,9},... | collective-permute-start | bytes 491528 | tf_op jit(solution)/shard_map/cond/branch_1_fun/ppermute | solution.py:270
  54.4 1.0 collective-permute-done.13.refs_8_
  55.8 7.1 %place.1 = bf16[512,2048]{1,0:T(8,128)(2,1)} custom-call(s32[1,2048]{1,0:T(1,128)S(1)} %bitcast.17, bf16[320,512]{1,0:T(8,128)(2,1)S(1)} %convolution_convert_fusion.refs_0_, bf16[320,512]{1,0:T(8,128)(2,1)S(1)} %collective-permute-done.6.refs_1_, bf16[160,512]{1,0:T(8,128)(2,1)S(1)} %collective-permute-done.7.refs_2_, ...), custom_call_target="tpu_custom_call" | custom-call | tf_op jit(solution)/shard_map/cond/branch_1_fun/place/pallas_call | solution.py:294
  62.9 34.4 %pairs.1 = (bf16[6912,2048]{1,0:T(8,128)(2,1)}, bf16[32,4,32,128]{3,2,1,0:T(8,128)(2,1)}) custom-call(bf16[6912,512]{1,0:T(8,128)(2,1)} %orb.1, bf16[512,2048]{1,0:T(8,128)(2,1)} %get-tuple-element.55.rows_t, bf16[2048,128]{1,0:T(8,128)(2,1)S(1)} %pad_maximum_fusion.1.panel, bf16[1024,864]{1,0:T(8,128)(2,1)S(1)} %copy-done, bf16[512,512]{1,0:T(8,128)(2,1)S(1)} %copy-done.3), custom_call_target="tpu_custom_call" | custom-call | tf_op jit(solution)/shard_map/pairs/pallas_call | solution.py:105
  97.3 7.7 %all-to-all-start = ((bf16[128,32,128]{2,1,0:T(8,128)(2,1)}), bf16[128,32,128]{2,1,0:T(8,128)(2,1)S(1)}, u32[]{:S(2)}, u32[]{:S(2)}) async-start(bf16[128,32,128]{2,1,0:T(8,128)(2,1)} %bitcast.5), calls=%async_computation | async-start | bytes 2097152 | tf_op jit(solution)/shard_map/all_to_all | solution.py:366
  105.0 18.3 %all-to-all-done = bf16[128,32,128]{2,1,0:T(8,128)(2,1)S(1)} async-done(((bf16[128,32,128]{2,1,0:T(8,128)(2,1)}), bf16[128,32,128]{2,1,0:T(8,128)(2,1)S(1)}, u32[]{:S(2)}, u32[]{:S(2)}) %all-to-all-start) | async-done | bytes 1048608 | tf_op jit(solution)/shard_map/all_to_all | solution.py:366
  123.3 10.0 %solve.1 = bf16[4096,128]{1,0:T(8,128)(2,1)S(1)} custom-call(s32[1]{0:T(128)} %bitcast.4.first, bf16[4096,128]{1,0:T(8,128)(2,1)S(1)} %bitcast.14, bf16[1536,1536]{1,0:T(8,128)(2,1)} %constant.301.clone.wide, bf16[1536,1536]{1,0:T(8,128)(2,1)} %constant.302.clone.wide_t, bf16[96,96]{1,0:T(8,128)(2,1)S(1)} %copy-done.5, bf16[96,96]{1,0:T(8,128)(2,1)S(1)} %copy-done.4), custom_call_target="tpu_custom_call" | custom-call | tf_op jit(solution)/shard_map/solve/pallas_call | solution.py:171
  133.3 23.2 %all_to_all.15 = bf16[128,32,128]{2,1,0:T(8,128)(2,1)S(1)} all-to-all(bf16[128,32,128]{2,1,0:T(8,128)(2,1)S(1)} %bitcast.15), channel_id=1, replica_groups=mesh['grid'=16,'vec'=8] {'grid','vec'}, dimensions={0} | all-to-all | bytes 2097152 | tf_op jit(solution)/shard_map/all_to_all | solution.py:369
  156.5 16.1 %project.1 = f32[128,8,128]{2,1,0:T(8,128)S(1)} custom-call(bf16[32,4,32,128]{3,2,1,0:T(8,128)(2,1)S(1)} %bitcast.16, bf16[512,512]{1,0:T(8,128)(2,1)S(1)} %copy-done.2, bf16[864,1024]{1,0:T(8,128)(2,1)S(1)} %copy-done.1, bf16[6912,2048]{1,0:T(8,128)(2,1)} %get-tuple-element.38.pair), custom_call_target="tpu_custom_call" | custom-call | tf_op jit(solution)/shard_map/project/pallas_call | solution.py:230
  172.6 18.5 %all_to_all.16 = f32[128,8,128]{2,1,0:T(8,128)S(1)} all-to-all(f32[128,8,128]{2,1,0:T(8,128)S(1)} %project.1), channel_id=1, replica_groups=mesh['grid'=16,'vec'=8] {'grid','vec'}, dimensions={0} | all-to-all | bytes 1048576 | tf_op jit(solution)/shard_map/all_to_all | solution.py:371
  (48 shorter events, 3.2 us)
Async XLA Ops:
  12.0 50.9 %copy-start = (bf16[1024,864]{1,0:T(8,128)(2,1)S(1)}, bf16[1024,864]{1,0:T(8,128)(2,1)}, u32[]{:S(2)}) copy-start(bf16[1024,864]{1,0:T(8,128)(2,1)} %constant.299.clone.ahead) | copy-start | bytes 5308420
  12.0 50.9 %copy-start.3 = (bf16[512,512]{1,0:T(8,128)(2,1)S(1)}, bf16[512,512]{1,0:T(8,128)(2,1)}, u32[]{:S(2)}) copy-start(bf16[512,512]{1,0:T(8,128)(2,1)} %constant.300.clone.swap) | copy-start | bytes 1572868
  17.9 6.5 %collective-permute-start.2 = (bf16[32,512]{1,0:T(8,128)(2,1)S(1)}, bf16[32,512]{1,0:T(8,128)(2,1)S(1)}, u32[]{:S(2)}, u32[]{:S(2)}) collective-permute-start(bf16[32,512]{1,0:T(8,128)(2,1)S(1)} %get-tuple-element.42), channel_id=1, source_target_pairs={{3,0},{0,1},{1,2},{2,3},{7,4},{4,5},{5,6},{6,7},{11,8},{8,9},{9,10... | collective-permute-start | bytes 98312 | tf_op jit(solution)/shard_map/cond/branch_1_fun/ppermute | solution.py:270
  20.1 4.3 %collective-permute-start.1 = (bf16[32,512]{1,0:T(8,128)(2,1)S(1)}, bf16[32,512]{1,0:T(8,128)(2,1)S(1)}, u32[]{:S(2)}, u32[]{:S(2)}) collective-permute-start(bf16[32,512]{1,0:T(8,128)(2,1)S(1)} %get-tuple-element.42), channel_id=1, source_target_pairs={{2,0},{3,1},{0,2},{1,3},{6,4},{7,5},{4,6},{5,7},{10,8},{11,9},{8,1... | collective-permute-start | bytes 98312 | tf_op jit(solution)/shard_map/cond/branch_1_fun/ppermute | solution.py:270
  22.7 3.1 %collective-permute-start = (bf16[32,512]{1,0:T(8,128)(2,1)S(1)}, bf16[32,512]{1,0:T(8,128)(2,1)S(1)}, u32[]{:S(2)}, u32[]{:S(2)}) collective-permute-start(bf16[32,512]{1,0:T(8,128)(2,1)S(1)} %get-tuple-element.42), channel_id=1, source_target_pairs={{1,0},{2,1},{3,2},{0,3},{5,4},{6,5},{7,6},{4,7},{9,8},{10,9},{11,1... | collective-permute-start | bytes 98312 | tf_op jit(solution)/shard_map/cond/branch_1_fun/ppermute | solution.py:270
  25.7 10.1 %collective-permute-start.5 = (bf16[128,512]{1,0:T(8,128)(2,1)S(1)}, bf16[128,512]{1,0:T(8,128)(2,1)S(1)}, u32[]{:S(2)}, u32[]{:S(2)}) collective-permute-start(bf16[128,512]{1,0:T(8,128)(2,1)S(1)} %pad_maximum_fusion), channel_id=1, source_target_pairs={{96,0},{97,1},{98,2},{99,3},{100,4},{101,5},{102,6},{103,7},{104,8... | collective-permute-start | bytes 393224 | tf_op jit(solution)/shard_map/cond/branch_1_fun/ppermute | solution.py:270
  27.5 8.3 %collective-permute-start.4 = (bf16[128,512]{1,0:T(8,128)(2,1)S(1)}, bf16[128,512]{1,0:T(8,128)(2,1)S(1)}, u32[]{:S(2)}, u32[]{:S(2)}) collective-permute-start(bf16[128,512]{1,0:T(8,128)(2,1)S(1)} %pad_maximum_fusion), channel_id=1, source_target_pairs={{64,0},{65,1},{66,2},{67,3},{68,4},{69,5},{70,6},{71,7},{72,8},{73... | collective-permute-start | bytes 393224 | tf_op jit(solution)/shard_map/cond/branch_1_fun/ppermute | solution.py:270
  30.8 5.0 %collective-permute-start.3 = (bf16[128,512]{1,0:T(8,128)(2,1)S(1)}, bf16[128,512]{1,0:T(8,128)(2,1)S(1)}, u32[]{:S(2)}, u32[]{:S(2)}) collective-permute-start(bf16[128,512]{1,0:T(8,128)(2,1)S(1)} %pad_maximum_fusion), channel_id=1, source_target_pairs={{32,0},{33,1},{34,2},{35,3},{36,4},{37,5},{38,6},{39,7},{40,8},{41... | collective-permute-start | bytes 393224 | tf_op jit(solution)/shard_map/cond/branch_1_fun/ppermute | solution.py:270
  36.2 7.9 %collective-permute-start.8 = (bf16[320,512]{1,0:T(8,128)(2,1)S(1)}, bf16[320,512]{1,0:T(8,128)(2,1)S(1)}, u32[]{:S(2)}, u32[]{:S(2)}) collective-permute-start(bf16[320,512]{1,0:T(8,128)(2,1)S(1)} %convolution_convert_fusion.refs_0_), channel_id=1, source_target_pairs={{20,0},{21,1},{22,2},{23,3},{16,4},{17,5},{18,6},{19,7},{28,8},{29... | collective-permute-start | bytes 983048 | tf_op jit(solution)/shard_map/cond/branch_1_fun/ppermute | solution.py:270
  37.5 6.9 %collective-permute-start.6 = (bf16[320,512]{1,0:T(8,128)(2,1)S(1)}, bf16[320,512]{1,0:T(8,128)(2,1)S(1)}, u32[]{:S(2)}, u32[]{:S(2)}) collective-permute-start(bf16[320,512]{1,0:T(8,128)(2,1)S(1)} %convolution_convert_fusion.refs_0_), channel_id=1, source_target_pairs={{16,0},{17,1},{18,2},{19,3},{20,4},{21,5},{22,6},{23,7},{24,8},{25... | collective-permute-start | bytes 983048 | tf_op jit(solution)/shard_map/cond/branch_1_fun/ppermute | solution.py:270
  39.0 15.5 %collective-permute-start.10 = (bf16[320,512]{1,0:T(8,128)(2,1)S(1)}, bf16[320,512]{1,0:T(8,128)(2,1)S(1)}, u32[]{:S(2)}, u32[]{:S(2)}) collective-permute-start(bf16[320,512]{1,0:T(8,128)(2,1)S(1)} %convolution_convert_fusion.refs_0_), channel_id=1, source_target_pairs={{8,0},{9,1},{10,2},{11,3},{12,4},{13,5},{14,6},{15,7},{0,8},{1,9},... | collective-permute-start | bytes 983048 | tf_op jit(solution)/shard_map/cond/branch_1_fun/ppermute | solution.py:270
  44.1 7.1 %collective-permute-start.9 = (bf16[160,512]{1,0:T(8,128)(2,1)S(1)}, bf16[160,512]{1,0:T(8,128)(2,1)S(1)}, u32[]{:S(2)}, u32[]{:S(2)}) collective-permute-start(bf16[160,512]{1,0:T(8,128)(2,1)S(1)} %slice.19), channel_id=1, source_target_pairs={{20,0},{21,1},{22,2},{23,3},{16,4},{17,5},{18,6},{19,7},{28,8},{29... | collective-permute-start | bytes 491528 | tf_op jit(solution)/shard_map/cond/branch_1_fun/ppermute | solution.py:270
  44.4 10.0 %collective-permute-start.7 = (bf16[160,512]{1,0:T(8,128)(2,1)S(1)}, bf16[160,512]{1,0:T(8,128)(2,1)S(1)}, u32[]{:S(2)}, u32[]{:S(2)}) collective-permute-start(bf16[160,512]{1,0:T(8,128)(2,1)S(1)} %slice.18), channel_id=1, source_target_pairs={{16,0},{17,1},{18,2},{19,3},{20,4},{21,5},{22,6},{23,7},{24,8},{25... | collective-permute-start | bytes 491528 | tf_op jit(solution)/shard_map/cond/branch_1_fun/ppermute | solution.py:270
  47.1 8.3 %collective-permute-start.14 = (bf16[320,512]{1,0:T(8,128)(2,1)S(1)}, bf16[320,512]{1,0:T(8,128)(2,1)S(1)}, u32[]{:S(2)}, u32[]{:S(2)}) collective-permute-start(bf16[320,512]{1,0:T(8,128)(2,1)S(1)} %collective-permute-done.8.refs_4_), channel_id=1, source_target_pairs={{8,0},{9,1},{10,2},{11,3},{12,4},{13,5},{14,6},{15,7},{0,8},{1,9},... | collective-permute-start | bytes 983048 | tf_op jit(solution)/shard_map/cond/branch_1_fun/ppermute | solution.py:270
  51.2 4.6 %collective-permute-start.11 = (bf16[320,512]{1,0:T(8,128)(2,1)S(1)}, bf16[320,512]{1,0:T(8,128)(2,1)S(1)}, u32[]{:S(2)}, u32[]{:S(2)}) collective-permute-start(bf16[320,512]{1,0:T(8,128)(2,1)S(1)} %collective-permute-done.6.refs_1_), channel_id=1, source_target_pairs={{8,0},{9,1},{10,2},{11,3},{12,4},{13,5},{14,6},{15,7},{0,8},{1,9},... | collective-permute-start | bytes 983048 | tf_op jit(solution)/shard_map/cond/branch_1_fun/ppermute | solution.py:270
  51.2 4.2 %collective-permute-start.13 = (bf16[160,512]{1,0:T(8,128)(2,1)S(1)}, bf16[160,512]{1,0:T(8,128)(2,1)S(1)}, u32[]{:S(2)}, u32[]{:S(2)}) collective-permute-start(bf16[160,512]{1,0:T(8,128)(2,1)S(1)} %collective-permute-done.9.refs_3_), channel_id=1, source_target_pairs={{8,0},{9,1},{10,2},{11,3},{12,4},{13,5},{14,6},{15,7},{0,8},{1,9},... | collective-permute-start | bytes 491528 | tf_op jit(solution)/shard_map/cond/branch_1_fun/ppermute | solution.py:270
  54.4 1.4 collective-permute-start.12
  62.9 60.4 %copy-start.4 = (bf16[96,96]{1,0:T(8,128)(2,1)S(1)}, bf16[96,96]{1,0:T(8,128)(2,1)}, u32[]{:S(2)}) copy-start(bf16[96,96]{1,0:T(8,128)(2,1)} %constant.304.clone.x_back) | copy-start | bytes 55300
  62.9 60.4 %copy-start.5 = (bf16[96,96]{1,0:T(8,128)(2,1)S(1)}, bf16[96,96]{1,0:T(8,128)(2,1)}, u32[]{:S(2)}) copy-start(bf16[96,96]{1,0:T(8,128)(2,1)} %constant.303.clone.x_ahead) | copy-start | bytes 55300
  97.3 26.0 %all-to-all-start = ((bf16[128,32,128]{2,1,0:T(8,128)(2,1)}), bf16[128,32,128]{2,1,0:T(8,128)(2,1)S(1)}, u32[]{:S(2)}, u32[]{:S(2)}) async-start(bf16[128,32,128]{2,1,0:T(8,128)(2,1)} %bitcast.5), calls=%async_computation | async-start | bytes 2097152 | tf_op jit(solution)/shard_map/all_to_all | solution.py:366
  123.3 33.2 %copy-start.1 = (bf16[864,1024]{1,0:T(8,128)(2,1)S(1)}, bf16[864,1024]{1,0:T(8,128)(2,1)}, u32[]{:S(2)}) copy-start(bf16[864,1024]{1,0:T(8,128)(2,1)} %constant.306.clone.back) | copy-start | bytes 5308420
  123.3 33.2 %copy-start.2 = (bf16[512,512]{1,0:T(8,128)(2,1)S(1)}, bf16[512,512]{1,0:T(8,128)(2,1)}, u32[]{:S(2)}) copy-start(bf16[512,512]{1,0:T(8,128)(2,1)} %constant.305.clone.unswap) | copy-start | bytes 1572868

commit v4 on v3

--- a/solution.py
+++ b/solution.py
@@ -12,7 +12,7 @@
 NG = 96
 HALF = NG // 2
 SCREEN = 2.25
-BOTH = ("grid", "vec")
+AXES = ("z", "x_lo", "core", "x_hi", "y")
 BF = jnp.bfloat16
 F32 = jnp.float32
 
@@ -22,6 +22,7 @@
 CG, CI = 4, 16
 ROWS = 32
 CELLS = 8 * NG
+WIDE = 12 * NG
 
 
 def basis_table():
@@ -70,7 +71,7 @@
 def pair_kernel(orb, rows_t, panel, ahead, swap, pair, send, fit):
     step = pl.program_id(0)
     npts = rows_t.shape[1]
-    chunk = 512
+    chunk = 256
     total = jnp.zeros((CELLS, 128), F32)
     for start in range(0, npts, chunk):
         corr = mm(orb[...], rows_t[:, start : start + chunk])
@@ -212,7 +213,7 @@
                 pot[start : start + NG, :] = final[:, yi * 64 : (yi + 1) * 64].astype(BF)
         acc[...] = jnp.zeros_like(acc)
 
-    block = pot[pl.ds(pl.multiple_of(step * CELLS, CELLS), CELLS), :]
+    block = pot[pl.ds(pl.multiple_of(step * WIDE, WIDE), WIDE), :]
     acc[...] += lax.dot_general(
         block, pair[...], (((0,), (0,)), ((), ())), preferred_element_type=F32
     )
@@ -225,7 +226,7 @@
 
 
 def project(got, pair, tab):
-    steps = pair.shape[0] // CELLS
+    steps = pair.shape[0] // WIDE
     whole = lambda shape: pl.BlockSpec(shape, lambda i: (0,) * len(shape))
     return pl.pallas_call(
         project_kernel,
@@ -234,7 +235,7 @@
             whole(got.shape),
             whole(tab["unswap"].shape),
             whole(tab["back"].shape),
-            pl.BlockSpec((CELLS, pair.shape[1]), lambda i: (i, 0)),
+            pl.BlockSpec((WIDE, pair.shape[1]), lambda i: (i, 0)),
         ],
         out_specs=whole((128, 8, 128)),
         out_shape=jax.ShapeDtypeStruct((128, 8, 128), F32),
@@ -267,7 +268,7 @@
         z, x, core, y = parts_of(device)
         source = device_at((z + dz) % 4, (x + dx) % 4, (core + dcore) % 2, (y + dy) % 4)
         pairs.append((source, device))
-    return lax.ppermute(data, BOTH, pairs)
+    return lax.ppermute(data, AXES, pairs)
 
 
 def place_kernel(count, slot, *refs):
@@ -295,11 +296,11 @@
         functools.partial(place_kernel, len(blocks)),
         in_specs=[vmem] * (1 + len(blocks)),
         out_specs=vmem,
-        out_shape=jax.ShapeDtypeStruct((norb, slot.shape[0]), BF),
+        out_shape=jax.ShapeDtypeStruct((norb, slot.shape[1]), BF),
         scratch_shapes=[pltpu.VMEM((slots, norb), BF)],
         compiler_params=pltpu.CompilerParams(vmem_limit_bytes=32 * 2**20),
         name="place",
-    )(slot[None], *blocks)
+    )(slot, *blocks)
 
 
 def summed_rows(orbitals, points, me):
@@ -308,73 +309,144 @@
     inside = (local_pos >= 0) & (local_pos < row_count)
     picked = jnp.take(orbitals, jnp.clip(local_pos, 0, row_count - 1), axis=0)
     picked = jnp.where(inside[:, None], picked, jnp.zeros_like(picked)).astype(F32)
-    return lax.psum(picked, BOTH).astype(BF).T
-
-
-def ranks(label):
-    index = lax.iota(jnp.int32, label.shape[0])
-    same = (label[:, None] == label[None, :]) & (index[:, None] < index[None, :])
-    return jnp.sum(same.astype(jnp.int32), axis=0)
-
-
-def spread_rows(orbitals, points, me, owner, own_rank, group_rank):
+    return lax.psum(picked, AXES).astype(BF).T
+
+
+def index_kernel(me, points, orbitals, fits, own, choose, slot, picks, spots, near, sems, one):
+    npts = points.shape[1]
     row_count = orbitals.shape[0]
-    z, x, core, y = parts_of(owner)
-    my_z, my_x, my_core, my_y = parts_of(me)
-    room = lax.iota(jnp.int32, ROOM)
-    mine = (owner == me)[None] & (own_rank[None] == room[:, None])
-    pick = jnp.sum(jnp.where(mine, (points - me * row_count)[None], 0), axis=1)
-    own = jnp.take(orbitals, pick, axis=0)
-    line = jnp.concatenate([own] + [bring(own, dy=d) for d in (1, 2, 3)], axis=0)
-    square = jnp.concatenate([line] + [bring(line, dz=d) for d in (1, 2, 3)], axis=0)
-    spot = (z - my_z) % 4 * (4 * ROOM) + (y - my_y) % 4 * ROOM + own_rank
-    group = lax.iota(jnp.int32, GROUP)
-    here = ((x == my_x) & (core == my_core))[None] & (group_rank[None] == group[:, None])
-    source = jnp.sum(jnp.where(here, spot[None] + 1, 0), axis=1) - 1
-    choose = source[:, None] == lax.iota(jnp.int32, 16 * ROOM)[None]
-    held = mm(choose.astype(BF), square).astype(BF)
+    my_z, my_x, my_core, my_y = parts_of(me[0])
+    owner = ((points[...].astype(F32) + 0.5) * (1.0 / row_count)).astype(jnp.int32)
+    z, y, core = owner >> 5, owner & 3, (owner >> 3) & 1
+    x = ((owner >> 2) & 1) * 2 + ((owner >> 4) & 1)
+    group = x * 2 + core
+    size = 256
+    early = lax.broadcasted_iota(jnp.int32, (size, size), 0) < lax.broadcasted_iota(
+        jnp.int32, (size, size), 1
+    )
+    early = jnp.where(early, 1.0, 0.0).astype(BF)
+
+    def ranks(label, labels):
+        index = lax.broadcasted_iota(jnp.int32, (labels, size), 0)
+        seen = jnp.zeros((labels, 1), F32)
+        found = []
+        for first in range(0, npts, size):
+            match = jnp.where(index == label[:, first : first + size], 1.0, 0.0)
+            before = mm(match.astype(BF), early) + seen
+            found.append(jnp.sum(match * before, axis=0, keepdims=True))
+            seen = seen + jnp.sum(match, axis=1, keepdims=True)
+        return jnp.concatenate(found, axis=1).astype(jnp.int32), jnp.max(seen)
+
+    own_rank, own_most = ranks(owner, 128)
+    group_rank, group_most = ranks(group, 16)
+    fits[0] = ((own_most <= ROOM) & (group_most <= GROUP)).astype(jnp.int32)
+
+    def lookup(key, value, first, rows):
+        number = lax.broadcasted_iota(jnp.int32, (rows, 128), 0) + first
+        total = jnp.zeros((rows, 128), jnp.int32)
+        for start in range(0, npts, 128):
+            total = total + jnp.where(
+                key[:, start : start + 128] == number, value[:, start : start + 128], 0
+            )
+        return jnp.sum(total.astype(F32), axis=1, keepdims=True).astype(jnp.int32)
+
+    key = jnp.where(owner == me[0], own_rank, -1)
+    pick = lookup(key, points[...] - me[0] * row_count, 0, ROOM)
+    picks[...] = jnp.broadcast_to(pick, (ROOM, 128))
+    move = pltpu.make_async_copy(picks, spots, one)
+    move.start()
+    move.wait()
+    copies = []
+    for place in range(ROOM):
+        start = pl.multiple_of((spots[place, 0] >> 4) << 4, 16)
+        copies.append(
+            pltpu.make_async_copy(
+                orbitals.at[pl.ds(start, 16), :],
+                near.at[pl.ds(place * 16, 16), :],
+                sems.at[place],
+            )
+        )
+        copies[-1].start()
+
+    spot = z * (4 * ROOM) + y * ROOM + own_rank
+    key = jnp.where((x == my_x) & (core == my_core), group_rank, -1)
+    for first in range(0, GROUP, 64):
+        source = lookup(key, spot + 1, first, 64) - 1
+        lane = lax.broadcasted_iota(jnp.int32, (64, 16 * ROOM), 1)
+        choose[first : first + 64, :] = jnp.where(source == lane, 1.0, 0.0).astype(BF)
+    slot[...] = (((core - my_core) & 1) * 4 + ((x - my_x) & 3)) * GROUP + group_rank
+    for copy in copies:
+        copy.wait()
+    lane = lax.broadcasted_iota(jnp.int32, (ROOM, 16 * ROOM), 1)
+    line = lax.broadcasted_iota(jnp.int32, (ROOM, 16 * ROOM), 0)
+    select = jnp.where(lane == line * 16 + (pick & 15), 1.0, 0.0).astype(BF)
+    own[...] = mm(select, near[...]).astype(BF)
+
+
+def index(me, points, orbitals):
+    vmem = pl.BlockSpec(memory_space=pltpu.VMEM)
+    smem = pl.BlockSpec(memory_space=pltpu.SMEM)
+    npts, norb = points.shape[0], orbitals.shape[1]
+    return pl.pallas_call(
+        index_kernel,
+        in_specs=[smem, vmem, pl.BlockSpec(memory_space=pl.ANY)],
+        out_specs=[smem, vmem, vmem, vmem],
+        out_shape=[
+            jax.ShapeDtypeStruct((1,), jnp.int32),
+            jax.ShapeDtypeStruct((ROOM, norb), BF),
+            jax.ShapeDtypeStruct((GROUP, 16 * ROOM), BF),
+            jax.ShapeDtypeStruct((1, npts), jnp.int32),
+        ],
+        scratch_shapes=[
+            pltpu.VMEM((ROOM, 128), jnp.int32),
+            pltpu.SMEM((ROOM, 128), jnp.int32),
+            pltpu.VMEM((16 * ROOM, norb), BF),
+            pltpu.SemaphoreType.DMA((ROOM,)),
+            pltpu.SemaphoreType.DMA,
+        ],
+        compiler_params=pltpu.CompilerParams(vmem_limit_bytes=16 * 2**20),
+        name="index",
+    )(me.reshape(1), points[None], orbitals)
+
+
+def gather_rows(orbitals, points, me):
+    fits, own, choose, slot = index(me, points, orbitals)
+    copies = jnp.broadcast_to(own[None], (16,) + own.shape)
+    square = lax.all_to_all(copies, ("z", "y"), 0, 0).reshape(16 * ROOM, own.shape[1])
+    held = mm(choose, square).astype(BF)
     right, left = bring(held, dx=1), bring(held, dx=3)
     half = GROUP // 2
     far_a, far_b = bring(right[:half], dx=1), bring(left[half:], dx=3)
     blocks = [held, right, far_a, far_b, left]
     blocks = blocks + [bring(block, dcore=1) for block in blocks]
-    slot = ((core - my_core) % 2 * 4 + (x - my_x) % 4) * GROUP + group_rank
-    return place(slot, blocks)
-
-
-def gather_rows(orbitals, points, me):
-    owner = points // orbitals.shape[0]
-    _, x, core, _ = parts_of(owner)
-    own_rank, group_rank = ranks(owner), ranks(x * 2 + core)
-    fits = (jnp.max(own_rank) < ROOM) & (jnp.max(group_rank) < GROUP)
     return lax.cond(
-        fits,
-        lambda: spread_rows(orbitals, points, me, owner, own_rank, group_rank),
+        fits[0] > 0,
+        lambda: place(slot, blocks),
         lambda: summed_rows(orbitals, points, me),
     )
 
 
 def shards(orbitals, inverse_panel, points):
     tab = tables()
-    vec_count = lax.axis_size("vec")
-    devices = lax.axis_size("grid") * vec_count
-    me = lax.axis_index("grid") * vec_count + lax.axis_index("vec")
+    devices = lax.axis_size(AXES)
+    me = lax.axis_index(AXES)
     npoints, cols = inverse_panel.shape
     rows_t = gather_rows(orbitals, points, me)
     panel2 = jnp.concatenate([inverse_panel, inverse_panel], axis=1)
     pair, send = make_pairs(orbitals, rows_t, panel2, tab)
-    planes = lax.all_to_all(send.reshape(devices, ROWS, 128), BOTH, 0, 0)
+    planes = lax.all_to_all(send.reshape(devices, ROWS, 128), AXES, 0, 0)
     first = (me // CG * MI).astype(jnp.int32).reshape(1)
     ret = solve(first, planes.reshape(devices * ROWS, 128), tab)
-    got = lax.all_to_all(ret.reshape(devices, ROWS, 128), BOTH, 0, 0)
+    got = lax.all_to_all(ret.reshape(devices, ROWS, 128), AXES, 0, 0)
     parts = project(got.reshape(MG, CG, ROWS, 128), pair, tab)
-    parts = lax.all_to_all(parts, BOTH, 0, 0)
+    parts = lax.all_to_all(parts, AXES, 0, 0)
     total = jnp.sum(parts, axis=0)
     return jnp.concatenate([total[:, :cols], total[:, cols:]], axis=0)
 
 
 def solution(mesh):
-    in_specs = (P(BOTH, None), P(), P())
+    fine = jax.sharding.Mesh(mesh.devices.reshape(4, 2, 2, 2, 4), AXES)
+    in_specs = (P(AXES, None), P(), P())
     return jax.shard_map(
-        shards, mesh=mesh, in_specs=in_specs, out_specs=P(BOTH, None), check_vma=False
+        shards, mesh=fine, in_specs=in_specs, out_specs=P(AXES, None), check_vma=False
     )

time: 192 us -> 175 us (0.911)
  blocking collectives: 41.7 us -> 60.8 us
  starting transfers between devices: 35.4 us -> 17.4 us
  other arithmetic: 12.1 us -> 1.03 us
  local copies, waits for them, and re-layouts: 5.95 us -> 1.14 us
  waiting for transfers between devices: 27.3 us -> 25.1 us
    all_to_all x2 -> x3, blocking collectives: 41.7 us -> 60.8 us  [the longest x1 23.2 us: shards(): got = lax.all_to_all(ret.reshape(devices, ROWS, 128), AXES, 0, 0)]
    ppermute x15 -> x9, starting transfers between devices: 27.8 us -> 11.4 us  [bring(): return lax.ppermute(data, AXES, pairs)]
    reduce_sum x3 -> x0, other arithmetic: 7.92 us -> none  [the longest x1 7.13 us: ranks(): return jnp.sum(same.astype(jnp.int32), axis=0)]
    gather x1 -> x0, local copies, waits for them, and re-layouts: 4.55 us -> none  [spread_rows(): own = jnp.take(orbitals, pick, axis=0)]
    pallas_call x0 -> x1, Pallas kernels: none -> 4.14 us  [index(): pl.pallas_call(index_kernel, in_specs=[smem, vmem, pl.BlockSpec(memory_sp...]
    pallas_call x1, Pallas kernels: 34.4 us -> 30.8 us  [make_pairs(): pl.pallas_call(pair_kernel, grid=(steps,), in_specs=[pl.BlockSpec((CELLS,...]
    ppermute x15 -> x9, waiting for transfers between devices: 8.96 us -> 6.84 us  [bring(): return lax.ppermute(data, AXES, pairs)]
  transfers between devices with their start and end apart: 16 -> 10, of which waited for: 6 -> 4; matrix products, arithmetic and copies ran while one was open for 0% -> 0% of each run, Pallas kernels for 0% -> 0%
where the time goes in v4:
time: 175 us
  Pallas kernels  68.2 us (39%)
  blocking collectives  60.8 us (35%)
  waiting for transfers between devices  25.1 us (14%)
  starting transfers between devices  17.4 us (10%)
    pallas_call x1, Pallas kernels, make_pairs(): pl.pallas_call(pair_kernel, grid=(steps,), in_specs=[pl.BlockSpec((CELLS,...  30.8 us
    all_to_all x1, blocking collectives, shards(): got = lax.all_to_all(ret.reshape(devices, ROWS, 128), AXES, 0, 0)  23.2 us
    all_to_all x1, blocking collectives, gather_rows(): lax.all_to_all(copies, ('z', 'y'), 0, 0).reshape(16 * ROOM, own.shape[1])  19.1 us
    all_to_all x1, blocking collectives, shards(): parts = lax.all_to_all(parts, AXES, 0, 0)  18.5 us
    all_to_all x1, waiting for transfers between devices, shards(): planes = lax.all_to_all(send.reshape(devices, ROWS, 128), AXES, 0, 0)  18.3 us
    pallas_call x1, Pallas kernels, project(): pl.pallas_call(project_kernel, grid=(steps,), in_specs=[whole(got.shape),...  14.6 us
    ppermute x9, starting transfers between devices, bring(): return lax.ppermute(data, AXES, pairs)  11.4 us
    pallas_call x1, Pallas kernels, solve(): pl.pallas_call(solve_kernel, in_specs=[pl.BlockSpec(memory_space=pltpu.SM...  9.9 us
  transfers between devices with their start and end apart: 10, of which 4 were waited for; matrix products, arithmetic and copies ran while one was open for 0% of the time, Pallas kernels for 0%

profile of v4, /device:TPU:1, one launch (start us, length us, event | category | flops | bytes accessed | tf_op | source)
XLA Modules:
  0.0 174.9 jit_solution(13420178498548166067)
XLA Ops:
  0.0 4.1 %index.1 = (s32[1]{0:T(128)}, bf16[32,512]{1,0:T(8,128)(2,1)S(1)}, bf16[320,512]{1,0:T(8,128)(2,1)S(1)}, s32[1,2048]{1,0:T(1,128)S(1)}) custom-call(s32[1]{0:T(128)} %bitcast.2.me, s32[1,2048]{1,0:T(1,128)} %bitcast.19, bf16[6912,512]{1,0:T(8,128)(2,1)} %orb.1), custom_call_target="tpu_custom_call" | custom-call | tf_op jit(solution)/shard_map/index/pallas_call | solution.py:390
  4.2 19.1 %all_to_all.20 = bf16[16,32,512]{2,1,0:T(8,128)(2,1)S(1)} all-to-all(bf16[16,32,512]{2,1,0:T(8,128)(2,1)S(1)} %broadcast_in_dim.31), channel_id=1, replica_groups=mesh['z'=4,'x_lo'=2,'core'=2,'x_hi'=2,'y'=4] {'z','y'}, dimensions={0} | all-to-all | bytes 1048576 | tf_op jit(solution)/shard_map/all_to_all | solution.py:415
  23.4 0.3 convolution_convert_fusion
  23.7 1.3 collective-permute-start.2
  25.0 1.4 collective-permute-start
  26.4 5.7 %collective-permute-done.2 = bf16[320,512]{1,0:T(8,128)(2,1)S(1)} collective-permute-done((bf16[320,512]{1,0:T(8,128)(2,1)S(1)}, bf16[320,512]{1,0:T(8,128)(2,1)S(1)}, u32[]{:S(2)}, u32[]{:S(2)}) %collective-permute-start.2) | collective-permute-done | bytes 327712 | tf_op jit(solution)/shard_map/ppermute | solution.py:271
  32.2 0.2 collective-permute-start.3
  32.3 2.7 %collective-permute-start.1 = (bf16[160,512]{1,0:T(8,128)(2,1)S(1)}, bf16[160,512]{1,0:T(8,128)(2,1)S(1)}, u32[]{:S(2)}, u32[]{:S(2)}) collective-permute-start(bf16[160,512]{1,0:T(8,128)(2,1)S(1)} %slice.18), channel_id=1, source_target_pairs={{16,0},{17,1},{18,2},{19,3},{20,4},{21,5},{22,6},{23,7},{24,8},{25... | collective-permute-start | bytes 491528 | tf_op jit(solution)/shard_map/ppermute | solution.py:271
  35.0 3.5 %collective-permute-start.4 = (bf16[320,512]{1,0:T(8,128)(2,1)S(1)}, bf16[320,512]{1,0:T(8,128)(2,1)S(1)}, u32[]{:S(2)}, u32[]{:S(2)}) collective-permute-start(bf16[320,512]{1,0:T(8,128)(2,1)S(1)} %convolution_convert_fusion), channel_id=1, source_target_pairs={{8,0},{9,1},{10,2},{11,3},{12,4},{13,5},{14,6},{15,7},{0,8},{1,9},... | collective-permute-start | bytes 983048 | tf_op jit(solution)/shard_map/ppermute | solution.py:271
  38.5 0.5 collective-permute-start.5
  39.7 0.3 copy.13
  40.0 1.7 collective-permute-start.7
  41.7 0.1 collective-permute-start.6
  41.8 0.3 pad_maximum_fusion.panel
  42.1 0.6 collective-permute-done.7
  42.8 0.5 collective-permute-done.6
  43.3 0.1 copy-done.13
  43.4 0.1 copy-done.8
  43.5 0.4 copy-done.9
  44.0 8.7 %conditional.1 = (bf16[512,2048]{1,0:T(8,128)(2,1)}) conditional(s32[]{:T(128)} %bitcast.4, (s32[]{:T(128)}, s32[2048]{0:T(1024)S(1)}, bf16[6912,512]{1,0:T(8,128)(2,1)}) %tuple.26, (s32[1,2048]{1,0:T(1,128)S(1)}, bf16[320,512]{1,0:T(8,128)(2,1)S(1)}, bf16[320,512]{1,0:T(8,128)(2,1)}, bf16[160,512]{1,0:T(8,128)(2,1)}, bf16[160,512]{1,0:T(8,128)(2,1)}, ...), branch_computations={%region_0.2_spmd, %region_2.3_spmd} | conditional | flops 4229121 | bytes 21012508 | solution.py:422
  44.0 8.7 %place.1 = bf16[512,2048]{1,0:T(8,128)(2,1)} custom-call(s32[1,2048]{1,0:T(1,128)S(1)} %get-tuple-element.39.slot, bf16[320,512]{1,0:T(8,128)(2,1)S(1)} %get-tuple-element.40.refs_0_, bf16[320,512]{1,0:T(8,128)(2,1)} %get-tuple-element.41.refs_1_, bf16[160,512]{1,0:T(8,128)(2,1)} %get-tuple-element.42.refs_2_, bf16[160,512]{1,0:T(8,128)(2,1)} %get-tuple-element.43.refs_3_, ...), custom_call_target="tpu_custom_call" | custom-call | tf_op jit(solution)/shard_map/cond/branch_1_fun/place/pallas_call | solution.py:295
  52.7 30.8 %pairs.1 = (bf16[6912,2048]{1,0:T(8,128)(2,1)}, bf16[32,4,32,128]{3,2,1,0:T(8,128)(2,1)}) custom-call(bf16[6912,512]{1,0:T(8,128)(2,1)} %orb.1, bf16[512,2048]{1,0:T(8,128)(2,1)} %get-tuple-element.62.rows_t, bf16[2048,128]{1,0:T(8,128)(2,1)S(1)} %pad_maximum_fusion.panel, bf16[1024,864]{1,0:T(8,128)(2,1)S(1)} %copy-done, bf16[512,512]{1,0:T(8,128)(2,1)S(1)} %copy-done.3), custom_call_target="tpu_custom_call" | custom-call | tf_op jit(solution)/shard_map/pairs/pallas_call | solution.py:106
  83.5 6.0 %all-to-all-start.1 = ((bf16[128,32,128]{2,1,0:T(8,128)(2,1)}), bf16[128,32,128]{2,1,0:T(8,128)(2,1)S(1)}, u32[]{:S(2)}, u32[]{:S(2)}) async-start(bf16[128,32,128]{2,1,0:T(8,128)(2,1)} %bitcast.6), calls=%async_computation.1 | async-start | bytes 2097152 | tf_op jit(solution)/shard_map/all_to_all | solution.py:437
  89.5 18.3 %all-to-all-done.1 = bf16[128,32,128]{2,1,0:T(8,128)(2,1)S(1)} async-done(((bf16[128,32,128]{2,1,0:T(8,128)(2,1)}), bf16[128,32,128]{2,1,0:T(8,128)(2,1)S(1)}, u32[]{:S(2)}, u32[]{:S(2)}) %all-to-all-start.1) | async-done | bytes 1048608 | tf_op jit(solution)/shard_map/all_to_all | solution.py:437
  107.8 9.9 %solve.1 = bf16[4096,128]{1,0:T(8,128)(2,1)S(1)} custom-call(s32[1]{0:T(128)} %bitcast.1.first, bf16[4096,128]{1,0:T(8,128)(2,1)S(1)} %bitcast.14, bf16[1536,1536]{1,0:T(8,128)(2,1)} %constant.90.clone.wide, bf16[1536,1536]{1,0:T(8,128)(2,1)} %constant.91.clone.wide_t, bf16[96,96]{1,0:T(8,128)(2,1)S(1)} %copy-done.5, bf16[96,96]{1,0:T(8,128)(2,1)S(1)} %copy-done.4), custom_call_target="tpu_custom_call" | custom-call | tf_op jit(solution)/shard_map/solve/pallas_call | solution.py:172
  117.7 0.0 copy-start.1
  117.8 23.2 %all_to_all.21 = bf16[128,32,128]{2,1,0:T(8,128)(2,1)S(1)} all-to-all(bf16[128,32,128]{2,1,0:T(8,128)(2,1)S(1)} %bitcast.15), channel_id=1, replica_groups=mesh['z'=4,'x_lo'=2,'core'=2,'x_hi'=2,'y'=4] {'z','x_lo','core','x_hi','y'}, dimensions={0} | all-to-all | bytes 2097152 | tf_op jit(solution)/shard_map/all_to_all | solution.py:440
  140.9 14.6 %project.1 = f32[128,8,128]{2,1,0:T(8,128)S(1)} custom-call(bf16[32,4,32,128]{3,2,1,0:T(8,128)(2,1)S(1)} %bitcast.16, bf16[512,512]{1,0:T(8,128)(2,1)S(1)} %copy-done.2, bf16[864,1024]{1,0:T(8,128)(2,1)S(1)} %copy-done.1, bf16[6912,2048]{1,0:T(8,128)(2,1)} %get-tuple-element.61.pair), custom_call_target="tpu_custom_call" | custom-call | tf_op jit(solution)/shard_map/project/pallas_call | solution.py:231
  155.5 18.5 %all_to_all.22 = f32[128,8,128]{2,1,0:T(8,128)S(1)} all-to-all(f32[128,8,128]{2,1,0:T(8,128)S(1)} %project.1), channel_id=1, replica_groups=mesh['z'=4,'x_lo'=2,'core'=2,'x_hi'=2,'y'=4] {'z','x_lo','core','x_hi','y'}, dimensions={0} | all-to-all | bytes 1048576 | tf_op jit(solution)/shard_map/all_to_all | solution.py:442
  174.1 0.1 reduce_sum.9
  174.2 0.1 fusion.1
  174.3 0.6 pad_maximum_fusion.1
  (36 shorter events, 0.1 us)
Async XLA Ops:
  4.2 35.6 %copy-start.10 = (bf16[2048,64]{0,1:T(8,128)(2,1)S(1)}, bf16[2048,64]{0,1:T(8,128)(2,1)}, u32[]{:S(2)}) copy-start(bf16[2048,64]{0,1:T(8,128)(2,1)} %param.14) | copy-start | bytes 786436
  23.4 20.6 %copy-start.14 = (s32[2048]{0:T(1024)S(1)}, s32[2048]{0:T(1024)}, u32[]{:S(2)}) copy-start(s32[2048]{0:T(1024)} %param.15) | copy-start | bytes 24580
  23.7 8.5 %collective-permute-start.2 = (bf16[320,512]{1,0:T(8,128)(2,1)S(1)}, bf16[320,512]{1,0:T(8,128)(2,1)S(1)}, u32[]{:S(2)}, u32[]{:S(2)}) collective-permute-start(bf16[320,512]{1,0:T(8,128)(2,1)S(1)} %convolution_convert_fusion), channel_id=1, source_target_pairs={{20,0},{21,1},{22,2},{23,3},{16,4},{17,5},{18,6},{19,7},{28,8},{29... | collective-permute-start | bytes 983048 | tf_op jit(solution)/shard_map/ppermute | solution.py:271
  25.0 7.3 %collective-permute-start = (bf16[320,512]{1,0:T(8,128)(2,1)S(1)}, bf16[320,512]{1,0:T(8,128)(2,1)S(1)}, u32[]{:S(2)}, u32[]{:S(2)}) collective-permute-start(bf16[320,512]{1,0:T(8,128)(2,1)S(1)} %convolution_convert_fusion), channel_id=1, source_target_pairs={{16,0},{17,1},{18,2},{19,3},{20,4},{21,5},{22,6},{23,7},{24,8},{25... | collective-permute-start | bytes 983048 | tf_op jit(solution)/shard_map/ppermute | solution.py:271
  32.2 7.8 %collective-permute-start.3 = (bf16[160,512]{1,0:T(8,128)(2,1)S(1)}, bf16[160,512]{1,0:T(8,128)(2,1)S(1)}, u32[]{:S(2)}, u32[]{:S(2)}) collective-permute-start(bf16[160,512]{1,0:T(8,128)(2,1)S(1)} %slice.19), channel_id=1, source_target_pairs={{20,0},{21,1},{22,2},{23,3},{16,4},{17,5},{18,6},{19,7},{28,8},{29... | collective-permute-start | bytes 491528 | tf_op jit(solution)/shard_map/ppermute | solution.py:271
  32.3 10.9 %copy-start.6 = (bf16[320,512]{1,0:T(8,128)(2,1)}, bf16[320,512]{1,0:T(8,128)(2,1)S(1)}, u32[]{:S(2)}) copy-start(bf16[320,512]{1,0:T(8,128)(2,1)S(1)} %collective-permute-done) | copy-start | bytes 983044
  32.3 9.4 %collective-permute-start.1 = (bf16[160,512]{1,0:T(8,128)(2,1)S(1)}, bf16[160,512]{1,0:T(8,128)(2,1)S(1)}, u32[]{:S(2)}, u32[]{:S(2)}) collective-permute-start(bf16[160,512]{1,0:T(8,128)(2,1)S(1)} %slice.18), channel_id=1, source_target_pairs={{16,0},{17,1},{18,2},{19,3},{20,4},{21,5},{22,6},{23,7},{24,8},{25... | collective-permute-start | bytes 491528 | tf_op jit(solution)/shard_map/ppermute | solution.py:271
  35.0 7.1 %collective-permute-start.4 = (bf16[320,512]{1,0:T(8,128)(2,1)S(1)}, bf16[320,512]{1,0:T(8,128)(2,1)S(1)}, u32[]{:S(2)}, u32[]{:S(2)}) collective-permute-start(bf16[320,512]{1,0:T(8,128)(2,1)S(1)} %convolution_convert_fusion), channel_id=1, source_target_pairs={{8,0},{9,1},{10,2},{11,3},{12,4},{13,5},{14,6},{15,7},{0,8},{1,9},... | collective-permute-start | bytes 983048 | tf_op jit(solution)/shard_map/ppermute | solution.py:271
  38.5 4.2 %collective-permute-start.8 = (bf16[320,512]{1,0:T(8,128)(2,1)S(1)}, bf16[320,512]{1,0:T(8,128)(2,1)S(1)}, u32[]{:S(2)}, u32[]{:S(2)}) collective-permute-start(bf16[320,512]{1,0:T(8,128)(2,1)S(1)} %collective-permute-done.2), channel_id=1, source_target_pairs={{8,0},{9,1},{10,2},{11,3},{12,4},{13,5},{14,6},{15,7},{0,8},{1,9},... | collective-permute-start | bytes 983048 | tf_op jit(solution)/shard_map/ppermute | solution.py:271
  38.5 4.7 %collective-permute-start.5 = (bf16[320,512]{1,0:T(8,128)(2,1)S(1)}, bf16[320,512]{1,0:T(8,128)(2,1)S(1)}, u32[]{:S(2)}, u32[]{:S(2)}) collective-permute-start(bf16[320,512]{1,0:T(8,128)(2,1)S(1)} %collective-permute-done), channel_id=1, source_target_pairs={{8,0},{9,1},{10,2},{11,3},{12,4},{13,5},{14,6},{15,7},{0,8},{1,9},... | collective-permute-start | bytes 983048 | tf_op jit(solution)/shard_map/ppermute | solution.py:271
  40.0 3.3 %copy-start.11 = (bf16[160,512]{1,0:T(8,128)(2,1)}, bf16[160,512]{1,0:T(8,128)(2,1)S(1)}, u32[]{:S(2)}) copy-start(bf16[160,512]{1,0:T(8,128)(2,1)S(1)} %collective-permute-done.3) | copy-start | bytes 491524
  40.0 2.7 %collective-permute-start.7 = (bf16[160,512]{1,0:T(8,128)(2,1)S(1)}, bf16[160,512]{1,0:T(8,128)(2,1)S(1)}, u32[]{:S(2)}, u32[]{:S(2)}) collective-permute-start(bf16[160,512]{1,0:T(8,128)(2,1)S(1)} %collective-permute-done.3), channel_id=1, source_target_pairs={{8,0},{9,1},{10,2},{11,3},{12,4},{13,5},{14,6},{15,7},{0,8},{1,9},... | collective-permute-start | bytes 491528 | tf_op jit(solution)/shard_map/ppermute | solution.py:271
  41.7 1.6 copy-start.12
  41.7 1.5 collective-permute-start.6
  42.1 1.2 copy-start.7
  42.8 0.7 copy-start.13
  42.8 0.8 copy-start.8
  43.3 0.7 copy-start.9
  44.0 8.7 %copy-start = (bf16[1024,864]{1,0:T(8,128)(2,1)S(1)}, bf16[1024,864]{1,0:T(8,128)(2,1)}, u32[]{:S(2)}) copy-start(bf16[1024,864]{1,0:T(8,128)(2,1)} %constant.88.clone.ahead) | copy-start | bytes 5308420
  44.0 8.7 %copy-start.3 = (bf16[512,512]{1,0:T(8,128)(2,1)S(1)}, bf16[512,512]{1,0:T(8,128)(2,1)}, u32[]{:S(2)}) copy-start(bf16[512,512]{1,0:T(8,128)(2,1)} %constant.89.clone.swap) | copy-start | bytes 1572868
  83.5 24.3 %copy-start.4 = (bf16[96,96]{1,0:T(8,128)(2,1)S(1)}, bf16[96,96]{1,0:T(8,128)(2,1)}, u32[]{:S(2)}) copy-start(bf16[96,96]{1,0:T(8,128)(2,1)} %constant.93.clone.x_back) | copy-start | bytes 55300
  83.5 24.3 %copy-start.5 = (bf16[96,96]{1,0:T(8,128)(2,1)S(1)}, bf16[96,96]{1,0:T(8,128)(2,1)}, u32[]{:S(2)}) copy-start(bf16[96,96]{1,0:T(8,128)(2,1)} %constant.92.clone.x_ahead) | copy-start | bytes 55300
  83.5 24.3 %all-to-all-start.1 = ((bf16[128,32,128]{2,1,0:T(8,128)(2,1)}), bf16[128,32,128]{2,1,0:T(8,128)(2,1)S(1)}, u32[]{:S(2)}, u32[]{:S(2)}) async-start(bf16[128,32,128]{2,1,0:T(8,128)(2,1)} %bitcast.6), calls=%async_computation.1 | async-start | bytes 2097152 | tf_op jit(solution)/shard_map/all_to_all | solution.py:437
  107.8 33.1 %copy-start.2 = (bf16[512,512]{1,0:T(8,128)(2,1)S(1)}, bf16[512,512]{1,0:T(8,128)(2,1)}, u32[]{:S(2)}) copy-start(bf16[512,512]{1,0:T(8,128)(2,1)} %constant.94.clone.unswap) | copy-start | bytes 1572868
  117.7 23.2 %copy-start.1 = (bf16[864,1024]{1,0:T(8,128)(2,1)S(1)}, bf16[864,1024]{1,0:T(8,128)(2,1)}, u32[]{:S(2)}) copy-start(bf16[864,1024]{1,0:T(8,128)(2,1)} %constant.95.clone.back) | copy-start | bytes 5308420

commit v5 on v4

--- a/solution.py
+++ b/solution.py
@@ -22,7 +22,7 @@
 CG, CI = 4, 16
 ROWS = 32
 CELLS = 8 * NG
-WIDE = 12 * NG
+WIDE = 9 * NG
 
 
 def basis_table():
@@ -54,7 +54,6 @@
         "swap": swap,
         "unswap": swap.T,
         "wide": wide,
-        "wide_t": wide.T,
         "x_ahead": x_basis.T,
         "x_back": x_basis,
     }
@@ -122,7 +121,7 @@
             jax.ShapeDtypeStruct((MG, CG, ROWS, 128), BF),
         ],
         scratch_shapes=[pltpu.VMEM((OCT * NG, 512), BF)],
-        compiler_params=pltpu.CompilerParams(vmem_limit_bytes=48 * 2**20),
+        compiler_params=pltpu.CompilerParams(vmem_limit_bytes=28 * 2**20),
         name="pairs",
     )(orbitals, rows_t, panel2, const(tab["ahead"]), const(tab["swap"]))
 
@@ -135,7 +134,9 @@
                 yield part * ROWS + octet * MI + mi, mi, spot // 12, spot % 12
 
 
-def solve_kernel(first, got, wide, wide_t, x_ahead, x_back, out, flat, field):
+def solve_kernel(first, got, table, x_ahead, x_back, out, flat, field, wide, sem):
+    fetch = pltpu.make_async_copy(table, wide, sem)
+    fetch.start()
     flat[...] = got[...].astype(F32)
     for row, mi, xr, yo in places():
         field[mi, xr * 32 : (xr + 1) * 32, yo * 128 : (yo + 1) * 128] = flat[
@@ -149,6 +150,7 @@
     square = lambda w: w.astype(F32) * w.astype(F32)
     factor = NG / (2.0 * math.pi) * (NG / (2.0 * math.pi))
     flat[...] = jnp.zeros_like(flat)
+    fetch.wait()
     spec_y = mm(field[...].reshape(MI * NG, NG * CI), wide[...]).astype(BF)
     backs = []
     for mi in range(MI):
@@ -159,7 +161,12 @@
         kernel = jnp.where(total > 0.5, factor / (total + SCREEN), 0.0) * gain
         scaled = (spec * kernel).astype(BF)
         backs.append(mm(x_back[...], scaled).astype(BF))
-    plane = mm(jnp.concatenate(backs, axis=0), wide_t[...])
+    plane = lax.dot_general(
+        jnp.concatenate(backs, axis=0),
+        wide[...],
+        (((1,), (1,)), ((), ())),
+        preferred_element_type=F32,
+    )
     for row, mi, xr, yo in places():
         flat[pl.ds(row, 32, stride=4 * ROWS), :] = plane[
             mi * NG + xr * 32 : mi * NG + (xr + 1) * 32, yo * 128 : (yo + 1) * 128
@@ -171,12 +178,15 @@
     vmem = pl.BlockSpec(memory_space=pltpu.VMEM)
     return pl.pallas_call(
         solve_kernel,
-        in_specs=[pl.BlockSpec(memory_space=pltpu.SMEM)] + [vmem] * 5,
+        in_specs=[pl.BlockSpec(memory_space=pltpu.SMEM), vmem, pl.BlockSpec(memory_space=pl.ANY)]
+        + [vmem] * 2,
         out_specs=vmem,
         out_shape=jax.ShapeDtypeStruct(got.shape, BF),
         scratch_shapes=[
             pltpu.VMEM(got.shape, F32),
             pltpu.VMEM((MI, NG, NG * CI), BF),
+            pltpu.VMEM(tab["wide"].shape, BF),
+            pltpu.SemaphoreType.DMA,
         ],
         compiler_params=pltpu.CompilerParams(vmem_limit_bytes=48 * 2**20),
         name="solve",
@@ -184,67 +194,62 @@
         first,
         got,
         const(tab["wide"]),
-        const(tab["wide_t"]),
         const(tab["x_ahead"]),
         const(tab["x_back"]),
     )
 
 
-def project_kernel(got, unswap, back, pair, out, spec, pot, acc):
-    step = pl.program_id(0)
-
-    @pl.when(step == 0)
-    def _():
-        for part in range(4):
-            rows = MG * ROWS // 4
-            block = jnp.concatenate(
-                [
-                    got[part * MG // 4 : (part + 1) * MG // 4, cg].reshape(rows, 128)
-                    for cg in range(CG)
-                ],
-                axis=1,
-            )
-            spec[part * rows : (part + 1) * rows, :] = mm(block, unswap[...]).astype(BF)
-        for octet in range(OCT):
-            final = mm(back[octet * NG : (octet + 1) * NG, :], spec[...])
-            final = final / float(NG**3)
-            for yi in range(8):
-                start = (octet * 8 + yi) * NG
-                pot[start : start + NG, :] = final[:, yi * 64 : (yi + 1) * 64].astype(BF)
-        acc[...] = jnp.zeros_like(acc)
-
-    block = pot[pl.ds(pl.multiple_of(step * WIDE, WIDE), WIDE), :]
-    acc[...] += lax.dot_general(
-        block, pair[...], (((0,), (0,)), ((), ())), preferred_element_type=F32
-    )
-
-    @pl.when(step == pl.num_programs(0) - 1)
-    def _():
-        scale = 1.0 / math.sqrt(float(NG**3))
-        turned = (acc[...] * scale).T.reshape(128, 2, 8, 64)
-        out[...] = jnp.concatenate([turned[:, 0], turned[:, 1]], axis=-1)
+def project_kernel(got, unswap, back, pair, out, spec, pot, acc, near, sems):
+    steps = pair.shape[0] // WIDE
+    blocks = [pl.ds(step * WIDE, WIDE) for step in range(steps)]
+    copies = [
+        pltpu.make_async_copy(pair.at[rows, :], near.at[rows, :], sems.at[step])
+        for step, rows in enumerate(blocks)
+    ]
+    for copy in copies:
+        copy.start()
+    for part in range(4):
+        rows = MG * ROWS // 4
+        block = jnp.concatenate(
+            [
+                got[part * MG // 4 : (part + 1) * MG // 4, cg].reshape(rows, 128)
+                for cg in range(CG)
+            ],
+            axis=1,
+        )
+        spec[part * rows : (part + 1) * rows, :] = mm(block, unswap[...]).astype(BF)
+    for octet in range(OCT):
+        final = mm(back[octet * NG : (octet + 1) * NG, :], spec[...])
+        final = final / float(NG**3)
+        for yi in range(8):
+            start = (octet * 8 + yi) * NG
+            pot[start : start + NG, :] = final[:, yi * 64 : (yi + 1) * 64].astype(BF)
+    acc[...] = jnp.zeros_like(acc)
+    for copy, rows in zip(copies, blocks):
+        copy.wait()
+        acc[...] += lax.dot_general(
+            pot[rows, :], near[rows, :], (((0,), (0,)), ((), ())), preferred_element_type=F32
+        )
+    scale = 1.0 / math.sqrt(float(NG**3))
+    turned = (acc[...] * scale).T.reshape(128, 2, 8, 64)
+    out[...] = jnp.concatenate([turned[:, 0], turned[:, 1]], axis=-1)
 
 
 def project(got, pair, tab):
-    steps = pair.shape[0] // WIDE
-    whole = lambda shape: pl.BlockSpec(shape, lambda i: (0,) * len(shape))
+    vmem = pl.BlockSpec(memory_space=pltpu.VMEM)
     return pl.pallas_call(
         project_kernel,
-        grid=(steps,),
-        in_specs=[
-            whole(got.shape),
-            whole(tab["unswap"].shape),
-            whole(tab["back"].shape),
-            pl.BlockSpec((WIDE, pair.shape[1]), lambda i: (i, 0)),
-        ],
-        out_specs=whole((128, 8, 128)),
+        in_specs=[vmem] * 3 + [pl.BlockSpec(memory_space=pl.ANY)],
+        out_specs=vmem,
         out_shape=jax.ShapeDtypeStruct((128, 8, 128), F32),
         scratch_shapes=[
             pltpu.VMEM((MG * ROWS, 512), BF),
             pltpu.VMEM((pair.shape[0], 64), BF),
             pltpu.VMEM((64, pair.shape[1]), F32),
-        ],
-        compiler_params=pltpu.CompilerParams(vmem_limit_bytes=48 * 2**20),
+            pltpu.VMEM(pair.shape, BF),
+            pltpu.SemaphoreType.DMA((pair.shape[0] // WIDE,)),
+        ],
+        compiler_params=pltpu.CompilerParams(vmem_limit_bytes=44 * 2**20),
         name="project",
     )(got, const(tab["unswap"]), const(tab["back"]), pair)
 
@@ -271,36 +276,47 @@
     return lax.ppermute(data, AXES, pairs)
 
 
-def place_kernel(count, slot, *refs):
-    blocks, out, turned = refs[:count], refs[count], refs[count + 1]
+def place_kernel(count, base, *refs):
+    blocks, (slot, *more), (out, held) = refs[:count], refs[count:-2], refs[-2:]
     start = 0
     for block in blocks:
         rows = block.shape[0]
-        turned[start : start + rows, :] = block[...]
+        held[start : start + rows, :] = block[...]
         start += rows
-    slots = turned.shape[0]
     chunk = 256
     for first in range(0, slot.shape[1], chunk):
-        index = lax.broadcasted_iota(jnp.int32, (slots, chunk), 0)
-        pick = jnp.where(index == slot[:, first : first + chunk], 1.0, 0.0).astype(BF)
-        out[:, first : first + chunk] = lax.dot_general(
-            turned[...], pick, (((0,), (0,)), ((), ())), preferred_element_type=F32
-        ).astype(BF)
-
-
-def place(slot, blocks):
+        wanted = slot[:, first : first + chunk]
+        picks = []
+        for block, number in zip(blocks, base):
+            index = lax.broadcasted_iota(jnp.int32, (block.shape[0], chunk), 0) + number
+            picks.append(jnp.where(index == wanted, 1.0, 0.0).astype(BF))
+        total = lax.dot_general(
+            held[...],
+            jnp.concatenate(picks, axis=0),
+            (((0,), (0,)), ((), ())),
+            preferred_element_type=F32,
+        )
+        if more:
+            total = total + more[0][:, first : first + chunk].astype(F32)
+        out[:, first : first + chunk] = total.astype(BF)
+
+
+def place(slot, blocks, base, more=()):
     vmem = pl.BlockSpec(memory_space=pltpu.VMEM)
-    norb = blocks[0].shape[1]
+    norb, npts = blocks[0].shape[1], slot.shape[1]
     slots = sum(block.shape[0] for block in blocks)
     return pl.pallas_call(
-        functools.partial(place_kernel, len(blocks)),
-        in_specs=[vmem] * (1 + len(blocks)),
+        functools.partial(place_kernel, len(blocks), base),
+        in_specs=[vmem] * (1 + len(blocks) + len(more)),
         out_specs=vmem,
-        out_shape=jax.ShapeDtypeStruct((norb, slot.shape[1]), BF),
+        out_shape=jax.ShapeDtypeStruct((norb, npts), BF),
         scratch_shapes=[pltpu.VMEM((slots, norb), BF)],
-        compiler_params=pltpu.CompilerParams(vmem_limit_bytes=32 * 2**20),
+        compiler_params=pltpu.CompilerParams(vmem_limit_bytes=20 * 2**20),
+        cost_estimate=pl.CostEstimate(
+            flops=2 * slots * norb * npts, bytes_accessed=4 * norb * npts, transcendentals=0
+        ),
         name="place",
-    )(slot, *blocks)
+    )(*blocks, slot, *more)
 
 
 def summed_rows(orbitals, points, me):
@@ -409,19 +425,28 @@
     )(me.reshape(1), points[None], orbitals)
 
 
-def gather_rows(orbitals, points, me):
-    fits, own, choose, slot = index(me, points, orbitals)
+def spread_rows(own, choose, slot):
     copies = jnp.broadcast_to(own[None], (16,) + own.shape)
     square = lax.all_to_all(copies, ("z", "y"), 0, 0).reshape(16 * ROOM, own.shape[1])
     held = mm(choose, square).astype(BF)
+    mate = lambda block: bring(block, dcore=1)
+    half, ring = GROUP // 2, 4 * GROUP
     right, left = bring(held, dx=1), bring(held, dx=3)
-    half = GROUP // 2
+    rows = place(slot, [held, mate(held)], (0, ring))
     far_a, far_b = bring(right[:half], dx=1), bring(left[half:], dx=3)
-    blocks = [held, right, far_a, far_b, left]
-    blocks = blocks + [bring(block, dcore=1) for block in blocks]
+    near = [right, left, mate(right), mate(left)]
+    rows = place(slot, near, (GROUP, 3 * GROUP, ring + GROUP, ring + 3 * GROUP), (rows,))
+    far_a, far_b, rows = lax.optimization_barrier((far_a, far_b, rows))
+    far = [far_a, far_b, mate(far_a), mate(far_b)]
+    start = 2 * GROUP
+    return place(slot, far, (start, start + half, ring + start, ring + start + half), (rows,))
+
+
+def gather_rows(orbitals, points, me):
+    fits, own, choose, slot = index(me, points, orbitals)
     return lax.cond(
         fits[0] > 0,
-        lambda: place(slot, blocks),
+        lambda: spread_rows(own, choose, slot),
         lambda: summed_rows(orbitals, points, me),
     )
 

time: 175 us -> 167 us (0.954)
  Pallas kernels: 68.2 us -> 62.9 us
  waiting for transfers between devices: 25.1 us -> 22.9 us
    pallas_call x2 -> x4, Pallas kernels: 23.4 us -> 20.5 us  [the longest x1 12.4 us: project(): pl.pallas_call(project_kernel, in_specs=[vmem] * 3 + [pl.BlockSpec(memory...]
    pallas_call x1, Pallas kernels: 9.9 us -> 7.4 us  [solve(): pl.pallas_call(solve_kernel, in_specs=[pl.BlockSpec(memory_space=pltpu.SM...]
    ppermute x9, waiting for transfers between devices: 6.84 us -> 4.57 us  [bring(): return lax.ppermute(data, AXES, pairs)]
  transfers between devices with their start and end apart: 10 -> 10, of which waited for: 4 -> 4; matrix products, arithmetic and copies ran while one was open for 0% -> 0% of each run, Pallas kernels for 0% -> 3%
where the time goes in v5:
time: 167 us
  Pallas kernels  62.9 us (38%)
  blocking collectives  60.7 us (36%)
  waiting for transfers between devices  22.9 us (14%)
  starting transfers between devices  17.4 us (10%)
    pallas_call x1, Pallas kernels, make_pairs(): pl.pallas_call(pair_kernel, grid=(steps,), in_specs=[pl.BlockSpec((CELLS,...  30.8 us
    all_to_all x1, blocking collectives, shards(): got = lax.all_to_all(ret.reshape(devices, ROWS, 128), AXES, 0, 0)  23.2 us
    all_to_all x1, blocking collectives, spread_rows(): lax.all_to_all(copies, ('z', 'y'), 0, 0).reshape(16 * ROOM, own.shape[1])  19 us
    all_to_all x1, blocking collectives, shards(): parts = lax.all_to_all(parts, AXES, 0, 0)  18.5 us
    all_to_all x1, waiting for transfers between devices, shards(): planes = lax.all_to_all(send.reshape(devices, ROWS, 128), AXES, 0, 0)  18.3 us
    ppermute x9, starting transfers between devices, bring(): return lax.ppermute(data, AXES, pairs)  12.4 us
    pallas_call x1, Pallas kernels, project(): pl.pallas_call(project_kernel, in_specs=[vmem] * 3 + [pl.BlockSpec(memory...  12.4 us
    pallas_call x3, Pallas kernels, place(): pl.pallas_call(functools.partial(place_kernel, len(blocks), base), in_spe...  8.09 us
  transfers between devices with their start and end apart: 10, of which 4 were waited for; matrix products, arithmetic and copies ran while one was open for 0% of the time, Pallas kernels for 3%

profile of v5, /device:TPU:1, one launch (start us, length us, event | category | flops | bytes accessed | tf_op | source)
XLA Modules:
  0.0 166.5 jit_solution(10272905217654342636)
XLA Ops:
  0.0 4.3 %index.1 = (s32[1]{0:T(128)}, bf16[32,512]{1,0:T(8,128)(2,1)S(1)}, bf16[320,512]{1,0:T(8,128)(2,1)S(1)}, s32[1,2048]{1,0:T(1,128)S(1)}) custom-call(s32[1]{0:T(128)} %bitcast.3.me, s32[1,2048]{1,0:T(1,128)} %bitcast.19, bf16[6912,512]{1,0:T(8,128)(2,1)} %orb.1), custom_call_target="tpu_custom_call" | custom-call | tf_op jit(solution)/shard_map/index/pallas_call | solution.py:406
  4.9 0.3 copy.12
  5.2 0.3 pad_maximum_fusion.panel
  5.5 0.0 copy-start.3
  5.5 44.6 %conditional.1 = (bf16[512,2048]{1,0:T(8,128)(2,1)}) conditional(s32[]{:T(128)} %bitcast.5, (s32[]{:T(128)}, s32[2048]{0:T(1024)S(1)}, bf16[6912,512]{1,0:T(8,128)(2,1)}) %tuple.20, (bf16[32,512]{1,0:T(8,128)(2,1)S(1)}, bf16[320,512]{1,0:T(8,128)(2,1)S(1)}, s32[1,2048]{1,0:T(1,128)S(1)}) %tuple.13), branch_computations={%region_0.2_spmd, %region_2.3_spmd} | conditional | flops 5536645120 | bytes 25198960 | solution.py:447
  5.6 19.0 %all_to_all.19 = bf16[16,32,512]{2,1,0:T(8,128)(2,1)S(1)} all-to-all(bf16[16,32,512]{2,1,0:T(8,128)(2,1)S(1)} %broadcast_in_dim.28), channel_id=1, replica_groups=mesh['z'=4,'x_lo'=2,'core'=2,'x_hi'=2,'y'=4] {'z','y'}, dimensions={0} | all-to-all | bytes 1048576 | tf_op jit(solution)/shard_map/cond/branch_1_fun/all_to_all | solution.py:430
  24.6 0.3 convolution_convert_fusion.refs_0_
  25.0 1.3 collective-permute-start.2
  26.2 1.5 collective-permute-start
  27.7 2.5 %collective-permute-start.6 = (bf16[320,512]{1,0:T(8,128)(2,1)S(1)}, bf16[320,512]{1,0:T(8,128)(2,1)S(1)}, u32[]{:S(2)}, u32[]{:S(2)}) collective-permute-start(bf16[320,512]{1,0:T(8,128)(2,1)S(1)} %convolution_convert_fusion.refs_0_), channel_id=1, source_target_pairs={{8,0},{9,1},{10,2},{11,3},{12,4},{13,5},{14,6},{15,7},{0,8},{1,9},... | collective-permute-start | bytes 983048 | tf_op jit(solution)/shard_map/cond/branch_1_fun/ppermute | solution.py:276
  30.2 3.2 %collective-permute-done.2.refs_1_ = bf16[320,512]{1,0:T(8,128)(2,1)S(1)} collective-permute-done((bf16[320,512]{1,0:T(8,128)(2,1)S(1)}, bf16[320,512]{1,0:T(8,128)(2,1)S(1)}, u32[]{:S(2)}, u32[]{:S(2)}) %collective-permute-start.2) | collective-permute-done | bytes 327712 | tf_op jit(solution)/shard_map/cond/branch_1_fun/ppermute | solution.py:276
  33.5 2.9 %collective-permute-start.5 = (bf16[320,512]{1,0:T(8,128)(2,1)S(1)}, bf16[320,512]{1,0:T(8,128)(2,1)S(1)}, u32[]{:S(2)}, u32[]{:S(2)}) collective-permute-start(bf16[320,512]{1,0:T(8,128)(2,1)S(1)} %collective-permute-done.2.refs_1_), channel_id=1, source_target_pairs={{8,0},{9,1},{10,2},{11,3},{12,4},{13,5},{14,6},{15,7},{0,8},{1,9},... | collective-permute-start | bytes 983048 | tf_op jit(solution)/shard_map/cond/branch_1_fun/ppermute | solution.py:276
  36.4 1.2 collective-permute-start.3
  37.6 1.8 %collective-permute-start.1 = (bf16[160,512]{1,0:T(8,128)(2,1)S(1)}, bf16[160,512]{1,0:T(8,128)(2,1)S(1)}, u32[]{:S(2)}, u32[]{:S(2)}) collective-permute-start(bf16[160,512]{1,0:T(8,128)(2,1)S(1)} %slice.16), channel_id=1, source_target_pairs={{16,0},{17,1},{18,2},{19,3},{20,4},{21,5},{22,6},{23,7},{24,8},{25... | collective-permute-start | bytes 491528 | tf_op jit(solution)/shard_map/cond/branch_1_fun/ppermute | solution.py:276
  39.4 1.8 %place.3.refs_5_ = bf16[512,2048]{1,0:T(8,128)(2,1)S(1)} custom-call(bf16[320,512]{1,0:T(8,128)(2,1)S(1)} %convolution_convert_fusion.refs_0_, bf16[320,512]{1,0:T(8,128)(2,1)S(1)} %collective-permute-done.6.refs_1_, s32[1,2048]{1,0:T(1,128)S(1)} %get-tuple-element.25.refs_2_.refs_4_), custom_call_target="tpu_custom_call" | custom-call | flops 1342177280 | bytes 4194304 | tf_op jit(solution)/shard_map/cond/branch_1_fun/place/pallas_call | solution.py:308
  41.3 2.9 %place.4.refs_5_ = bf16[512,2048]{1,0:T(8,128)(2,1)S(1)} custom-call(bf16[320,512]{1,0:T(8,128)(2,1)S(1)} %collective-permute-done.refs_0_, bf16[320,512]{1,0:T(8,128)(2,1)S(1)} %collective-permute-done.2.refs_1_, bf16[320,512]{1,0:T(8,128)(2,1)S(1)} %collective-permute-done.4.refs_2_, bf16[320,512]{1,0:T(8,128)(2,1)S(1)} %collective-permute-done.5.refs_3_, ...), custom_call_target="tpu_custom_call" | custom-call | flops 2684354560 | bytes 4194304 | tf_op jit(solution)/shard_map/cond/branch_1_fun/place/pallas_call | solution.py:308
  44.3 1.1 collective-permute-start.7
  45.4 0.1 collective-permute-start.8
  45.5 0.9 collective-permute-done.7.refs_2_
  46.4 0.4 collective-permute-done.8.refs_3_
  46.8 3.3 %place.5 = bf16[512,2048]{1,0:T(8,128)(2,1)} custom-call(bf16[160,512]{1,0:T(8,128)(2,1)S(1)} %collective-permute-done.1.refs_0_, bf16[160,512]{1,0:T(8,128)(2,1)S(1)} %collective-permute-done.3.refs_1_, bf16[160,512]{1,0:T(8,128)(2,1)S(1)} %collective-permute-done.7.refs_2_, bf16[160,512]{1,0:T(8,128)(2,1)S(1)} %collective-permute-done.8.refs_3_, ...), custom_call_target="tpu_custom_call" | custom-call | flops 1342177280 | bytes 4194304 | tf_op jit(solution)/shard_map/cond/branch_1_fun/place/pallas_call | solution.py:308
  50.1 30.8 %pairs.1 = (bf16[6912,2048]{1,0:T(8,128)(2,1)}, bf16[32,4,32,128]{3,2,1,0:T(8,128)(2,1)}) custom-call(bf16[6912,512]{1,0:T(8,128)(2,1)} %orb.1, bf16[512,2048]{1,0:T(8,128)(2,1)} %get-tuple-element.41.rows_t, bf16[2048,128]{1,0:T(8,128)(2,1)S(1)} %pad_maximum_fusion.panel, bf16[1024,864]{1,0:T(8,128)(2,1)S(1)} %copy-done, bf16[512,512]{1,0:T(8,128)(2,1)S(1)} %copy-done.3), custom_call_target="tpu_custom_call" | custom-call | tf_op jit(solution)/shard_map/pairs/pallas_call | solution.py:105
  80.9 5.0 %all-to-all-start.1 = ((bf16[128,32,128]{2,1,0:T(8,128)(2,1)}), bf16[128,32,128]{2,1,0:T(8,128)(2,1)S(1)}, u32[]{:S(2)}, u32[]{:S(2)}) async-start(bf16[128,32,128]{2,1,0:T(8,128)(2,1)} %bitcast.6), calls=%async_computation.1 | async-start | bytes 2097152 | tf_op jit(solution)/shard_map/all_to_all | solution.py:462
  85.9 18.3 %all-to-all-done.1 = bf16[128,32,128]{2,1,0:T(8,128)(2,1)S(1)} async-done(((bf16[128,32,128]{2,1,0:T(8,128)(2,1)}), bf16[128,32,128]{2,1,0:T(8,128)(2,1)S(1)}, u32[]{:S(2)}, u32[]{:S(2)}) %all-to-all-start.1) | async-done | bytes 1048608 | tf_op jit(solution)/shard_map/all_to_all | solution.py:462
  104.2 7.4 %solve.1 = bf16[4096,128]{1,0:T(8,128)(2,1)S(1)} custom-call(s32[1]{0:T(128)} %bitcast.2.first, bf16[4096,128]{1,0:T(8,128)(2,1)S(1)} %bitcast.15, bf16[1536,1536]{1,0:T(8,128)(2,1)} %constant.88.clone.table, bf16[96,96]{1,0:T(8,128)(2,1)S(1)} %copy-done.5, bf16[96,96]{1,0:T(8,128)(2,1)S(1)} %copy-done.4), custom_call_target="tpu_custom_call" | custom-call | tf_op jit(solution)/shard_map/solve/pallas_call | solution.py:179
  111.7 0.0 copy-start.1
  111.7 23.2 %all_to_all.20 = bf16[128,32,128]{2,1,0:T(8,128)(2,1)S(1)} all-to-all(bf16[128,32,128]{2,1,0:T(8,128)(2,1)S(1)} %bitcast.16), channel_id=1, replica_groups=mesh['z'=4,'x_lo'=2,'core'=2,'x_hi'=2,'y'=4] {'z','x_lo','core','x_hi','y'}, dimensions={0} | all-to-all | bytes 2097152 | tf_op jit(solution)/shard_map/all_to_all | solution.py:465
  134.8 12.4 %project.1 = f32[128,8,128]{2,1,0:T(8,128)S(1)} custom-call(bf16[32,4,32,128]{3,2,1,0:T(8,128)(2,1)S(1)} %bitcast.14, bf16[512,512]{1,0:T(8,128)(2,1)S(1)} %copy-done.2, bf16[864,1024]{1,0:T(8,128)(2,1)S(1)} %copy-done.1, bf16[6912,2048]{1,0:T(8,128)(2,1)} %get-tuple-element.40.pair), custom_call_target="tpu_custom_call" | custom-call | tf_op jit(solution)/shard_map/project/pallas_call | solution.py:240
  147.2 18.5 %all_to_all.21 = f32[128,8,128]{2,1,0:T(8,128)S(1)} all-to-all(f32[128,8,128]{2,1,0:T(8,128)S(1)} %project.1), channel_id=1, replica_groups=mesh['z'=4,'x_lo'=2,'core'=2,'x_hi'=2,'y'=4] {'z','x_lo','core','x_hi','y'}, dimensions={0} | all-to-all | bytes 1048576 | tf_op jit(solution)/shard_map/all_to_all | solution.py:467
  165.7 0.1 reduce_sum.9
  165.9 0.1 fusion.1
  165.9 0.6 pad_maximum_fusion.1
  (24 shorter events, 0.1 us)
Async XLA Ops:
  0.0 4.9 %copy-start.6 = (bf16[2048,64]{0,1:T(8,128)(2,1)S(1)}, bf16[2048,64]{0,1:T(8,128)(2,1)}, u32[]{:S(2)}) copy-start(bf16[2048,64]{0,1:T(8,128)(2,1)} %param.13) | copy-start | bytes 786436
  0.0 5.5 %copy-start.7 = (s32[2048]{0:T(1024)S(1)}, s32[2048]{0:T(1024)}, u32[]{:S(2)}) copy-start(s32[2048]{0:T(1024)} %param.14) | copy-start | bytes 24580
  5.5 44.6 %copy-start = (bf16[1024,864]{1,0:T(8,128)(2,1)S(1)}, bf16[1024,864]{1,0:T(8,128)(2,1)}, u32[]{:S(2)}) copy-start(bf16[1024,864]{1,0:T(8,128)(2,1)} %constant.86.clone.ahead) | copy-start | bytes 5308420
  5.5 44.6 %copy-start.3 = (bf16[512,512]{1,0:T(8,128)(2,1)S(1)}, bf16[512,512]{1,0:T(8,128)(2,1)}, u32[]{:S(2)}) copy-start(bf16[512,512]{1,0:T(8,128)(2,1)} %constant.87.clone.swap) | copy-start | bytes 1572868
  25.0 8.5 %collective-permute-start.2 = (bf16[320,512]{1,0:T(8,128)(2,1)S(1)}, bf16[320,512]{1,0:T(8,128)(2,1)S(1)}, u32[]{:S(2)}, u32[]{:S(2)}) collective-permute-start(bf16[320,512]{1,0:T(8,128)(2,1)S(1)} %convolution_convert_fusion.refs_0_), channel_id=1, source_target_pairs={{20,0},{21,1},{22,2},{23,3},{16,4},{17,5},{18,6},{19,7},{28,8},{29... | collective-permute-start | bytes 983048 | tf_op jit(solution)/shard_map/cond/branch_1_fun/ppermute | solution.py:276
  26.2 10.2 %collective-permute-start = (bf16[320,512]{1,0:T(8,128)(2,1)S(1)}, bf16[320,512]{1,0:T(8,128)(2,1)S(1)}, u32[]{:S(2)}, u32[]{:S(2)}) collective-permute-start(bf16[320,512]{1,0:T(8,128)(2,1)S(1)} %convolution_convert_fusion.refs_0_), channel_id=1, source_target_pairs={{16,0},{17,1},{18,2},{19,3},{20,4},{21,5},{22,6},{23,7},{24,8},{25... | collective-permute-start | bytes 983048 | tf_op jit(solution)/shard_map/cond/branch_1_fun/ppermute | solution.py:276
  27.7 11.7 %collective-permute-start.6 = (bf16[320,512]{1,0:T(8,128)(2,1)S(1)}, bf16[320,512]{1,0:T(8,128)(2,1)S(1)}, u32[]{:S(2)}, u32[]{:S(2)}) collective-permute-start(bf16[320,512]{1,0:T(8,128)(2,1)S(1)} %convolution_convert_fusion.refs_0_), channel_id=1, source_target_pairs={{8,0},{9,1},{10,2},{11,3},{12,4},{13,5},{14,6},{15,7},{0,8},{1,9},... | collective-permute-start | bytes 983048 | tf_op jit(solution)/shard_map/cond/branch_1_fun/ppermute | solution.py:276
  33.5 7.8 %collective-permute-start.5 = (bf16[320,512]{1,0:T(8,128)(2,1)S(1)}, bf16[320,512]{1,0:T(8,128)(2,1)S(1)}, u32[]{:S(2)}, u32[]{:S(2)}) collective-permute-start(bf16[320,512]{1,0:T(8,128)(2,1)S(1)} %collective-permute-done.2.refs_1_), channel_id=1, source_target_pairs={{8,0},{9,1},{10,2},{11,3},{12,4},{13,5},{14,6},{15,7},{0,8},{1,9},... | collective-permute-start | bytes 983048 | tf_op jit(solution)/shard_map/cond/branch_1_fun/ppermute | solution.py:276
  36.4 4.9 %collective-permute-start.4 = (bf16[320,512]{1,0:T(8,128)(2,1)S(1)}, bf16[320,512]{1,0:T(8,128)(2,1)S(1)}, u32[]{:S(2)}, u32[]{:S(2)}) collective-permute-start(bf16[320,512]{1,0:T(8,128)(2,1)S(1)} %collective-permute-done.refs_0_), channel_id=1, source_target_pairs={{8,0},{9,1},{10,2},{11,3},{12,4},{13,5},{14,6},{15,7},{0,8},{1,9},... | collective-permute-start | bytes 983048 | tf_op jit(solution)/shard_map/cond/branch_1_fun/ppermute | solution.py:276
  36.4 7.8 %collective-permute-start.3 = (bf16[160,512]{1,0:T(8,128)(2,1)S(1)}, bf16[160,512]{1,0:T(8,128)(2,1)S(1)}, u32[]{:S(2)}, u32[]{:S(2)}) collective-permute-start(bf16[160,512]{1,0:T(8,128)(2,1)S(1)} %slice.17), channel_id=1, source_target_pairs={{20,0},{21,1},{22,2},{23,3},{16,4},{17,5},{18,6},{19,7},{28,8},{29... | collective-permute-start | bytes 491528 | tf_op jit(solution)/shard_map/cond/branch_1_fun/ppermute | solution.py:276
  37.6 6.7 %collective-permute-start.1 = (bf16[160,512]{1,0:T(8,128)(2,1)S(1)}, bf16[160,512]{1,0:T(8,128)(2,1)S(1)}, u32[]{:S(2)}, u32[]{:S(2)}) collective-permute-start(bf16[160,512]{1,0:T(8,128)(2,1)S(1)} %slice.16), channel_id=1, source_target_pairs={{16,0},{17,1},{18,2},{19,3},{20,4},{21,5},{22,6},{23,7},{24,8},{25... | collective-permute-start | bytes 491528 | tf_op jit(solution)/shard_map/cond/branch_1_fun/ppermute | solution.py:276
  44.3 2.2 %collective-permute-start.7 = (bf16[160,512]{1,0:T(8,128)(2,1)S(1)}, bf16[160,512]{1,0:T(8,128)(2,1)S(1)}, u32[]{:S(2)}, u32[]{:S(2)}) collective-permute-start(bf16[160,512]{1,0:T(8,128)(2,1)S(1)} %collective-permute-done.1.refs_0_), channel_id=1, source_target_pairs={{8,0},{9,1},{10,2},{11,3},{12,4},{13,5},{14,6},{15,7},{0,8},{1,9},... | collective-permute-start | bytes 491528 | tf_op jit(solution)/shard_map/cond/branch_1_fun/ppermute | solution.py:276
  45.4 1.4 collective-permute-start.8
  80.9 23.4 %copy-start.4 = (bf16[96,96]{1,0:T(8,128)(2,1)S(1)}, bf16[96,96]{1,0:T(8,128)(2,1)}, u32[]{:S(2)}) copy-start(bf16[96,96]{1,0:T(8,128)(2,1)} %constant.90.clone.x_back) | copy-start | bytes 55300
  80.9 23.4 %copy-start.5 = (bf16[96,96]{1,0:T(8,128)(2,1)S(1)}, bf16[96,96]{1,0:T(8,128)(2,1)}, u32[]{:S(2)}) copy-start(bf16[96,96]{1,0:T(8,128)(2,1)} %constant.89.clone.x_ahead) | copy-start | bytes 55300
  80.9 23.4 %all-to-all-start.1 = ((bf16[128,32,128]{2,1,0:T(8,128)(2,1)}), bf16[128,32,128]{2,1,0:T(8,128)(2,1)S(1)}, u32[]{:S(2)}, u32[]{:S(2)}) async-start(bf16[128,32,128]{2,1,0:T(8,128)(2,1)} %bitcast.6), calls=%async_computation.1 | async-start | bytes 2097152 | tf_op jit(solution)/shard_map/all_to_all | solution.py:462
  104.2 30.6 %copy-start.2 = (bf16[512,512]{1,0:T(8,128)(2,1)S(1)}, bf16[512,512]{1,0:T(8,128)(2,1)}, u32[]{:S(2)}) copy-start(bf16[512,512]{1,0:T(8,128)(2,1)} %constant.91.clone.unswap) | copy-start | bytes 1572868
  111.7 23.2 %copy-start.1 = (bf16[864,1024]{1,0:T(8,128)(2,1)S(1)}, bf16[864,1024]{1,0:T(8,128)(2,1)}, u32[]{:S(2)}) copy-start(bf16[864,1024]{1,0:T(8,128)(2,1)} %constant.92.clone.back) | copy-start | bytes 5308420

commit v6 on v5

--- a/solution.py
+++ b/solution.py
@@ -70,13 +70,17 @@
 def pair_kernel(orb, rows_t, panel, ahead, swap, pair, send, fit):
     step = pl.program_id(0)
     npts = rows_t.shape[1]
-    chunk = 256
-    total = jnp.zeros((CELLS, 128), F32)
-    for start in range(0, npts, chunk):
-        corr = mm(orb[...], rows_t[:, start : start + chunk])
-        block = (corr * corr).astype(BF)
-        pair[:, start : start + chunk] = block
-        total = total + mm(block, panel[start : start + chunk, :])
+    chunk, rows = 1024, 256
+    totals = []
+    for first in range(0, CELLS, rows):
+        total = jnp.zeros((rows, 128), F32)
+        for start in range(0, npts, chunk):
+            corr = mm(orb[first : first + rows, :], rows_t[:, start : start + chunk])
+            block = (corr * corr).astype(BF)
+            pair[first : first + rows, start : start + chunk] = block
+            total = total + mm(block, panel[start : start + chunk, :])
+        totals.append(total)
+    total = jnp.concatenate(totals, axis=0)
     low = lax.broadcasted_iota(jnp.int32, (NG, 128), 1) < 64
     for two in range(4):
         even = total[2 * two * NG : (2 * two + 1) * NG]
@@ -149,7 +153,6 @@
     wave_y, wave_x = wave_of(lane), wave_of(subl)
     square = lambda w: w.astype(F32) * w.astype(F32)
     factor = NG / (2.0 * math.pi) * (NG / (2.0 * math.pi))
-    flat[...] = jnp.zeros_like(flat)
     fetch.wait()
     spec_y = mm(field[...].reshape(MI * NG, NG * CI), wide[...]).astype(BF)
     backs = []
@@ -328,45 +331,42 @@
     return lax.psum(picked, AXES).astype(BF).T
 
 
-def index_kernel(me, points, orbitals, fits, own, choose, slot, picks, spots, near, sems, one):
-    npts = points.shape[1]
+def owners(points, row_count):
+    return ((points.astype(F32) + 0.5) * (1.0 / row_count)).astype(jnp.int32)
+
+
+def ranks(label, labels):
+    size = 256
+    shape = (size, size)
+    early = lax.broadcasted_iota(jnp.int32, shape, 0) < lax.broadcasted_iota(jnp.int32, shape, 1)
+    early = jnp.where(early, 1.0, 0.0).astype(BF)
+    index = lax.broadcasted_iota(jnp.int32, (labels, size), 0)
+    seen = jnp.zeros((labels, 1), F32)
+    found = []
+    for first in range(0, label.shape[1], size):
+        match = jnp.where(index == label[:, first : first + size], 1.0, 0.0)
+        before = mm(match.astype(BF), early) + seen
+        found.append(jnp.sum(match * before, axis=0, keepdims=True))
+        seen = seen + jnp.sum(match, axis=1, keepdims=True)
+    return jnp.concatenate(found, axis=1).astype(jnp.int32), jnp.max(seen)
+
+
+def lookup(key, value, first, rows):
+    number = lax.broadcasted_iota(jnp.int32, (rows, 128), 0) + first
+    total = jnp.zeros((rows, 128), jnp.int32)
+    for start in range(0, key.shape[1], 128):
+        total = total + jnp.where(
+            key[:, start : start + 128] == number, value[:, start : start + 128], 0
+        )
+    return jnp.sum(total.astype(F32), axis=1, keepdims=True).astype(jnp.int32)
+
+
+def own_kernel(me, points, orbitals, own, rank, picks, spots, near, sems, one):
     row_count = orbitals.shape[0]
-    my_z, my_x, my_core, my_y = parts_of(me[0])
-    owner = ((points[...].astype(F32) + 0.5) * (1.0 / row_count)).astype(jnp.int32)
-    z, y, core = owner >> 5, owner & 3, (owner >> 3) & 1
-    x = ((owner >> 2) & 1) * 2 + ((owner >> 4) & 1)
-    group = x * 2 + core
-    size = 256
-    early = lax.broadcasted_iota(jnp.int32, (size, size), 0) < lax.broadcasted_iota(
-        jnp.int32, (size, size), 1
-    )
-    early = jnp.where(early, 1.0, 0.0).astype(BF)
-
-    def ranks(label, labels):
-        index = lax.broadcasted_iota(jnp.int32, (labels, size), 0)
-        seen = jnp.zeros((labels, 1), F32)
-        found = []
-        for first in range(0, npts, size):
-            match = jnp.where(index == label[:, first : first + size], 1.0, 0.0)
-            before = mm(match.astype(BF), early) + seen
-            found.append(jnp.sum(match * before, axis=0, keepdims=True))
-            seen = seen + jnp.sum(match, axis=1, keepdims=True)
-        return jnp.concatenate(found, axis=1).astype(jnp.int32), jnp.max(seen)
-
-    own_rank, own_most = ranks(owner, 128)
-    group_rank, group_most = ranks(group, 16)
-    fits[0] = ((own_most <= ROOM) & (group_most <= GROUP)).astype(jnp.int32)
-
-    def lookup(key, value, first, rows):
-        number = lax.broadcasted_iota(jnp.int32, (rows, 128), 0) + first
-        total = jnp.zeros((rows, 128), jnp.int32)
-        for start in range(0, npts, 128):
-            total = total + jnp.where(
-                key[:, start : start + 128] == number, value[:, start : start + 128], 0
-            )
-        return jnp.sum(total.astype(F32), axis=1, keepdims=True).astype(jnp.int32)
-
-    key = jnp.where(owner == me[0], own_rank, -1)
+    owner = owners(points[...], row_count)
+    mine = owner == me[0]
+    own_rank, _ = ranks(jnp.where(mine, 0, 16), 16)
+    key = jnp.where(mine, own_rank, -1)
     pick = lookup(key, points[...] - me[0] * row_count, 0, ROOM)
     picks[...] = jnp.broadcast_to(pick, (ROOM, 128))
     move = pltpu.make_async_copy(picks, spots, one)
@@ -383,7 +383,23 @@
             )
         )
         copies[-1].start()
-
+    rank[...] = owner
+    for copy in copies:
+        copy.wait()
+    lane = lax.broadcasted_iota(jnp.int32, (ROOM, 16 * ROOM), 1)
+    line = lax.broadcasted_iota(jnp.int32, (ROOM, 16 * ROOM), 0)
+    select = jnp.where(lane == line * 16 + (pick & 15), 1.0, 0.0).astype(BF)
+    own[...] = mm(select, near[...]).astype(BF)
+
+
+def index_kernel(me, owner_of, fits, choose, slot):
+    _, my_x, my_core, _ = parts_of(me[0])
+    owner = owner_of[...]
+    z, y, core = owner >> 5, owner & 3, (owner >> 3) & 1
+    x = ((owner >> 2) & 1) * 2 + ((owner >> 4) & 1)
+    own_rank, own_most = ranks(owner, 128)
+    group_rank, group_most = ranks(x * 2 + core, 16)
+    fits[0] = ((own_most <= ROOM) & (group_most <= GROUP)).astype(jnp.int32)
     spot = z * (4 * ROOM) + y * ROOM + own_rank
     key = jnp.where((x == my_x) & (core == my_core), group_rank, -1)
     for first in range(0, GROUP, 64):
@@ -391,26 +407,18 @@
         lane = lax.broadcasted_iota(jnp.int32, (64, 16 * ROOM), 1)
         choose[first : first + 64, :] = jnp.where(source == lane, 1.0, 0.0).astype(BF)
     slot[...] = (((core - my_core) & 1) * 4 + ((x - my_x) & 3)) * GROUP + group_rank
-    for copy in copies:
-        copy.wait()
-    lane = lax.broadcasted_iota(jnp.int32, (ROOM, 16 * ROOM), 1)
-    line = lax.broadcasted_iota(jnp.int32, (ROOM, 16 * ROOM), 0)
-    select = jnp.where(lane == line * 16 + (pick & 15), 1.0, 0.0).astype(BF)
-    own[...] = mm(select, near[...]).astype(BF)
-
-
-def index(me, points, orbitals):
+
+
+def fetch_own(me, points, orbitals):
     vmem = pl.BlockSpec(memory_space=pltpu.VMEM)
     smem = pl.BlockSpec(memory_space=pltpu.SMEM)
     npts, norb = points.shape[0], orbitals.shape[1]
     return pl.pallas_call(
-        index_kernel,
+        own_kernel,
         in_specs=[smem, vmem, pl.BlockSpec(memory_space=pl.ANY)],
-        out_specs=[smem, vmem, vmem, vmem],
+        out_specs=[vmem, vmem],
         out_shape=[
-            jax.ShapeDtypeStruct((1,), jnp.int32),
             jax.ShapeDtypeStruct((ROOM, norb), BF),
-            jax.ShapeDtypeStruct((GROUP, 16 * ROOM), BF),
             jax.ShapeDtypeStruct((1, npts), jnp.int32),
         ],
         scratch_shapes=[
@@ -421,14 +429,31 @@
             pltpu.SemaphoreType.DMA,
         ],
         compiler_params=pltpu.CompilerParams(vmem_limit_bytes=16 * 2**20),
+        name="own",
+    )(me.reshape(1), points[None], orbitals)
+
+
+def index(me, owner):
+    vmem = pl.BlockSpec(memory_space=pltpu.VMEM)
+    smem = pl.BlockSpec(memory_space=pltpu.SMEM)
+    return pl.pallas_call(
+        index_kernel,
+        in_specs=[smem, vmem],
+        out_specs=[smem, vmem, vmem],
+        out_shape=[
+            jax.ShapeDtypeStruct((1,), jnp.int32),
+            jax.ShapeDtypeStruct((GROUP, 16 * ROOM), BF),
+            jax.ShapeDtypeStruct(owner.shape, jnp.int32),
+        ],
+        compiler_params=pltpu.CompilerParams(vmem_limit_bytes=16 * 2**20),
+        cost_estimate=pl.CostEstimate(
+            flops=3 * 10**9, bytes_accessed=10**7, transcendentals=0
+        ),
         name="index",
-    )(me.reshape(1), points[None], orbitals)
-
-
-def spread_rows(own, choose, slot):
-    copies = jnp.broadcast_to(own[None], (16,) + own.shape)
-    square = lax.all_to_all(copies, ("z", "y"), 0, 0).reshape(16 * ROOM, own.shape[1])
-    held = mm(choose, square).astype(BF)
+    )(me.reshape(1), owner)
+
+
+def spread_rows(held, slot):
     mate = lambda block: bring(block, dcore=1)
     half, ring = GROUP // 2, 4 * GROUP
     right, left = bring(held, dx=1), bring(held, dx=3)
@@ -443,10 +468,14 @@
 
 
 def gather_rows(orbitals, points, me):
-    fits, own, choose, slot = index(me, points, orbitals)
+    own, owner = fetch_own(me, points, orbitals)
+    copies = jnp.broadcast_to(own[None], (16,) + own.shape)
+    square = lax.all_to_all(copies, ("z", "y"), 0, 0).reshape(16 * ROOM, own.shape[1])
+    fits, choose, slot = index(me, owner)
+    held = mm(choose, square).astype(BF)
     return lax.cond(
         fits[0] > 0,
-        lambda: spread_rows(own, choose, slot),
+        lambda: spread_rows(held, slot),
         lambda: summed_rows(orbitals, points, me),
     )
 

time: 167 us -> 165 us (0.988)
  blocking collectives: 60.7 us -> 41.7 us
  starting transfers between devices: 17.4 us -> 26.4 us
  waiting for transfers between devices: 22.9 us -> 31.2 us
    all_to_all x1 -> x0, blocking collectives: 19 us -> none  [spread_rows(): lax.all_to_all(copies, ('z', 'y'), 0, 0).reshape(16 * ROOM, own.shape[1])]
    all_to_all x0 -> x1, starting transfers between devices: none -> 8.99 us  [gather_rows(): lax.all_to_all(copies, ('z', 'y'), 0, 0).reshape(16 * ROOM, own.shape[1])]
    all_to_all x0 -> x1, waiting for transfers between devices: none -> 8.26 us  [gather_rows(): lax.all_to_all(copies, ('z', 'y'), 0, 0).reshape(16 * ROOM, own.shape[1])]
    pallas_call x1 -> x2, Pallas kernels: 4.32 us -> 4.55 us  [the longest x1 3.49 us: fetch_own(): pl.pallas_call(own_kernel, in_specs=[smem, vmem, pl.BlockSpec(memory_spac...]
  transfers between devices with their start and end apart: 10 -> 11, of which waited for: 4 -> 5; matrix products, arithmetic and copies ran while one was open for 0% -> 0% of each run, Pallas kernels for 3% -> 4%
where the time goes in v6:
time: 165 us
  Pallas kernels  62.2 us (38%)
  blocking collectives  41.7 us (25%)
  waiting for transfers between devices  31.2 us (19%)
  starting transfers between devices  26.4 us (16%)
    pallas_call x1, Pallas kernels, make_pairs(): pl.pallas_call(pair_kernel, grid=(steps,), in_specs=[pl.BlockSpec((CELLS,...  29.8 us
    all_to_all x1, blocking collectives, shards(): got = lax.all_to_all(ret.reshape(devices, ROWS, 128), AXES, 0, 0)  23.2 us
    all_to_all x1, blocking collectives, shards(): parts = lax.all_to_all(parts, AXES, 0, 0)  18.5 us
    all_to_all x1, waiting for transfers between devices, shards(): planes = lax.all_to_all(send.reshape(devices, ROWS, 128), AXES, 0, 0)  18.3 us
    pallas_call x1, Pallas kernels, project(): pl.pallas_call(project_kernel, in_specs=[vmem] * 3 + [pl.BlockSpec(memory...  12.4 us
    ppermute x9, starting transfers between devices, bring(): return lax.ppermute(data, AXES, pairs)  12.3 us
    all_to_all x1, starting transfers between devices, gather_rows(): lax.all_to_all(copies, ('z', 'y'), 0, 0).reshape(16 * ROOM, own.shape[1])  8.99 us
    all_to_all x1, waiting for transfers between devices, gather_rows(): lax.all_to_all(copies, ('z', 'y'), 0, 0).reshape(16 * ROOM, own.shape[1])  8.26 us
  transfers between devices with their start and end apart: 11, of which 5 were waited for; matrix products, arithmetic and copies ran while one was open for 0% of the time, Pallas kernels for 4%

profile of v6, /device:TPU:1, one launch (start us, length us, event | category | flops | bytes accessed | tf_op | source)
XLA Modules:
  0.0 165.0 jit_solution(12023334746339751125)
XLA Ops:
  0.0 3.5 %own.1 = (bf16[32,512]{1,0:T(8,128)(2,1)S(1)}, s32[1,2048]{1,0:T(1,128)S(1)}) custom-call(s32[1]{0:T(128)} %bitcast.2.me, s32[1,2048]{1,0:T(1,128)} %bitcast.19, bf16[6912,512]{1,0:T(8,128)(2,1)} %orb.1), custom_call_target="tpu_custom_call" | custom-call | tf_op jit(solution)/shard_map/own/pallas_call | solution.py:416
  3.5 0.9 broadcast_in_dim.31
  4.4 9.0 %all-to-all-start = ((bf16[16,32,512]{2,1,0:T(8,128)(2,1)}), bf16[16,32,512]{2,1,0:T(8,128)(2,1)S(1)}, u32[]{:S(2)}, u32[]{:S(2)}) async-start(bf16[16,32,512]{2,1,0:T(8,128)(2,1)} %broadcast_in_dim.31), calls=%async_computation | async-start | bytes 1048576 | tf_op jit(solution)/shard_map/all_to_all | solution.py:473
  13.4 1.1 index.1
  15.1 0.3 copy.12
  15.3 0.3 pad_maximum_fusion.panel
  15.6 8.3 %all-to-all-done = bf16[16,32,512]{2,1,0:T(8,128)(2,1)S(1)} async-done(((bf16[16,32,512]{2,1,0:T(8,128)(2,1)}), bf16[16,32,512]{2,1,0:T(8,128)(2,1)S(1)}, u32[]{:S(2)}, u32[]{:S(2)}) %all-to-all-start) | async-done | bytes 524320 | tf_op jit(solution)/shard_map/all_to_all | solution.py:473
  23.9 0.3 convolution_convert_fusion
  24.3 25.1 %conditional.1 = (bf16[512,2048]{1,0:T(8,128)(2,1)}) conditional(s32[]{:T(128)} %bitcast.4, (s32[]{:T(128)}, s32[2048]{0:T(1024)S(1)}, bf16[6912,512]{1,0:T(8,128)(2,1)}) %tuple.20, (bf16[320,512]{1,0:T(8,128)(2,1)S(1)}, s32[1,2048]{1,0:T(1,128)S(1)}) %tuple.13), branch_computations={%region_0.2_spmd, %region_2.3_spmd} | conditional | flops 5368709120 | bytes 22413680 | solution.py:476
  24.3 1.2 collective-permute-start.2
  25.5 1.6 collective-permute-start
  27.1 2.5 %collective-permute-start.6 = (bf16[320,512]{1,0:T(8,128)(2,1)S(1)}, bf16[320,512]{1,0:T(8,128)(2,1)S(1)}, u32[]{:S(2)}, u32[]{:S(2)}) collective-permute-start(bf16[320,512]{1,0:T(8,128)(2,1)S(1)} %get-tuple-element.21.refs_0_), channel_id=1, source_target_pairs={{8,0},{9,1},{10,2},{11,3},{12,4},{13,5},{14,6},{15,7},{0,8},{1,9},... | collective-permute-start | bytes 983048 | tf_op jit(solution)/shard_map/cond/branch_1_fun/ppermute | solution.py:279
  29.5 3.3 %collective-permute-done.2.refs_1_ = bf16[320,512]{1,0:T(8,128)(2,1)S(1)} collective-permute-done((bf16[320,512]{1,0:T(8,128)(2,1)S(1)}, bf16[320,512]{1,0:T(8,128)(2,1)S(1)}, u32[]{:S(2)}, u32[]{:S(2)}) %collective-permute-start.2) | collective-permute-done | bytes 327712 | tf_op jit(solution)/shard_map/cond/branch_1_fun/ppermute | solution.py:279
  32.9 2.9 %collective-permute-start.5 = (bf16[320,512]{1,0:T(8,128)(2,1)S(1)}, bf16[320,512]{1,0:T(8,128)(2,1)S(1)}, u32[]{:S(2)}, u32[]{:S(2)}) collective-permute-start(bf16[320,512]{1,0:T(8,128)(2,1)S(1)} %collective-permute-done.2.refs_1_), channel_id=1, source_target_pairs={{8,0},{9,1},{10,2},{11,3},{12,4},{13,5},{14,6},{15,7},{0,8},{1,9},... | collective-permute-start | bytes 983048 | tf_op jit(solution)/shard_map/cond/branch_1_fun/ppermute | solution.py:279
  35.7 1.1 collective-permute-start.3
  36.9 1.9 %collective-permute-start.1 = (bf16[160,512]{1,0:T(8,128)(2,1)S(1)}, bf16[160,512]{1,0:T(8,128)(2,1)S(1)}, u32[]{:S(2)}, u32[]{:S(2)}) collective-permute-start(bf16[160,512]{1,0:T(8,128)(2,1)S(1)} %slice.16), channel_id=1, source_target_pairs={{16,0},{17,1},{18,2},{19,3},{20,4},{21,5},{22,6},{23,7},{24,8},{25... | collective-permute-start | bytes 491528 | tf_op jit(solution)/shard_map/cond/branch_1_fun/ppermute | solution.py:279
  38.8 1.8 %place.3.refs_5_ = bf16[512,2048]{1,0:T(8,128)(2,1)S(1)} custom-call(bf16[320,512]{1,0:T(8,128)(2,1)S(1)} %get-tuple-element.21.refs_0_, bf16[320,512]{1,0:T(8,128)(2,1)S(1)} %collective-permute-done.6.refs_1_, s32[1,2048]{1,0:T(1,128)S(1)} %get-tuple-element.22.refs_2_.refs_4_), custom_call_target="tpu_custom_call" | custom-call | flops 1342177280 | bytes 4194304 | tf_op jit(solution)/shard_map/cond/branch_1_fun/place/pallas_call | solution.py:311
  40.6 2.9 %place.4.refs_5_ = bf16[512,2048]{1,0:T(8,128)(2,1)S(1)} custom-call(bf16[320,512]{1,0:T(8,128)(2,1)S(1)} %collective-permute-done.refs_0_, bf16[320,512]{1,0:T(8,128)(2,1)S(1)} %collective-permute-done.2.refs_1_, bf16[320,512]{1,0:T(8,128)(2,1)S(1)} %collective-permute-done.4.refs_2_, bf16[320,512]{1,0:T(8,128)(2,1)S(1)} %collective-permute-done.5.refs_3_, ...), custom_call_target="tpu_custom_call" | custom-call | flops 2684354560 | bytes 4194304 | tf_op jit(solution)/shard_map/cond/branch_1_fun/place/pallas_call | solution.py:311
  43.6 1.1 collective-permute-start.7
  44.7 0.1 collective-permute-start.8
  44.8 0.9 collective-permute-done.7.refs_2_
  45.8 0.4 collective-permute-done.8.refs_3_
  46.1 3.3 %place.5 = bf16[512,2048]{1,0:T(8,128)(2,1)} custom-call(bf16[160,512]{1,0:T(8,128)(2,1)S(1)} %collective-permute-done.1.refs_0_, bf16[160,512]{1,0:T(8,128)(2,1)S(1)} %collective-permute-done.3.refs_1_, bf16[160,512]{1,0:T(8,128)(2,1)S(1)} %collective-permute-done.7.refs_2_, bf16[160,512]{1,0:T(8,128)(2,1)S(1)} %collective-permute-done.8.refs_3_, ...), custom_call_target="tpu_custom_call" | custom-call | flops 1342177280 | bytes 4194304 | tf_op jit(solution)/shard_map/cond/branch_1_fun/place/pallas_call | solution.py:311
  49.4 29.8 %pairs.1 = (bf16[6912,2048]{1,0:T(8,128)(2,1)}, bf16[32,4,32,128]{3,2,1,0:T(8,128)(2,1)}) custom-call(bf16[6912,512]{1,0:T(8,128)(2,1)} %orb.1, bf16[512,2048]{1,0:T(8,128)(2,1)} %get-tuple-element.40.rows_t, bf16[2048,128]{1,0:T(8,128)(2,1)S(1)} %pad_maximum_fusion.panel, bf16[1024,864]{1,0:T(8,128)(2,1)S(1)} %copy-done, bf16[512,512]{1,0:T(8,128)(2,1)S(1)} %copy-done.3), custom_call_target="tpu_custom_call" | custom-call | tf_op jit(solution)/shard_map/pairs/pallas_call | solution.py:109
  79.3 5.1 %all-to-all-start.1 = ((bf16[128,32,128]{2,1,0:T(8,128)(2,1)}), bf16[128,32,128]{2,1,0:T(8,128)(2,1)S(1)}, u32[]{:S(2)}, u32[]{:S(2)}) async-start(bf16[128,32,128]{2,1,0:T(8,128)(2,1)} %bitcast.6), calls=%async_computation.1 | async-start | bytes 2097152 | tf_op jit(solution)/shard_map/all_to_all | solution.py:491
  84.4 18.3 %all-to-all-done.1 = bf16[128,32,128]{2,1,0:T(8,128)(2,1)S(1)} async-done(((bf16[128,32,128]{2,1,0:T(8,128)(2,1)}), bf16[128,32,128]{2,1,0:T(8,128)(2,1)S(1)}, u32[]{:S(2)}, u32[]{:S(2)}) %all-to-all-start.1) | async-done | bytes 1048608 | tf_op jit(solution)/shard_map/all_to_all | solution.py:491
  102.7 7.4 %solve.1 = bf16[4096,128]{1,0:T(8,128)(2,1)S(1)} custom-call(s32[1]{0:T(128)} %bitcast.1.first, bf16[4096,128]{1,0:T(8,128)(2,1)S(1)} %bitcast.15, bf16[1536,1536]{1,0:T(8,128)(2,1)} %constant.88.clone.table, bf16[96,96]{1,0:T(8,128)(2,1)S(1)} %copy-done.5, bf16[96,96]{1,0:T(8,128)(2,1)S(1)} %copy-done.4), custom_call_target="tpu_custom_call" | custom-call | tf_op jit(solution)/shard_map/solve/pallas_call | solution.py:182
  110.1 23.2 %all_to_all.20 = bf16[128,32,128]{2,1,0:T(8,128)(2,1)S(1)} all-to-all(bf16[128,32,128]{2,1,0:T(8,128)(2,1)S(1)} %bitcast.16), channel_id=1, replica_groups=mesh['z'=4,'x_lo'=2,'core'=2,'x_hi'=2,'y'=4] {'z','x_lo','core','x_hi','y'}, dimensions={0} | all-to-all | bytes 2097152 | tf_op jit(solution)/shard_map/all_to_all | solution.py:494
  133.3 12.4 %project.1 = f32[128,8,128]{2,1,0:T(8,128)S(1)} custom-call(bf16[32,4,32,128]{3,2,1,0:T(8,128)(2,1)S(1)} %bitcast.14, bf16[512,512]{1,0:T(8,128)(2,1)S(1)} %copy-done.2, bf16[864,1024]{1,0:T(8,128)(2,1)S(1)} %copy-done.1, bf16[6912,2048]{1,0:T(8,128)(2,1)} %get-tuple-element.39.pair), custom_call_target="tpu_custom_call" | custom-call | tf_op jit(solution)/shard_map/project/pallas_call | solution.py:243
  145.6 18.5 %all_to_all.21 = f32[128,8,128]{2,1,0:T(8,128)S(1)} all-to-all(f32[128,8,128]{2,1,0:T(8,128)S(1)} %project.1), channel_id=1, replica_groups=mesh['z'=4,'x_lo'=2,'core'=2,'x_hi'=2,'y'=4] {'z','x_lo','core','x_hi','y'}, dimensions={0} | all-to-all | bytes 1048576 | tf_op jit(solution)/shard_map/all_to_all | solution.py:496
  164.2 0.1 reduce_sum.9
  164.4 0.6 pad_maximum_fusion.1
  (26 shorter events, 0.2 us)
Async XLA Ops:
  4.4 19.6 %all-to-all-start = ((bf16[16,32,512]{2,1,0:T(8,128)(2,1)}), bf16[16,32,512]{2,1,0:T(8,128)(2,1)S(1)}, u32[]{:S(2)}, u32[]{:S(2)}) async-start(bf16[16,32,512]{2,1,0:T(8,128)(2,1)} %broadcast_in_dim.31), calls=%async_computation | async-start | bytes 1048576 | tf_op jit(solution)/shard_map/all_to_all | solution.py:473
  13.4 1.7 %copy-start.6 = (bf16[2048,64]{0,1:T(8,128)(2,1)S(1)}, bf16[2048,64]{0,1:T(8,128)(2,1)}, u32[]{:S(2)}) copy-start(bf16[2048,64]{0,1:T(8,128)(2,1)} %param.13) | copy-start | bytes 786436
  14.4 9.8 %copy-start.7 = (s32[2048]{0:T(1024)S(1)}, s32[2048]{0:T(1024)}, u32[]{:S(2)}) copy-start(s32[2048]{0:T(1024)} %param.14) | copy-start | bytes 24580
  24.3 25.2 %copy-start = (bf16[1024,864]{1,0:T(8,128)(2,1)S(1)}, bf16[1024,864]{1,0:T(8,128)(2,1)}, u32[]{:S(2)}) copy-start(bf16[1024,864]{1,0:T(8,128)(2,1)} %constant.86.clone.ahead) | copy-start | bytes 5308420
  24.3 25.2 %copy-start.3 = (bf16[512,512]{1,0:T(8,128)(2,1)S(1)}, bf16[512,512]{1,0:T(8,128)(2,1)}, u32[]{:S(2)}) copy-start(bf16[512,512]{1,0:T(8,128)(2,1)} %constant.87.clone.swap) | copy-start | bytes 1572868
  24.3 8.6 %collective-permute-start.2 = (bf16[320,512]{1,0:T(8,128)(2,1)S(1)}, bf16[320,512]{1,0:T(8,128)(2,1)S(1)}, u32[]{:S(2)}, u32[]{:S(2)}) collective-permute-start(bf16[320,512]{1,0:T(8,128)(2,1)S(1)} %get-tuple-element.21.refs_0_), channel_id=1, source_target_pairs={{20,0},{21,1},{22,2},{23,3},{16,4},{17,5},{18,6},{19,7},{28,8},{29... | collective-permute-start | bytes 983048 | tf_op jit(solution)/shard_map/cond/branch_1_fun/ppermute | solution.py:279
  25.5 10.2 %collective-permute-start = (bf16[320,512]{1,0:T(8,128)(2,1)S(1)}, bf16[320,512]{1,0:T(8,128)(2,1)S(1)}, u32[]{:S(2)}, u32[]{:S(2)}) collective-permute-start(bf16[320,512]{1,0:T(8,128)(2,1)S(1)} %get-tuple-element.21.refs_0_), channel_id=1, source_target_pairs={{16,0},{17,1},{18,2},{19,3},{20,4},{21,5},{22,6},{23,7},{24,8},{25... | collective-permute-start | bytes 983048 | tf_op jit(solution)/shard_map/cond/branch_1_fun/ppermute | solution.py:279
  27.1 11.7 %collective-permute-start.6 = (bf16[320,512]{1,0:T(8,128)(2,1)S(1)}, bf16[320,512]{1,0:T(8,128)(2,1)S(1)}, u32[]{:S(2)}, u32[]{:S(2)}) collective-permute-start(bf16[320,512]{1,0:T(8,128)(2,1)S(1)} %get-tuple-element.21.refs_0_), channel_id=1, source_target_pairs={{8,0},{9,1},{10,2},{11,3},{12,4},{13,5},{14,6},{15,7},{0,8},{1,9},... | collective-permute-start | bytes 983048 | tf_op jit(solution)/shard_map/cond/branch_1_fun/ppermute | solution.py:279
  32.9 7.8 %collective-permute-start.5 = (bf16[320,512]{1,0:T(8,128)(2,1)S(1)}, bf16[320,512]{1,0:T(8,128)(2,1)S(1)}, u32[]{:S(2)}, u32[]{:S(2)}) collective-permute-start(bf16[320,512]{1,0:T(8,128)(2,1)S(1)} %collective-permute-done.2.refs_1_), channel_id=1, source_target_pairs={{8,0},{9,1},{10,2},{11,3},{12,4},{13,5},{14,6},{15,7},{0,8},{1,9},... | collective-permute-start | bytes 983048 | tf_op jit(solution)/shard_map/cond/branch_1_fun/ppermute | solution.py:279
  35.7 4.9 %collective-permute-start.4 = (bf16[320,512]{1,0:T(8,128)(2,1)S(1)}, bf16[320,512]{1,0:T(8,128)(2,1)S(1)}, u32[]{:S(2)}, u32[]{:S(2)}) collective-permute-start(bf16[320,512]{1,0:T(8,128)(2,1)S(1)} %collective-permute-done.refs_0_), channel_id=1, source_target_pairs={{8,0},{9,1},{10,2},{11,3},{12,4},{13,5},{14,6},{15,7},{0,8},{1,9},... | collective-permute-start | bytes 983048 | tf_op jit(solution)/shard_map/cond/branch_1_fun/ppermute | solution.py:279
  35.7 7.8 %collective-permute-start.3 = (bf16[160,512]{1,0:T(8,128)(2,1)S(1)}, bf16[160,512]{1,0:T(8,128)(2,1)S(1)}, u32[]{:S(2)}, u32[]{:S(2)}) collective-permute-start(bf16[160,512]{1,0:T(8,128)(2,1)S(1)} %slice.17), channel_id=1, source_target_pairs={{20,0},{21,1},{22,2},{23,3},{16,4},{17,5},{18,6},{19,7},{28,8},{29... | collective-permute-start | bytes 491528 | tf_op jit(solution)/shard_map/cond/branch_1_fun/ppermute | solution.py:279
  36.9 6.7 %collective-permute-start.1 = (bf16[160,512]{1,0:T(8,128)(2,1)S(1)}, bf16[160,512]{1,0:T(8,128)(2,1)S(1)}, u32[]{:S(2)}, u32[]{:S(2)}) collective-permute-start(bf16[160,512]{1,0:T(8,128)(2,1)S(1)} %slice.16), channel_id=1, source_target_pairs={{16,0},{17,1},{18,2},{19,3},{20,4},{21,5},{22,6},{23,7},{24,8},{25... | collective-permute-start | bytes 491528 | tf_op jit(solution)/shard_map/cond/branch_1_fun/ppermute | solution.py:279
  43.6 2.2 %collective-permute-start.7 = (bf16[160,512]{1,0:T(8,128)(2,1)S(1)}, bf16[160,512]{1,0:T(8,128)(2,1)S(1)}, u32[]{:S(2)}, u32[]{:S(2)}) collective-permute-start(bf16[160,512]{1,0:T(8,128)(2,1)S(1)} %collective-permute-done.1.refs_0_), channel_id=1, source_target_pairs={{8,0},{9,1},{10,2},{11,3},{12,4},{13,5},{14,6},{15,7},{0,8},{1,9},... | collective-permute-start | bytes 491528 | tf_op jit(solution)/shard_map/cond/branch_1_fun/ppermute | solution.py:279
  44.7 1.4 collective-permute-start.8
  79.3 23.4 %copy-start.4 = (bf16[96,96]{1,0:T(8,128)(2,1)S(1)}, bf16[96,96]{1,0:T(8,128)(2,1)}, u32[]{:S(2)}) copy-start(bf16[96,96]{1,0:T(8,128)(2,1)} %constant.90.clone.x_back) | copy-start | bytes 55300
  79.3 23.4 %copy-start.5 = (bf16[96,96]{1,0:T(8,128)(2,1)S(1)}, bf16[96,96]{1,0:T(8,128)(2,1)}, u32[]{:S(2)}) copy-start(bf16[96,96]{1,0:T(8,128)(2,1)} %constant.89.clone.x_ahead) | copy-start | bytes 55300
  79.3 23.4 %all-to-all-start.1 = ((bf16[128,32,128]{2,1,0:T(8,128)(2,1)}), bf16[128,32,128]{2,1,0:T(8,128)(2,1)S(1)}, u32[]{:S(2)}, u32[]{:S(2)}) async-start(bf16[128,32,128]{2,1,0:T(8,128)(2,1)} %bitcast.6), calls=%async_computation.1 | async-start | bytes 2097152 | tf_op jit(solution)/shard_map/all_to_all | solution.py:491
  102.7 30.6 %copy-start.2 = (bf16[512,512]{1,0:T(8,128)(2,1)S(1)}, bf16[512,512]{1,0:T(8,128)(2,1)}, u32[]{:S(2)}) copy-start(bf16[512,512]{1,0:T(8,128)(2,1)} %constant.91.clone.unswap) | copy-start | bytes 1572868
  110.1 23.2 %copy-start.1 = (bf16[864,1024]{1,0:T(8,128)(2,1)S(1)}, bf16[864,1024]{1,0:T(8,128)(2,1)}, u32[]{:S(2)}) copy-start(bf16[864,1024]{1,0:T(8,128)(2,1)} %constant.92.clone.back) | copy-start | bytes 5308420

commit v7 on v6

--- a/solution.py
+++ b/solution.py
@@ -21,6 +21,10 @@
 MG, MI = 32, 3
 CG, CI = 4, 16
 ROWS = 32
+ROOM = 32
+GROUP = 320
+HALF_GROUP = GROUP // 2
+FAR = (2 * GROUP, 2 * GROUP + HALF_GROUP, 6 * GROUP, 6 * GROUP + HALF_GROUP)
 CELLS = 8 * NG
 WIDE = 9 * NG
 
@@ -67,8 +71,15 @@
     return jnp.dot(a, b, preferred_element_type=F32)
 
 
-def pair_kernel(orb, rows_t, panel, ahead, swap, pair, send, fit):
+def pair_kernel(
+    orb, part_t, slot, far0, far1, far2, far3, panel, ahead, swap, pair, send, fit, rows_t, held
+):
     step = pl.program_id(0)
+
+    @pl.when(step == 0)
+    def _():
+        fill(FAR, (far0, far1, far2, far3), slot, (part_t,), held, rows_t)
+
     npts = rows_t.shape[1]
     chunk, rows = 1024, 256
     totals = []
@@ -101,8 +112,8 @@
                 ].reshape(MG // 4, ROWS, 128)
 
 
-def make_pairs(orbitals, rows_t, panel2, tab):
-    npts = rows_t.shape[1]
+def make_pairs(orbitals, part_t, slot, far, panel2, tab):
+    npts = part_t.shape[1]
     norb = orbitals.shape[1]
     steps = orbitals.shape[0] // CELLS
     whole = lambda shape: pl.BlockSpec(shape, lambda i: (0,) * len(shape))
@@ -111,7 +122,9 @@
         grid=(steps,),
         in_specs=[
             pl.BlockSpec((CELLS, norb), lambda i: (i, 0)),
-            whole(rows_t.shape),
+            whole(part_t.shape),
+            whole(slot.shape),
+            *[whole(block.shape) for block in far],
             whole(panel2.shape),
             whole(tab["ahead"].shape),
             whole(tab["swap"].shape),
@@ -124,10 +137,14 @@
             jax.ShapeDtypeStruct((orbitals.shape[0], npts), BF),
             jax.ShapeDtypeStruct((MG, CG, ROWS, 128), BF),
         ],
-        scratch_shapes=[pltpu.VMEM((OCT * NG, 512), BF)],
-        compiler_params=pltpu.CompilerParams(vmem_limit_bytes=28 * 2**20),
+        scratch_shapes=[
+            pltpu.VMEM((OCT * NG, 512), BF),
+            pltpu.VMEM(part_t.shape, BF),
+            pltpu.VMEM((4 * HALF_GROUP, norb), BF),
+        ],
+        compiler_params=pltpu.CompilerParams(vmem_limit_bytes=36 * 2**20),
         name="pairs",
-    )(orbitals, rows_t, panel2, const(tab["ahead"]), const(tab["swap"]))
+    )(orbitals, part_t, slot, *far, panel2, const(tab["ahead"]), const(tab["swap"]))
 
 
 def places():
@@ -138,7 +155,7 @@
                 yield part * ROWS + octet * MI + mi, mi, spot // 12, spot % 12
 
 
-def solve_kernel(first, got, table, x_ahead, x_back, out, flat, field, wide, sem):
+def solve_kernel(me, got, table, x_ahead, x_back, out, flat, field, wide, sem):
     fetch = pltpu.make_async_copy(table, wide, sem)
     fetch.start()
     flat[...] = got[...].astype(F32)
@@ -157,7 +174,7 @@
     spec_y = mm(field[...].reshape(MI * NG, NG * CI), wide[...]).astype(BF)
     backs = []
     for mi in range(MI):
-        wave_z = wave_of(first[0] + mi)
+        wave_z = wave_of((me[0] >> 2) * MI + mi)
         spec = mm(x_ahead[...], spec_y[mi * NG : (mi + 1) * NG])
         total = square(wave_x) + square(wave_y) + square(wave_z)
         gain = weight(wave_x) * (weight(wave_y) * weight(wave_z))
@@ -177,7 +194,7 @@
     out[...] = flat[...].astype(BF)
 
 
-def solve(first, got, tab):
+def solve(me, got, tab):
     vmem = pl.BlockSpec(memory_space=pltpu.VMEM)
     return pl.pallas_call(
         solve_kernel,
@@ -194,7 +211,7 @@
         compiler_params=pltpu.CompilerParams(vmem_limit_bytes=48 * 2**20),
         name="solve",
     )(
-        first,
+        me,
         got,
         const(tab["wide"]),
         const(tab["x_ahead"]),
@@ -257,10 +274,6 @@
     )(got, const(tab["unswap"]), const(tab["back"]), pair)
 
 
-ROOM = 32
-GROUP = 320
-
-
 def parts_of(device):
     grid, vec = device // 8, device % 8
     return grid // 4, (vec // 4) * 2 + (grid // 2) % 2, grid % 2, vec % 4
@@ -279,8 +292,7 @@
     return lax.ppermute(data, AXES, pairs)
 
 
-def place_kernel(count, base, *refs):
-    blocks, (slot, *more), (out, held) = refs[:count], refs[count:-2], refs[-2:]
+def fill(base, blocks, slot, more, held, out):
     start = 0
     for block in blocks:
         rows = block.shape[0]
@@ -302,6 +314,11 @@
         if more:
             total = total + more[0][:, first : first + chunk].astype(F32)
         out[:, first : first + chunk] = total.astype(BF)
+
+
+def place_kernel(count, base, *refs):
+    blocks, (slot, *more), (out, held) = refs[:count], refs[count:-2], refs[-2:]
+    fill(base, blocks, slot, more, held, out)
 
 
 def place(slot, blocks, base, more=()):
@@ -399,14 +416,16 @@
     x = ((owner >> 2) & 1) * 2 + ((owner >> 4) & 1)
     own_rank, own_most = ranks(owner, 128)
     group_rank, group_most = ranks(x * 2 + core, 16)
-    fits[0] = ((own_most <= ROOM) & (group_most <= GROUP)).astype(jnp.int32)
+    fit = (own_most <= ROOM) & (group_most <= GROUP)
+    fits[0] = fit.astype(jnp.int32)
     spot = z * (4 * ROOM) + y * ROOM + own_rank
     key = jnp.where((x == my_x) & (core == my_core), group_rank, -1)
     for first in range(0, GROUP, 64):
         source = lookup(key, spot + 1, first, 64) - 1
         lane = lax.broadcasted_iota(jnp.int32, (64, 16 * ROOM), 1)
         choose[first : first + 64, :] = jnp.where(source == lane, 1.0, 0.0).astype(BF)
-    slot[...] = (((core - my_core) & 1) * 4 + ((x - my_x) & 3)) * GROUP + group_rank
+    number = (((core - my_core) & 1) * 4 + ((x - my_x) & 3)) * GROUP + group_rank
+    slot[...] = jnp.where(fit, number, -1)
 
 
 def fetch_own(me, points, orbitals):
@@ -462,9 +481,7 @@
     near = [right, left, mate(right), mate(left)]
     rows = place(slot, near, (GROUP, 3 * GROUP, ring + GROUP, ring + 3 * GROUP), (rows,))
     far_a, far_b, rows = lax.optimization_barrier((far_a, far_b, rows))
-    far = [far_a, far_b, mate(far_a), mate(far_b)]
-    start = 2 * GROUP
-    return place(slot, far, (start, start + half, ring + start, ring + start + half), (rows,))
+    return rows, far_a, far_b, mate(far_a), mate(far_b)
 
 
 def gather_rows(orbitals, points, me):
@@ -473,11 +490,13 @@
     square = lax.all_to_all(copies, ("z", "y"), 0, 0).reshape(16 * ROOM, own.shape[1])
     fits, choose, slot = index(me, owner)
     held = mm(choose, square).astype(BF)
-    return lax.cond(
+    none = jnp.zeros((HALF_GROUP, orbitals.shape[1]), BF)
+    rows, *far = lax.cond(
         fits[0] > 0,
         lambda: spread_rows(held, slot),
-        lambda: summed_rows(orbitals, points, me),
+        lambda: (summed_rows(orbitals, points, me), none, none, none, none),
     )
+    return rows, slot, far
 
 
 def shards(orbitals, inverse_panel, points):
@@ -485,12 +504,11 @@
     devices = lax.axis_size(AXES)
     me = lax.axis_index(AXES)
     npoints, cols = inverse_panel.shape
-    rows_t = gather_rows(orbitals, points, me)
+    part_t, slot, far = gather_rows(orbitals, points, me)
     panel2 = jnp.concatenate([inverse_panel, inverse_panel], axis=1)
-    pair, send = make_pairs(orbitals, rows_t, panel2, tab)
+    pair, send = make_pairs(orbitals, part_t, slot, far, panel2, tab)
     planes = lax.all_to_all(send.reshape(devices, ROWS, 128), AXES, 0, 0)
-    first = (me // CG * MI).astype(jnp.int32).reshape(1)
-    ret = solve(first, planes.reshape(devices * ROWS, 128), tab)
+    ret = solve(me.reshape(1), planes.reshape(devices * ROWS, 128), tab)
     got = lax.all_to_all(ret.reshape(devices, ROWS, 128), AXES, 0, 0)
     parts = project(got.reshape(MG, CG, ROWS, 128), pair, tab)
     parts = lax.all_to_all(parts, AXES, 0, 0)

time: 165 us -> 164 us (level)
  blocking collectives: 41.7 us -> 63.7 us
  waiting for transfers between devices: 31.2 us -> 13.4 us
  starting transfers between devices: 26.4 us -> 20.5 us
    all_to_all x0 -> x1, blocking collectives: none -> 22 us  [shards(): planes = lax.all_to_all(send.reshape(devices, ROWS, 128), AXES, 0, 0)]
    all_to_all x1 -> x0, waiting for transfers between devices: 18.3 us -> none  [shards(): planes = lax.all_to_all(send.reshape(devices, ROWS, 128), AXES, 0, 0)]
    all_to_all x1 -> x0, starting transfers between devices: 5.07 us -> none  [shards(): planes = lax.all_to_all(send.reshape(devices, ROWS, 128), AXES, 0, 0)]
    pallas_call x3 -> x2, Pallas kernels: 8.07 us -> 6.24 us  [place(): pl.pallas_call(functools.partial(place_kernel, len(blocks), base), in_spe...]
    pallas_call x1, Pallas kernels: 29.8 us -> 31.7 us  [make_pairs(): pl.pallas_call(pair_kernel, grid=(steps,), in_specs=[pl.BlockSpec((CELLS,...]
  transfers between devices with their start and end apart: 11 -> 10, of which waited for: 5 -> 4; matrix products, arithmetic and copies ran while one was open for 0% -> 0% of each run, Pallas kernels for 4% -> 4%
where the time goes in v7:
time: 164 us
  blocking collectives  63.7 us (39%)
  Pallas kernels  62.5 us (38%)
  starting transfers between devices  20.5 us (12%)
  waiting for transfers between devices  13.4 us (8%)
    pallas_call x1, Pallas kernels, make_pairs(): pl.pallas_call(pair_kernel, grid=(steps,), in_specs=[pl.BlockSpec((CELLS,...  31.7 us
    all_to_all x1, blocking collectives, shards(): got = lax.all_to_all(ret.reshape(devices, ROWS, 128), AXES, 0, 0)  23.2 us
    all_to_all x1, blocking collectives, shards(): planes = lax.all_to_all(send.reshape(devices, ROWS, 128), AXES, 0, 0)  22 us
    all_to_all x1, blocking collectives, shards(): parts = lax.all_to_all(parts, AXES, 0, 0)  18.5 us
    pallas_call x1, Pallas kernels, project(): pl.pallas_call(project_kernel, in_specs=[vmem] * 3 + [pl.BlockSpec(memory...  12.4 us
    ppermute x9, starting transfers between devices, bring(): return lax.ppermute(data, AXES, pairs)  12.2 us
    all_to_all x1, waiting for transfers between devices, gather_rows(): lax.all_to_all(copies, ('z', 'y'), 0, 0).reshape(16 * ROOM, own.shape[1])  8.41 us
    all_to_all x1, starting transfers between devices, gather_rows(): lax.all_to_all(copies, ('z', 'y'), 0, 0).reshape(16 * ROOM, own.shape[1])  8.3 us
  transfers between devices with their start and end apart: 10, of which 4 were waited for; matrix products, arithmetic and copies ran while one was open for 0% of the time, Pallas kernels for 4%

profile of v7, /device:TPU:1, one launch (start us, length us, event | category | flops | bytes accessed | tf_op | source)
XLA Modules:
  0.0 163.5 jit_solution(3326019054983355417)
XLA Ops:
  0.0 3.9 %own.1 = (bf16[32,512]{1,0:T(8,128)(2,1)S(1)}, s32[1,2048]{1,0:T(1,128)S(1)}) custom-call(s32[1]{0:T(128)} %bitcast.1.me, s32[1,2048]{1,0:T(1,128)} %bitcast.19, bf16[6912,512]{1,0:T(8,128)(2,1)} %orb.1), custom_call_target="tpu_custom_call" | custom-call | tf_op jit(solution)/shard_map/own/pallas_call | solution.py:435
  3.9 0.9 broadcast_in_dim.34
  4.8 8.3 %all-to-all-start = ((bf16[16,32,512]{2,1,0:T(8,128)(2,1)}), bf16[16,32,512]{2,1,0:T(8,128)(2,1)S(1)}, u32[]{:S(2)}, u32[]{:S(2)}) async-start(bf16[16,32,512]{2,1,0:T(8,128)(2,1)} %broadcast_in_dim.34), calls=%async_computation | async-start | bytes 1048576 | tf_op jit(solution)/shard_map/all_to_all | solution.py:490
  13.1 1.0 index.1
  14.7 0.3 copy.12
  14.9 0.3 pad_maximum_fusion.panel
  15.2 8.4 %all-to-all-done = bf16[16,32,512]{2,1,0:T(8,128)(2,1)S(1)} async-done(((bf16[16,32,512]{2,1,0:T(8,128)(2,1)}), bf16[16,32,512]{2,1,0:T(8,128)(2,1)S(1)}, u32[]{:S(2)}, u32[]{:S(2)}) %all-to-all-start) | async-done | bytes 524320 | tf_op jit(solution)/shard_map/all_to_all | solution.py:490
  23.6 0.3 convolution_convert_fusion
  24.0 0.0 copy-start
  24.0 23.5 %conditional.1 = (bf16[160,512]{1,0:T(8,128)(2,1)}, bf16[160,512]{1,0:T(8,128)(2,1)}, bf16[160,512]{1,0:T(8,128)(2,1)}, bf16[160,512]{1,0:T(8,128)(2,1)}, bf16[512,2048]{1,0:T(8,128)(2,1)}) conditional(s32[]{:T(128)} %bitcast.3, (s32[]{:T(128)}, s32[2048]{0:T(1024)S(1)}, bf16[6912,512]{1,0:T(8,128)(2,1)}) %tuple.23, (bf16[320,512]{1,0:T(8,128)(2,1)S(1)}, ...), branch_computations={%region_0.2_spmd, %region_2.3_spmd} | conditional | flops 4026531840 | bytes 21667908 | solution.py:494
  24.0 1.2 collective-permute-start.2
  25.3 1.5 collective-permute-start
  26.8 2.4 %collective-permute-start.6 = (bf16[320,512]{1,0:T(8,128)(2,1)S(1)}, bf16[320,512]{1,0:T(8,128)(2,1)S(1)}, u32[]{:S(2)}, u32[]{:S(2)}) collective-permute-start(bf16[320,512]{1,0:T(8,128)(2,1)S(1)} %get-tuple-element.18.refs_0_), channel_id=1, source_target_pairs={{8,0},{9,1},{10,2},{11,3},{12,4},{13,5},{14,6},{15,7},{0,8},{1,9},... | collective-permute-start | bytes 983048 | tf_op jit(solution)/shard_map/cond/branch_1_fun/ppermute | solution.py:292
  29.3 3.3 %collective-permute-done.2.refs_1_ = bf16[320,512]{1,0:T(8,128)(2,1)S(1)} collective-permute-done((bf16[320,512]{1,0:T(8,128)(2,1)S(1)}, bf16[320,512]{1,0:T(8,128)(2,1)S(1)}, u32[]{:S(2)}, u32[]{:S(2)}) %collective-permute-start.2) | collective-permute-done | bytes 327712 | tf_op jit(solution)/shard_map/cond/branch_1_fun/ppermute | solution.py:292
  32.6 2.8 %collective-permute-start.5 = (bf16[320,512]{1,0:T(8,128)(2,1)S(1)}, bf16[320,512]{1,0:T(8,128)(2,1)S(1)}, u32[]{:S(2)}, u32[]{:S(2)}) collective-permute-start(bf16[320,512]{1,0:T(8,128)(2,1)S(1)} %collective-permute-done.2.refs_1_), channel_id=1, source_target_pairs={{8,0},{9,1},{10,2},{11,3},{12,4},{13,5},{14,6},{15,7},{0,8},{1,9},... | collective-permute-start | bytes 983048 | tf_op jit(solution)/shard_map/cond/branch_1_fun/ppermute | solution.py:292
  35.5 1.5 collective-permute-start.3
  37.0 1.6 collective-permute-start.1
  38.5 1.8 %place.2.refs_5_ = bf16[512,2048]{1,0:T(8,128)(2,1)S(1)} custom-call(bf16[320,512]{1,0:T(8,128)(2,1)S(1)} %get-tuple-element.18.refs_0_, bf16[320,512]{1,0:T(8,128)(2,1)S(1)} %collective-permute-done.6.refs_1_, s32[1,2048]{1,0:T(1,128)S(1)} %get-tuple-element.19.refs_2_.refs_4_), custom_call_target="tpu_custom_call" | custom-call | flops 1342177280 | bytes 4194304 | tf_op jit(solution)/shard_map/cond/branch_1_fun/place/pallas_call | solution.py:328
  40.4 4.4 %place.3 = bf16[512,2048]{1,0:T(8,128)(2,1)} custom-call(bf16[320,512]{1,0:T(8,128)(2,1)S(1)} %collective-permute-done.refs_0_, bf16[320,512]{1,0:T(8,128)(2,1)S(1)} %collective-permute-done.2.refs_1_, bf16[320,512]{1,0:T(8,128)(2,1)S(1)} %collective-permute-done.4.refs_2_, bf16[320,512]{1,0:T(8,128)(2,1)S(1)} %collective-permute-done.5.refs_3_, ...), custom_call_target="tpu_custom_call" | custom-call | flops 2684354560 | bytes 4194304 | tf_op jit(solution)/shard_map/cond/branch_1_fun/place/pallas_call | solution.py:328
  44.8 1.0 collective-permute-start.7
  45.8 0.1 collective-permute-start.8
  45.9 1.3 collective-permute-done.7
  47.2 0.4 collective-permute-done.8
  47.6 31.7 %pairs.1 = (bf16[6912,2048]{1,0:T(8,128)(2,1)}, bf16[32,4,32,128]{3,2,1,0:T(8,128)(2,1)S(1)}) custom-call(bf16[6912,512]{1,0:T(8,128)(2,1)} %orb.1, bf16[512,2048]{1,0:T(8,128)(2,1)} %get-tuple-element.52.part_t, s32[1,2048]{1,0:T(1,128)S(1)} %get-tuple-element.39.slot, bf16[160,512]{1,0:T(8,128)(2,1)} %get-tuple-element.41.far0, ...), custom_call_target="tpu_custom_call" | custom-call | tf_op jit(solution)/shard_map/pairs/pallas_call | solution.py:120
  79.2 22.0 %all_to_all.20 = bf16[128,32,128]{2,1,0:T(8,128)(2,1)S(1)} all-to-all(bf16[128,32,128]{2,1,0:T(8,128)(2,1)S(1)} %bitcast.16), channel_id=1, replica_groups=mesh['z'=4,'x_lo'=2,'core'=2,'x_hi'=2,'y'=4] {'z','x_lo','core','x_hi','y'}, dimensions={0} | all-to-all | bytes 2097152 | tf_op jit(solution)/shard_map/all_to_all | solution.py:510
  101.3 7.4 %solve.1 = bf16[4096,128]{1,0:T(8,128)(2,1)S(1)} custom-call(s32[1]{0:T(128)} %bitcast.1.me, bf16[4096,128]{1,0:T(8,128)(2,1)S(1)} %bitcast.14, bf16[1536,1536]{1,0:T(8,128)(2,1)} %constant.73.clone.table, bf16[96,96]{1,0:T(8,128)(2,1)S(1)} %copy-done.5, bf16[96,96]{1,0:T(8,128)(2,1)S(1)} %copy-done.4), custom_call_target="tpu_custom_call" | custom-call | tf_op jit(solution)/shard_map/solve/pallas_call | solution.py:199
  108.7 23.2 %all_to_all.21 = bf16[128,32,128]{2,1,0:T(8,128)(2,1)S(1)} all-to-all(bf16[128,32,128]{2,1,0:T(8,128)(2,1)S(1)} %bitcast.15), channel_id=1, replica_groups=mesh['z'=4,'x_lo'=2,'core'=2,'x_hi'=2,'y'=4] {'z','x_lo','core','x_hi','y'}, dimensions={0} | all-to-all | bytes 2097152 | tf_op jit(solution)/shard_map/all_to_all | solution.py:512
  131.8 12.4 %project.1 = f32[128,8,128]{2,1,0:T(8,128)S(1)} custom-call(bf16[32,4,32,128]{3,2,1,0:T(8,128)(2,1)S(1)} %bitcast.13, bf16[512,512]{1,0:T(8,128)(2,1)S(1)} %copy-done.2, bf16[864,1024]{1,0:T(8,128)(2,1)S(1)} %copy-done.1, bf16[6912,2048]{1,0:T(8,128)(2,1)} %get-tuple-element.46.pair), custom_call_target="tpu_custom_call" | custom-call | tf_op jit(solution)/shard_map/project/pallas_call | solution.py:260
  144.2 18.5 %all_to_all.22 = f32[128,8,128]{2,1,0:T(8,128)S(1)} all-to-all(f32[128,8,128]{2,1,0:T(8,128)S(1)} %project.1), channel_id=1, replica_groups=mesh['z'=4,'x_lo'=2,'core'=2,'x_hi'=2,'y'=4] {'z','x_lo','core','x_hi','y'}, dimensions={0} | all-to-all | bytes 1048576 | tf_op jit(solution)/shard_map/all_to_all | solution.py:514
  162.7 0.1 reduce_sum.9
  162.9 0.1 fusion.1
  162.9 0.6 pad_maximum_fusion.1
  (24 shorter events, 0.1 us)
Async XLA Ops:
  4.8 18.9 %all-to-all-start = ((bf16[16,32,512]{2,1,0:T(8,128)(2,1)}), bf16[16,32,512]{2,1,0:T(8,128)(2,1)S(1)}, u32[]{:S(2)}, u32[]{:S(2)}) async-start(bf16[16,32,512]{2,1,0:T(8,128)(2,1)} %broadcast_in_dim.34), calls=%async_computation | async-start | bytes 1048576 | tf_op jit(solution)/shard_map/all_to_all | solution.py:490
  13.1 1.6 copy-start.6
  14.1 9.9 %copy-start.7 = (s32[2048]{0:T(1024)S(1)}, s32[2048]{0:T(1024)}, u32[]{:S(2)}) copy-start(s32[2048]{0:T(1024)} %param.14) | copy-start | bytes 24580
  24.0 23.6 %copy-start = (bf16[1024,864]{1,0:T(8,128)(2,1)S(1)}, bf16[1024,864]{1,0:T(8,128)(2,1)}, u32[]{:S(2)}) copy-start(bf16[1024,864]{1,0:T(8,128)(2,1)} %constant.71.clone.ahead) | copy-start | bytes 5308420
  24.0 23.6 %copy-start.3 = (bf16[512,512]{1,0:T(8,128)(2,1)S(1)}, bf16[512,512]{1,0:T(8,128)(2,1)}, u32[]{:S(2)}) copy-start(bf16[512,512]{1,0:T(8,128)(2,1)} %constant.72.clone.swap) | copy-start | bytes 1572868
  24.0 8.6 %collective-permute-start.2 = (bf16[320,512]{1,0:T(8,128)(2,1)S(1)}, bf16[320,512]{1,0:T(8,128)(2,1)S(1)}, u32[]{:S(2)}, u32[]{:S(2)}) collective-permute-start(bf16[320,512]{1,0:T(8,128)(2,1)S(1)} %get-tuple-element.18.refs_0_), channel_id=1, source_target_pairs={{20,0},{21,1},{22,2},{23,3},{16,4},{17,5},{18,6},{19,7},{28,8},{29... | collective-permute-start | bytes 983048 | tf_op jit(solution)/shard_map/cond/branch_1_fun/ppermute | solution.py:292
  25.3 10.2 %collective-permute-start = (bf16[320,512]{1,0:T(8,128)(2,1)S(1)}, bf16[320,512]{1,0:T(8,128)(2,1)S(1)}, u32[]{:S(2)}, u32[]{:S(2)}) collective-permute-start(bf16[320,512]{1,0:T(8,128)(2,1)S(1)} %get-tuple-element.18.refs_0_), channel_id=1, source_target_pairs={{16,0},{17,1},{18,2},{19,3},{20,4},{21,5},{22,6},{23,7},{24,8},{25... | collective-permute-start | bytes 983048 | tf_op jit(solution)/shard_map/cond/branch_1_fun/ppermute | solution.py:292
  26.8 11.7 %collective-permute-start.6 = (bf16[320,512]{1,0:T(8,128)(2,1)S(1)}, bf16[320,512]{1,0:T(8,128)(2,1)S(1)}, u32[]{:S(2)}, u32[]{:S(2)}) collective-permute-start(bf16[320,512]{1,0:T(8,128)(2,1)S(1)} %get-tuple-element.18.refs_0_), channel_id=1, source_target_pairs={{8,0},{9,1},{10,2},{11,3},{12,4},{13,5},{14,6},{15,7},{0,8},{1,9},... | collective-permute-start | bytes 983048 | tf_op jit(solution)/shard_map/cond/branch_1_fun/ppermute | solution.py:292
  32.6 7.8 %collective-permute-start.5 = (bf16[320,512]{1,0:T(8,128)(2,1)S(1)}, bf16[320,512]{1,0:T(8,128)(2,1)S(1)}, u32[]{:S(2)}, u32[]{:S(2)}) collective-permute-start(bf16[320,512]{1,0:T(8,128)(2,1)S(1)} %collective-permute-done.2.refs_1_), channel_id=1, source_target_pairs={{8,0},{9,1},{10,2},{11,3},{12,4},{13,5},{14,6},{15,7},{0,8},{1,9},... | collective-permute-start | bytes 983048 | tf_op jit(solution)/shard_map/cond/branch_1_fun/ppermute | solution.py:292
  35.4 5.0 %collective-permute-start.4 = (bf16[320,512]{1,0:T(8,128)(2,1)S(1)}, bf16[320,512]{1,0:T(8,128)(2,1)S(1)}, u32[]{:S(2)}, u32[]{:S(2)}) collective-permute-start(bf16[320,512]{1,0:T(8,128)(2,1)S(1)} %collective-permute-done.refs_0_), channel_id=1, source_target_pairs={{8,0},{9,1},{10,2},{11,3},{12,4},{13,5},{14,6},{15,7},{0,8},{1,9},... | collective-permute-start | bytes 983048 | tf_op jit(solution)/shard_map/cond/branch_1_fun/ppermute | solution.py:292
  35.5 9.3 %collective-permute-start.3 = (bf16[160,512]{1,0:T(8,128)(2,1)S(1)}, bf16[160,512]{1,0:T(8,128)(2,1)}, u32[]{:S(2)}, u32[]{:S(2)}) collective-permute-start(bf16[160,512]{1,0:T(8,128)(2,1)S(1)} %slice.17), channel_id=1, source_target_pairs={{20,0},{21,1},{22,2},{23,3},{16,4},{17,5},{18,6},{19,7},{28,8},{29... | collective-permute-start | bytes 491528 | tf_op jit(solution)/shard_map/cond/branch_1_fun/ppermute | solution.py:292
  37.0 7.8 %collective-permute-start.1 = (bf16[160,512]{1,0:T(8,128)(2,1)S(1)}, bf16[160,512]{1,0:T(8,128)(2,1)}, u32[]{:S(2)}, u32[]{:S(2)}) collective-permute-start(bf16[160,512]{1,0:T(8,128)(2,1)S(1)} %slice.16), channel_id=1, source_target_pairs={{16,0},{17,1},{18,2},{19,3},{20,4},{21,5},{22,6},{23,7},{24,8},{25... | collective-permute-start | bytes 491528 | tf_op jit(solution)/shard_map/cond/branch_1_fun/ppermute | solution.py:292
  44.8 2.4 %collective-permute-start.7 = (bf16[160,512]{1,0:T(8,128)(2,1)}, bf16[160,512]{1,0:T(8,128)(2,1)}, u32[]{:S(2)}, u32[]{:S(2)}) collective-permute-start(bf16[160,512]{1,0:T(8,128)(2,1)} %collective-permute-done.1), channel_id=1, source_target_pairs={{8,0},{9,1},{10,2},{11,3},{12,4},{13,5},{14,6},{15,7},{0,8},{1,9},... | collective-permute-start | bytes 491528 | tf_op jit(solution)/shard_map/cond/branch_1_fun/ppermute | solution.py:292
  45.8 1.7 %collective-permute-start.8 = (bf16[160,512]{1,0:T(8,128)(2,1)}, bf16[160,512]{1,0:T(8,128)(2,1)}, u32[]{:S(2)}, u32[]{:S(2)}) collective-permute-start(bf16[160,512]{1,0:T(8,128)(2,1)} %collective-permute-done.3), channel_id=1, source_target_pairs={{8,0},{9,1},{10,2},{11,3},{12,4},{13,5},{14,6},{15,7},{0,8},{1,9},... | collective-permute-start | bytes 491528 | tf_op jit(solution)/shard_map/cond/branch_1_fun/ppermute | solution.py:292
  79.2 22.0 %copy-start.4 = (bf16[96,96]{1,0:T(8,128)(2,1)S(1)}, bf16[96,96]{1,0:T(8,128)(2,1)}, u32[]{:S(2)}) copy-start(bf16[96,96]{1,0:T(8,128)(2,1)} %constant.75.clone.x_back) | copy-start | bytes 55300
  79.2 22.0 %copy-start.5 = (bf16[96,96]{1,0:T(8,128)(2,1)S(1)}, bf16[96,96]{1,0:T(8,128)(2,1)}, u32[]{:S(2)}) copy-start(bf16[96,96]{1,0:T(8,128)(2,1)} %constant.74.clone.x_ahead) | copy-start | bytes 55300
  101.3 30.6 %copy-start.2 = (bf16[512,512]{1,0:T(8,128)(2,1)S(1)}, bf16[512,512]{1,0:T(8,128)(2,1)}, u32[]{:S(2)}) copy-start(bf16[512,512]{1,0:T(8,128)(2,1)} %constant.76.clone.unswap) | copy-start | bytes 1572868
  108.7 23.2 %copy-start.1 = (bf16[864,1024]{1,0:T(8,128)(2,1)S(1)}, bf16[864,1024]{1,0:T(8,128)(2,1)}, u32[]{:S(2)}) copy-start(bf16[864,1024]{1,0:T(8,128)(2,1)} %constant.77.clone.back) | copy-start | bytes 5308420

commit v8 on v7

--- a/solution.py
+++ b/solution.py
@@ -71,14 +71,19 @@
     return jnp.dot(a, b, preferred_element_type=F32)
 
 
-def pair_kernel(
-    orb, part_t, slot, far0, far1, far2, far3, panel, ahead, swap, pair, send, fit, rows_t, held
-):
+def pair_kernel(fits, spare, orb, part_t, slot, far0, far1, far2, far3, *refs):
+    panel, ahead, swap, pair, send, fit, rows_t, held, sem = refs
     step = pl.program_id(0)
 
-    @pl.when(step == 0)
+    @pl.when((step == 0) & (fits[0] > 0))
     def _():
         fill(FAR, (far0, far1, far2, far3), slot, (part_t,), held, rows_t)
+
+    @pl.when((step == 0) & (fits[0] <= 0))
+    def _():
+        copy = pltpu.make_async_copy(spare, rows_t, sem)
+        copy.start()
+        copy.wait()
 
     npts = rows_t.shape[1]
     chunk, rows = 1024, 256
@@ -112,7 +117,7 @@
                 ].reshape(MG // 4, ROWS, 128)
 
 
-def make_pairs(orbitals, part_t, slot, far, panel2, tab):
+def make_pairs(fits, spare, orbitals, part_t, slot, far, panel2, tab):
     npts = part_t.shape[1]
     norb = orbitals.shape[1]
     steps = orbitals.shape[0] // CELLS
@@ -121,6 +126,8 @@
         pair_kernel,
         grid=(steps,),
         in_specs=[
+            pl.BlockSpec(memory_space=pltpu.SMEM),
+            pl.BlockSpec(memory_space=pl.ANY),
             pl.BlockSpec((CELLS, norb), lambda i: (i, 0)),
             whole(part_t.shape),
             whole(slot.shape),
@@ -141,10 +148,11 @@
             pltpu.VMEM((OCT * NG, 512), BF),
             pltpu.VMEM(part_t.shape, BF),
             pltpu.VMEM((4 * HALF_GROUP, norb), BF),
-        ],
-        compiler_params=pltpu.CompilerParams(vmem_limit_bytes=36 * 2**20),
+            pltpu.SemaphoreType.DMA,
+        ],
+        compiler_params=pltpu.CompilerParams(vmem_limit_bytes=54 * 2**20),
         name="pairs",
-    )(orbitals, part_t, slot, *far, panel2, const(tab["ahead"]), const(tab["swap"]))
+    )(fits, spare, orbitals, part_t, slot, *far, panel2, const(tab["ahead"]), const(tab["swap"]))
 
 
 def places():
@@ -489,14 +497,16 @@
     copies = jnp.broadcast_to(own[None], (16,) + own.shape)
     square = lax.all_to_all(copies, ("z", "y"), 0, 0).reshape(16 * ROOM, own.shape[1])
     fits, choose, slot = index(me, owner)
+    shape = (orbitals.shape[1], points.shape[0])
+    spare = lax.cond(
+        fits[0] > 0,
+        lambda: jnp.zeros(shape, BF),
+        lambda: summed_rows(orbitals, points, me),
+    )
+    square, _ = lax.optimization_barrier((square, spare[:8, :128]))
     held = mm(choose, square).astype(BF)
-    none = jnp.zeros((HALF_GROUP, orbitals.shape[1]), BF)
-    rows, *far = lax.cond(
-        fits[0] > 0,
-        lambda: spread_rows(held, slot),
-        lambda: (summed_rows(orbitals, points, me), none, none, none, none),
-    )
-    return rows, slot, far
+    rows, *far = spread_rows(held, slot)
+    return fits, spare, rows, slot, far
 
 
 def shards(orbitals, inverse_panel, points):
@@ -504,9 +514,9 @@
     devices = lax.axis_size(AXES)
     me = lax.axis_index(AXES)
     npoints, cols = inverse_panel.shape
-    part_t, slot, far = gather_rows(orbitals, points, me)
+    fits, spare, part_t, slot, far = gather_rows(orbitals, points, me)
     panel2 = jnp.concatenate([inverse_panel, inverse_panel], axis=1)
-    pair, send = make_pairs(orbitals, part_t, slot, far, panel2, tab)
+    pair, send = make_pairs(fits, spare, orbitals, part_t, slot, far, panel2, tab)
     planes = lax.all_to_all(send.reshape(devices, ROWS, 128), AXES, 0, 0)
     ret = solve(me.reshape(1), planes.reshape(devices * ROWS, 128), tab)
     got = lax.all_to_all(ret.reshape(devices, ROWS, 128), AXES, 0, 0)

time: 164 us -> 170 us (1.037)
  local copies, waits for them, and re-layouts: 1.27 us -> 4.95 us
    unnamed x17 -> x27, local copies, waits for them, and re-layouts: 0.32 us -> 2.4 us
    pallas_call x1, Pallas kernels: 31.7 us -> 33.6 us  [make_pairs(): pl.pallas_call(pair_kernel, grid=(steps,), in_specs=[pl.BlockSpec(memory_...]
  transfers between devices with their start and end apart: 10 -> 10, of which waited for: 4 -> 3; matrix products, arithmetic and copies ran while one was open for 0% -> 2% of each run, Pallas kernels for 4% -> 3%
where the time goes in v8:
time: 170 us; the launch traced here: 169 us
  blocking collectives  64.2 us (38%)
  Pallas kernels  62.9 us (37%)
  starting transfers between devices  20.8 us (12%)
  waiting for transfers between devices  13.3 us (8%)
  local copies, waits for them, and re-layouts  4.95 us (3%)
  other arithmetic  1.82 us (1%)
    pallas_call x1, Pallas kernels, make_pairs(): pl.pallas_call(pair_kernel, grid=(steps,), in_specs=[pl.BlockSpec(memory_...  33.6 us
    all_to_all x1, blocking collectives, shards(): got = lax.all_to_all(ret.reshape(devices, ROWS, 128), AXES, 0, 0)  23.2 us
    all_to_all x1, blocking collectives, shards(): planes = lax.all_to_all(send.reshape(devices, ROWS, 128), AXES, 0, 0)  22.5 us
    all_to_all x1, blocking collectives, shards(): parts = lax.all_to_all(parts, AXES, 0, 0)  18.5 us
    pallas_call x1, Pallas kernels, project(): pl.pallas_call(project_kernel, in_specs=[vmem] * 3 + [pl.BlockSpec(memory...  12.4 us
    ppermute x9, starting transfers between devices, bring(): return lax.ppermute(data, AXES, pairs)  12.2 us
    all_to_all x1, waiting for transfers between devices, gather_rows(): lax.all_to_all(copies, ('z', 'y'), 0, 0).reshape(16 * ROOM, own.shape[1])  9.63 us
    all_to_all x1, starting transfers between devices, gather_rows(): lax.all_to_all(copies, ('z', 'y'), 0, 0).reshape(16 * ROOM, own.shape[1])  8.67 us
  transfers between devices with their start and end apart: 10, of which 3 were waited for; matrix products, arithmetic and copies ran while one was open for 2% of the time, Pallas kernels for 3%

profile of v8, /device:TPU:1, one launch (start us, length us, event | category | flops | bytes accessed | tf_op | source)
XLA Modules:
  0.0 169.2 jit_solution(13181249396116506215)
XLA Ops:
  0.0 3.8 %own.1 = (bf16[32,512]{1,0:T(8,128)(2,1)S(1)}, s32[1,2048]{1,0:T(1,128)S(1)}) custom-call(s32[1]{0:T(128)} %bitcast.1.me, s32[1,2048]{1,0:T(1,128)} %bitcast.19, bf16[6912,512]{1,0:T(8,128)(2,1)} %orb.1), custom_call_target="tpu_custom_call" | custom-call | tf_op jit(solution)/shard_map/own/pallas_call | solution.py:443
  3.8 0.9 broadcast_in_dim.31
  4.6 8.7 %all-to-all-start = ((bf16[16,32,512]{2,1,0:T(8,128)(2,1)}), bf16[16,32,512]{2,1,0:T(8,128)(2,1)S(1)}, u32[]{:S(2)}, u32[]{:S(2)}) async-start(bf16[16,32,512]{2,1,0:T(8,128)(2,1)} %broadcast_in_dim.31), calls=%async_computation | async-start | bytes 1048576 | tf_op jit(solution)/shard_map/all_to_all | solution.py:498
  13.3 1.0 index.1
  14.3 9.6 %all-to-all-done = bf16[16,32,512]{2,1,0:T(8,128)(2,1)S(1)} async-done(((bf16[16,32,512]{2,1,0:T(8,128)(2,1)}), bf16[16,32,512]{2,1,0:T(8,128)(2,1)S(1)}, u32[]{:S(2)}, u32[]{:S(2)}) %all-to-all-start) | async-done | bytes 524320 | tf_op jit(solution)/shard_map/all_to_all | solution.py:498
  23.9 0.3 convolution_convert_fusion.refs_0_
  24.3 1.1 collective-permute-start.2
  25.4 1.7 collective-permute-start
  27.0 2.4 %collective-permute-start.6 = (bf16[320,512]{1,0:T(8,128)(2,1)S(1)}, bf16[320,512]{1,0:T(8,128)(2,1)S(1)}, u32[]{:S(2)}, u32[]{:S(2)}) collective-permute-start(bf16[320,512]{1,0:T(8,128)(2,1)S(1)} %convolution_convert_fusion.refs_0_), channel_id=1, source_target_pairs={{8,0},{9,1},{10,2},{11,3},{12,4},{13,5},{14,6},{15,7},{0,8},{1,9},... | collective-permute-start | bytes 983048 | tf_op jit(solution)/shard_map/ppermute | solution.py:300
  29.4 3.5 %collective-permute-done.2.refs_1_ = bf16[320,512]{1,0:T(8,128)(2,1)S(1)} collective-permute-done((bf16[320,512]{1,0:T(8,128)(2,1)S(1)}, bf16[320,512]{1,0:T(8,128)(2,1)S(1)}, u32[]{:S(2)}, u32[]{:S(2)}) %collective-permute-start.2) | collective-permute-done | bytes 327712 | tf_op jit(solution)/shard_map/ppermute | solution.py:300
  32.9 2.8 %collective-permute-start.5 = (bf16[320,512]{1,0:T(8,128)(2,1)S(1)}, bf16[320,512]{1,0:T(8,128)(2,1)S(1)}, u32[]{:S(2)}, u32[]{:S(2)}) collective-permute-start(bf16[320,512]{1,0:T(8,128)(2,1)S(1)} %collective-permute-done.2.refs_1_), channel_id=1, source_target_pairs={{8,0},{9,1},{10,2},{11,3},{12,4},{13,5},{14,6},{15,7},{0,8},{1,9},... | collective-permute-start | bytes 983048 | tf_op jit(solution)/shard_map/ppermute | solution.py:300
  36.3 0.3 copy.11
  36.6 1.6 conditional.1
  36.6 1.6 broadcast.16.clone
  38.2 1.1 collective-permute-start.3
  39.4 1.9 %collective-permute-start.1 = (bf16[160,512]{1,0:T(8,128)(2,1)S(1)}, bf16[160,512]{1,0:T(8,128)(2,1)S(1)}, u32[]{:S(2)}, u32[]{:S(2)}) collective-permute-start(bf16[160,512]{1,0:T(8,128)(2,1)S(1)} %slice.19), channel_id=1, source_target_pairs={{16,0},{17,1},{18,2},{19,3},{20,4},{21,5},{22,6},{23,7},{24,8},{25... | collective-permute-start | bytes 491528 | tf_op jit(solution)/shard_map/ppermute | solution.py:300
  41.3 1.8 %place.2.refs_5_ = bf16[512,2048]{1,0:T(8,128)(2,1)S(1)} custom-call(bf16[320,512]{1,0:T(8,128)(2,1)S(1)} %convolution_convert_fusion.refs_0_, bf16[320,512]{1,0:T(8,128)(2,1)S(1)} %collective-permute-done.6.refs_1_, s32[1,2048]{1,0:T(1,128)S(1)} %get-tuple-element.31.refs_2_.refs_4_.slot), custom_call_target="tpu_custom_call" | custom-call | flops 1342177280 | bytes 4194304 | tf_op jit(solution)/shard_map/place/pallas_call | solution.py:336
  43.2 2.9 %place.3.part_t = bf16[512,2048]{1,0:T(8,128)(2,1)S(1)} custom-call(bf16[320,512]{1,0:T(8,128)(2,1)S(1)} %collective-permute-done.refs_0_, bf16[320,512]{1,0:T(8,128)(2,1)S(1)} %collective-permute-done.2.refs_1_, bf16[320,512]{1,0:T(8,128)(2,1)S(1)} %collective-permute-done.4.refs_2_, bf16[320,512]{1,0:T(8,128)(2,1)S(1)} %collective-permute-done.5.refs_3_, ...), custom_call_target="tpu_custom_call" | custom-call | flops 2684354560 | bytes 4194304 | tf_op jit(solution)/shard_map/place/pallas_call | solution.py:336
  46.1 1.4 copy-done
  47.6 1.1 collective-permute-start.7
  48.8 1.1 pad_maximum_fusion.refs_0_
  49.9 0.2 collective-permute-done.8.far3
  50.1 0.4 copy-done.10
  50.5 0.2 copy-done.11
  50.8 33.6 %pairs.1 = (bf16[6912,2048]{1,0:T(8,128)(2,1)}, bf16[32,4,32,128]{3,2,1,0:T(8,128)(2,1)}) custom-call(s32[1]{0:T(128)} %get-tuple-element.28.fits, bf16[512,2048]{1,0:T(8,128)(2,1)S(1)} %copy-done.6, bf16[6912,512]{1,0:T(8,128)(2,1)} %orb.1, bf16[512,2048]{1,0:T(8,128)(2,1)} %copy-done, s32[1,2048]{1,0:T(1,128)} %copy-done.5, bf16[160,512]{1,0:T(8,128)(2,1)} %copy-done.9, ...), custom_call_target="tpu_custom_call" | custom-call | tf_op jit(solution)/shard_map/pairs/pallas_call | solution.py:125
  84.4 22.5 %all_to_all.20 = bf16[128,32,128]{2,1,0:T(8,128)(2,1)S(1)} all-to-all(bf16[128,32,128]{2,1,0:T(8,128)(2,1)} %bitcast.18), channel_id=1, replica_groups=mesh['z'=4,'x_lo'=2,'core'=2,'x_hi'=2,'y'=4] {'z','x_lo','core','x_hi','y'}, dimensions={0} | all-to-all | bytes 2097152 | tf_op jit(solution)/shard_map/all_to_all | solution.py:520
  106.9 7.4 %solve.1 = bf16[4096,128]{1,0:T(8,128)(2,1)S(1)} custom-call(s32[1]{0:T(128)} %bitcast.1.me, bf16[4096,128]{1,0:T(8,128)(2,1)S(1)} %bitcast.14, bf16[1536,1536]{1,0:T(8,128)(2,1)} %constant.74.clone.table, bf16[96,96]{1,0:T(8,128)(2,1)S(1)} %copy-done.4, bf16[96,96]{1,0:T(8,128)(2,1)S(1)} %copy-done.3), custom_call_target="tpu_custom_call" | custom-call | tf_op jit(solution)/shard_map/solve/pallas_call | solution.py:207
  114.3 23.2 %all_to_all.21 = bf16[128,32,128]{2,1,0:T(8,128)(2,1)S(1)} all-to-all(bf16[128,32,128]{2,1,0:T(8,128)(2,1)S(1)} %bitcast.15), channel_id=1, replica_groups=mesh['z'=4,'x_lo'=2,'core'=2,'x_hi'=2,'y'=4] {'z','x_lo','core','x_hi','y'}, dimensions={0} | all-to-all | bytes 2097152 | tf_op jit(solution)/shard_map/all_to_all | solution.py:522
  137.5 12.4 %project.1 = f32[128,8,128]{2,1,0:T(8,128)S(1)} custom-call(bf16[32,4,32,128]{3,2,1,0:T(8,128)(2,1)S(1)} %bitcast.13, bf16[512,512]{1,0:T(8,128)(2,1)S(1)} %copy-done.2, bf16[864,1024]{1,0:T(8,128)(2,1)S(1)} %copy-done.1, bf16[6912,2048]{1,0:T(8,128)(2,1)} %get-tuple-element.36.pair), custom_call_target="tpu_custom_call" | custom-call | tf_op jit(solution)/shard_map/project/pallas_call | solution.py:268
  149.9 18.5 %all_to_all.22 = f32[128,8,128]{2,1,0:T(8,128)S(1)} all-to-all(f32[128,8,128]{2,1,0:T(8,128)S(1)} %project.1), channel_id=1, replica_groups=mesh['z'=4,'x_lo'=2,'core'=2,'x_hi'=2,'y'=4] {'z','x_lo','core','x_hi','y'}, dimensions={0} | all-to-all | bytes 1048576 | tf_op jit(solution)/shard_map/all_to_all | solution.py:524
  168.4 0.1 reduce_sum.9
  168.6 0.6 pad_maximum_fusion.1
  (35 shorter events, 0.3 us)
Async XLA Ops:
  4.6 19.3 %all-to-all-start = ((bf16[16,32,512]{2,1,0:T(8,128)(2,1)}), bf16[16,32,512]{2,1,0:T(8,128)(2,1)S(1)}, u32[]{:S(2)}, u32[]{:S(2)}) async-start(bf16[16,32,512]{2,1,0:T(8,128)(2,1)} %broadcast_in_dim.31), calls=%async_computation | async-start | bytes 1048576 | tf_op jit(solution)/shard_map/all_to_all | solution.py:498
  13.3 23.0 %copy-start.7 = (bf16[2048,64]{0,1:T(8,128)(2,1)S(1)}, bf16[2048,64]{0,1:T(8,128)(2,1)}, u32[]{:S(2)}) copy-start(bf16[2048,64]{0,1:T(8,128)(2,1)} %param.13) | copy-start | bytes 786436
  13.3 23.3 %copy-start.12 = (s32[2048]{0:T(1024)S(1)}, s32[2048]{0:T(1024)}, u32[]{:S(2)}) copy-start(s32[2048]{0:T(1024)} %param.14) | copy-start | bytes 24580
  14.3 28.8 %copy-start.5 = (s32[1,2048]{1,0:T(1,128)}, s32[1,2048]{1,0:T(1,128)S(1)}, u32[]{:S(2)}) copy-start(s32[1,2048]{1,0:T(1,128)S(1)} %get-tuple-element.31.refs_2_.refs_4_.slot) | copy-start | bytes 24580
  24.3 8.6 %collective-permute-start.2 = (bf16[320,512]{1,0:T(8,128)(2,1)S(1)}, bf16[320,512]{1,0:T(8,128)(2,1)S(1)}, u32[]{:S(2)}, u32[]{:S(2)}) collective-permute-start(bf16[320,512]{1,0:T(8,128)(2,1)S(1)} %convolution_convert_fusion.refs_0_), channel_id=1, source_target_pairs={{20,0},{21,1},{22,2},{23,3},{16,4},{17,5},{18,6},{19,7},{28,8},{29... | collective-permute-start | bytes 983048 | tf_op jit(solution)/shard_map/ppermute | solution.py:300
  25.4 10.3 %collective-permute-start = (bf16[320,512]{1,0:T(8,128)(2,1)S(1)}, bf16[320,512]{1,0:T(8,128)(2,1)S(1)}, u32[]{:S(2)}, u32[]{:S(2)}) collective-permute-start(bf16[320,512]{1,0:T(8,128)(2,1)S(1)} %convolution_convert_fusion.refs_0_), channel_id=1, source_target_pairs={{16,0},{17,1},{18,2},{19,3},{20,4},{21,5},{22,6},{23,7},{24,8},{25... | collective-permute-start | bytes 983048 | tf_op jit(solution)/shard_map/ppermute | solution.py:300
  27.0 14.2 %collective-permute-start.6 = (bf16[320,512]{1,0:T(8,128)(2,1)S(1)}, bf16[320,512]{1,0:T(8,128)(2,1)S(1)}, u32[]{:S(2)}, u32[]{:S(2)}) collective-permute-start(bf16[320,512]{1,0:T(8,128)(2,1)S(1)} %convolution_convert_fusion.refs_0_), channel_id=1, source_target_pairs={{8,0},{9,1},{10,2},{11,3},{12,4},{13,5},{14,6},{15,7},{0,8},{1,9},... | collective-permute-start | bytes 983048 | tf_op jit(solution)/shard_map/ppermute | solution.py:300
  32.9 10.2 %collective-permute-start.5 = (bf16[320,512]{1,0:T(8,128)(2,1)S(1)}, bf16[320,512]{1,0:T(8,128)(2,1)S(1)}, u32[]{:S(2)}, u32[]{:S(2)}) collective-permute-start(bf16[320,512]{1,0:T(8,128)(2,1)S(1)} %collective-permute-done.2.refs_1_), channel_id=1, source_target_pairs={{8,0},{9,1},{10,2},{11,3},{12,4},{13,5},{14,6},{15,7},{0,8},{1,9},... | collective-permute-start | bytes 983048 | tf_op jit(solution)/shard_map/ppermute | solution.py:300
  35.7 7.4 %collective-permute-start.4 = (bf16[320,512]{1,0:T(8,128)(2,1)S(1)}, bf16[320,512]{1,0:T(8,128)(2,1)S(1)}, u32[]{:S(2)}, u32[]{:S(2)}) collective-permute-start(bf16[320,512]{1,0:T(8,128)(2,1)S(1)} %collective-permute-done.refs_0_), channel_id=1, source_target_pairs={{8,0},{9,1},{10,2},{11,3},{12,4},{13,5},{14,6},{15,7},{0,8},{1,9},... | collective-permute-start | bytes 983048 | tf_op jit(solution)/shard_map/ppermute | solution.py:300
  38.2 9.3 %collective-permute-start.3 = (bf16[160,512]{1,0:T(8,128)(2,1)S(1)}, bf16[160,512]{1,0:T(8,128)(2,1)S(1)}, u32[]{:S(2)}, u32[]{:S(2)}) collective-permute-start(bf16[160,512]{1,0:T(8,128)(2,1)S(1)} %slice.20), channel_id=1, source_target_pairs={{20,0},{21,1},{22,2},{23,3},{16,4},{17,5},{18,6},{19,7},{28,8},{29... | collective-permute-start | bytes 491528 | tf_op jit(solution)/shard_map/ppermute | solution.py:300
  39.4 8.1 %collective-permute-start.1 = (bf16[160,512]{1,0:T(8,128)(2,1)S(1)}, bf16[160,512]{1,0:T(8,128)(2,1)S(1)}, u32[]{:S(2)}, u32[]{:S(2)}) collective-permute-start(bf16[160,512]{1,0:T(8,128)(2,1)S(1)} %slice.19), channel_id=1, source_target_pairs={{16,0},{17,1},{18,2},{19,3},{20,4},{21,5},{22,6},{23,7},{24,8},{25... | collective-permute-start | bytes 491528 | tf_op jit(solution)/shard_map/ppermute | solution.py:300
  43.2 7.6 %copy-start.6 = (bf16[512,2048]{1,0:T(8,128)(2,1)S(1)}, bf16[512,2048]{1,0:T(8,128)(2,1)}, u32[]{:S(2)}) copy-start(bf16[512,2048]{1,0:T(8,128)(2,1)} %get-tuple-element.37.spare) | copy-start | bytes 6291460
  46.1 1.4 copy-start
  47.5 2.6 %copy-start.8 = (bf16[160,512]{1,0:T(8,128)(2,1)}, bf16[160,512]{1,0:T(8,128)(2,1)S(1)}, u32[]{:S(2)}) copy-start(bf16[160,512]{1,0:T(8,128)(2,1)S(1)} %collective-permute-done.3.far1) | copy-start | bytes 491524
  47.6 2.6 %copy-start.9 = (bf16[160,512]{1,0:T(8,128)(2,1)}, bf16[160,512]{1,0:T(8,128)(2,1)S(1)}, u32[]{:S(2)}) copy-start(bf16[160,512]{1,0:T(8,128)(2,1)S(1)} %collective-permute-done.1.far0) | copy-start | bytes 491524
  47.6 2.3 %collective-permute-start.7 = (bf16[160,512]{1,0:T(8,128)(2,1)S(1)}, bf16[160,512]{1,0:T(8,128)(2,1)S(1)}, u32[]{:S(2)}, u32[]{:S(2)}) collective-permute-start(bf16[160,512]{1,0:T(8,128)(2,1)S(1)} %collective-permute-done.1.far0), channel_id=1, source_target_pairs={{8,0},{9,1},{10,2},{11,3},{12,4},{13,5},{14,6},{15,7},{0,8},{1,9},... | collective-permute-start | bytes 491528 | tf_op jit(solution)/shard_map/ppermute | solution.py:300
  48.7 1.4 collective-permute-start.8
  49.9 0.7 copy-start.10
  50.1 0.7 copy-start.11
  84.4 22.6 %copy-start.3 = (bf16[96,96]{1,0:T(8,128)(2,1)S(1)}, bf16[96,96]{1,0:T(8,128)(2,1)}, u32[]{:S(2)}) copy-start(bf16[96,96]{1,0:T(8,128)(2,1)} %constant.76.clone.x_back) | copy-start | bytes 55300
  84.4 22.6 %copy-start.4 = (bf16[96,96]{1,0:T(8,128)(2,1)S(1)}, bf16[96,96]{1,0:T(8,128)(2,1)}, u32[]{:S(2)}) copy-start(bf16[96,96]{1,0:T(8,128)(2,1)} %constant.75.clone.x_ahead) | copy-start | bytes 55300
  106.9 30.6 %copy-start.2 = (bf16[512,512]{1,0:T(8,128)(2,1)S(1)}, bf16[512,512]{1,0:T(8,128)(2,1)}, u32[]{:S(2)}) copy-start(bf16[512,512]{1,0:T(8,128)(2,1)} %constant.77.clone.unswap) | copy-start | bytes 1572868
  114.3 23.2 %copy-start.1 = (bf16[864,1024]{1,0:T(8,128)(2,1)S(1)}, bf16[864,1024]{1,0:T(8,128)(2,1)}, u32[]{:S(2)}) copy-start(bf16[864,1024]{1,0:T(8,128)(2,1)} %constant.78.clone.back) | copy-start | bytes 5308420
